TPU v7x, 256 devices: a whole 4x4x8 slice. The times are simulated.
256 devices in a mesh: dp: 32 (over x_lo, z, core), section: 8 (over y, x_hi).
Axes of the slice: x: 4 (x_hi: 2, x_lo: 2; x = x_hi * 2 + x_lo), y: 4, z: 8, core: 2. Of those that a mesh axis runs over, the one named last changes fastest.
Arguments:
- noise: bfloat16 [128, 64, 1536], P('dp'), may hold values from -6 to 6
- sched_index: int32 [128, 3], P('dp'), may hold values from 0 to 1000, as said below
- text_ids: int32 [128, 77], replicated, may hold values from 0 to 49407
- text_table: bfloat16 [49408, 1536], P('dp'), may hold values from -24 to 24
- time_weight: bfloat16 [256, 1536], replicated, may hold values from -0.375 to 0.375
- block_weight: bfloat16 [8, 1536, 1536], P('section', 'dp'), may hold values from -0.15625 to 0.15625
- block_mod: float32 [8, 3, 1536], P('section'), may hold values from -3 to 3
- student_weight: bfloat16 [1536, 1536], P('dp', 'section'), may hold values from -0.15625 to 0.15625
- student_mod: float32 [3, 1536], replicated, may hold values from -3 to 3
- feature_weight: bfloat16 [1536, 512], P('section'), may hold values from -0.15625 to 0.15625
- lin_weight: float32 [512], replicated, may hold values from 0.01 to 0.1
- token_weight: float32 [8192], P('dp'), may hold values from 0.5 to 2
Outputs:
- teacher_latents: bfloat16 [128, 64, 1536], P('dp')
- student_grad: float32 [1536, 1536], P(None, 'section')
- token_distance: float32 [8192], P(('dp', 'section'))
Inputs may be any that keep to these rules, and one draw needn't show every extreme that they name: `sched_index`: each row falls strictly from left to right, by 62 to 250 a step, and starts at 500 or higher.
All inputs are finite; a program needn't handle non-finite values.
Results may differ from a plain program's by a relative error of at most 0.024.
Values may be sent and summed in bfloat16 or wider, within the bound.
A program may use at most 64 MiB of HBM per device.

v0:
```python
import math

import jax
import jax.numpy as jnp
from jax import lax
from jax.sharding import Mesh
from jax.sharding import PartitionSpec as P

LEVELS = 1000
DP = ("dp_0", "dp_1", "dp_2")
DP_SECTION = ("dp_0", "dp_1", "dp_2", "section")


def in_blocks(x, dim, count):
    shape = x.shape
    blocks = x.reshape(*shape[:dim], count, shape[dim] // count, *shape[dim + 1 :])
    return jnp.moveaxis(blocks, dim, 0)


def summed_on_arrival(x, axis, dim):
    blocks = in_blocks(x, dim, lax.axis_size(axis))
    arrived = lax.all_to_all(blocks, axis, split_axis=0, concat_axis=0, tiled=True)
    return arrived.sum(axis=0)


def from_behind(block, axis, distance):
    devices = range(lax.axis_size(axis))
    route = [((i - distance) % len(devices), i) for i in devices]
    return lax.ppermute(block, axis, route)


def picked(x, axis, root):
    return lax.dynamic_index_in_dim(lax.all_gather(x, axis), root, 0, keepdims=False)


def in_order(blocks, dim):
    blocks = jnp.moveaxis(blocks, 0, dim)
    shape = blocks.shape
    return blocks.reshape(*shape[:dim], shape[dim] * shape[dim + 1], *shape[dim + 2 :])


def from_everyone(x, axis):
    copies = jnp.broadcast_to(x, (lax.axis_size(axis), *x.shape))
    return lax.all_to_all(copies, axis, split_axis=0, concat_axis=0, tiled=True)


def collect(x, axis, dim):
    return in_order(from_everyone(x, axis), dim)


def sum_at_owner(x, axis, dim):
    blocks = in_blocks(x, dim, lax.axis_size(axis))
    arrived = lax.all_to_all(blocks, axis, split_axis=0, concat_axis=0, tiled=True)
    return arrived.astype(jnp.float32).sum(axis=0)


def side_by_side(arrays, axis, dim, along):
    widths = [a.shape[along] for a in arrays]
    both = jnp.concatenate(arrays, axis=along)
    result = sum_at_owner(both, axis, dim)
    return tuple(jnp.split(result, [sum(widths[:k]) for k in range(1, len(widths))], axis=along))


def filled_up(lines, count):
    spare = -len(lines) % count
    return jnp.pad(lines, [(0, spare)] + [(0, 0)] * (lines.ndim - 1))


def gather_axes(x, axes, dim):
    far, near = axes
    initial = from_everyone(x, far)
    blocks = jnp.swapaxes(from_everyone(initial, near), 0, 1)
    return in_order(blocks.reshape(-1, *x.shape), dim)


def summed_rows(x, axes, dim):
    far, near = axes
    own = sum_at_owner(in_blocks(x, dim, lax.axis_size(far)), near, dim + 1)
    return jnp.sum(
        lax.all_to_all(own.astype(jnp.bfloat16), far, 0, 0, tiled=True).astype(jnp.float32), axis=0
    )


def sum_by_parts(x, axes):
    lines = x.reshape(-1, x.shape[-1])
    padded = filled_up(lines, lax.axis_size(axes[0]) * lax.axis_size(axes[1]))
    whole = gather_axes(summed_rows(padded, axes, 0).astype(jnp.bfloat16), axes, 0)
    return lax.slice_in_dim(whole, 0, len(lines)).reshape(x.shape).astype(jnp.float32)


def modulated(hidden_f, cond_vec, gains):
    mean_sq = jnp.mean(hidden_f * hidden_f, axis=-1, keepdims=True)
    normed = hidden_f * lax.rsqrt(mean_sq + 1e-06)
    return normed * (1.0 + cond_vec * gains[0]) + cond_vec * gains[1]


def teacher_block(hidden, weight, gains, cond_vec):
    hidden_f = hidden.astype(jnp.float32)
    inputs = modulated(hidden_f, cond_vec, gains).astype(jnp.bfloat16)
    mixed = jnp.dot(inputs, weight, preferred_element_type=jnp.float32)
    return (hidden_f + (1.0 + cond_vec * gains[2]) * jax.nn.gelu(mixed)).astype(jnp.bfloat16)


def distance(feat_student, feat_teacher, lin_weight):
    relu_s = jax.nn.relu(feat_student)
    relu_t = jax.nn.relu(feat_teacher)
    unit_s = relu_s * lax.rsqrt(jnp.mean(relu_s * relu_s, axis=-1, keepdims=True) + 1e-06)
    unit_t = relu_t * lax.rsqrt(jnp.mean(relu_t * relu_t, axis=-1, keepdims=True) + 1e-06)
    gap = unit_s - unit_t
    return jnp.sum(lin_weight * gap * gap, axis=-1)


def store(buffer, value, valid, slot_id):
    old_value = lax.dynamic_index_in_dim(buffer, slot_id, 0, keepdims=False)
    return lax.dynamic_update_index_in_dim(buffer, jnp.where(valid, value, old_value), slot_id, 0)


def local(
    noise,
    sched_index,
    text_ids,
    text_table,
    time_weight,
    block_weight,
    block_mod,
    student_weight,
    student_mod,
    feature_weight,
    lin_weight,
    token_weight,
):
    batches, tokens, model_width = noise.shape
    steps = sched_index.shape[1] - 1
    sections = lax.axis_size("section")
    own_section = lax.axis_index("section")
    vocab_rows = text_table.shape[0]
    offset = lax.axis_index(DP) * vocab_rows
    text_len = text_ids.shape[1]
    local_ids = text_ids - offset
    vocab_ids = jnp.arange(vocab_rows, dtype=jnp.int32)

    def add_group(group_id, counts):
        id_block = lax.dynamic_slice_in_dim(local_ids, group_id * 7, 7, 1)
        return counts + jnp.sum((id_block[:, :, None] == vocab_ids).astype(jnp.float32), axis=1)

    counts = lax.fori_loop(
        0,
        text_len // 7,
        add_group,
        jnp.zeros((batches * lax.axis_size(DP), vocab_rows), jnp.float32),
    )
    pooled = summed_on_arrival(
        jnp.dot(counts.astype(jnp.bfloat16), text_table, preferred_element_type=jnp.float32)
        / text_len,
        DP,
        0,
    )
    weights = lax.all_gather(block_weight, DP, axis=1, tiled=True)[0]
    section_mod = block_mod[0]
    indices_f = sched_index.astype(jnp.float32)
    half_freq = time_weight.shape[0] // 2
    frequency = jnp.exp(-math.log(10000.0) * jnp.arange(half_freq, dtype=jnp.float32) / half_freq)
    angles = indices_f[:, :, None] * frequency
    embedding = jnp.concatenate([jnp.cos(angles), jnp.sin(angles)], axis=-1).astype(jnp.bfloat16)
    time_embed = jnp.dot(
        embedding.reshape(-1, 2 * half_freq), time_weight, preferred_element_type=jnp.float32
    )
    conditions = jax.nn.silu(
        time_embed.reshape(batches, steps + 1, model_width) + pooled[:, None, :]
    )
    deltas = (indices_f[:, 1:] - indices_f[:, :-1]) / LEVELS
    surplus = max(0, batches - sections)
    period = sections + surplus
    tick_count = steps * sections + batches - 1 + (steps - 1) * surplus
    sender = (own_section + sections - 1) % sections

    def locate(section_at, tick_now):
        active = jnp.zeros((), jnp.bool_)
        slot_id = jnp.zeros((), jnp.int32)
        pass_id = jnp.zeros((), jnp.int32)
        for pass_now in range(steps):
            candidate = tick_now - section_at - pass_now * period
            fits = (candidate >= 0) & (candidate < batches)
            slot_id = jnp.where(fits, candidate, slot_id)
            pass_id = jnp.where(fits, pass_now, pass_id)
            active = active | fits
        return (active, slot_id, pass_id)

    def run_block(active, hidden, cond_vec):
        return lax.cond(
            active,
            lambda hidden_in: teacher_block(hidden_in, weights, section_mod, cond_vec),
            lambda hidden_in: hidden_in,
            hidden,
        )

    def tick_entry(tick_now, buffers):
        arrived, iterates = buffers
        active, slot_id, pass_id = locate(own_section, tick_now)
        hidden = lax.dynamic_index_in_dim(arrived, slot_id, 0, keepdims=False)
        start_x = lax.dynamic_index_in_dim(iterates, slot_id, 0, keepdims=False)
        is_first = own_section == 0
        step_size = deltas[slot_id, jnp.maximum(pass_id - 1, 0)]
        advanced = (start_x.astype(jnp.float32) + step_size * hidden.astype(jnp.float32)).astype(
            jnp.bfloat16
        )
        hidden = jnp.where(is_first & (pass_id >= 1), advanced, hidden)
        iterates = store(iterates, hidden, is_first & active, slot_id)
        result = run_block(active, hidden, conditions[slot_id, pass_id])
        got_hidden = from_behind(result, "section", 1)
        valid, source, unused = locate(sender, tick_now)
        arrived = store(arrived, got_hidden, valid, source)
        return (arrived, iterates)

    arrived, iterates = lax.fori_loop(0, tick_count, tick_entry, (noise, noise))
    latest = (
        iterates.astype(jnp.float32)
        + deltas[:, steps - 1][:, None, None] * arrived.astype(jnp.float32)
    ).astype(jnp.bfloat16)
    root_section = 0
    teacher = picked(latest, "section", root_section)
    col_count = student_weight.shape[1]
    first_col = own_section * col_count
    row_count = batches * tokens
    noise_f = noise.astype(jnp.float32)
    cond_zero = conditions[:, 0][:, None, :]
    time_zero = (indices_f[:, 0] / LEVELS)[:, None, None]
    inputs = (
        modulated(noise_f, cond_zero, student_mod)
        .astype(jnp.bfloat16)
        .reshape(row_count, model_width)
    )
    mixed = jnp.dot(inputs, collect(student_weight, DP, 0), preferred_element_type=jnp.float32)
    z_cols = lax.dynamic_slice_in_dim(noise_f, first_col, col_count, 2).reshape(
        row_count, col_count
    )
    gate_full = 1.0 + cond_zero * student_mod[2]
    gate_rows = jnp.broadcast_to(
        lax.dynamic_slice_in_dim(gate_full, first_col, col_count, 2), (batches, tokens, col_count)
    ).reshape(row_count, col_count)
    t_rows = jnp.broadcast_to(time_zero, (batches, tokens, 1)).reshape(row_count, 1)

    def advance(mixed_in):
        return z_cols - t_rows * (z_cols + gate_rows * jax.nn.gelu(mixed_in))

    moved, pull_back = jax.vjp(advance, mixed)
    feat_student = jnp.dot(
        moved.astype(jnp.bfloat16), feature_weight, preferred_element_type=jnp.float32
    )
    target_cols = lax.dynamic_slice_in_dim(teacher, first_col, col_count, 2).reshape(
        row_count, col_count
    )
    feat_teacher = jnp.dot(target_cols, feature_weight, preferred_element_type=jnp.float32)
    share_rows = row_count // sections
    part_student, part_teacher = side_by_side(
        (feat_student.astype(jnp.bfloat16), feat_teacher.astype(jnp.bfloat16)), "section", 0, 1
    )
    weight_share = lax.dynamic_slice_in_dim(token_weight, own_section * share_rows, share_rows, 0)

    def objective(feat_in):
        token_dist = distance(feat_in, part_teacher, lin_weight)
        return (jnp.sum(weight_share * token_dist), token_dist)

    total, pull_feat, token_distance = jax.vjp(objective, part_student, has_aux=True)
    grad_share = pull_feat(jnp.ones_like(total))[0].astype(jnp.bfloat16)
    grad_feat = collect(grad_share, "section", 0)
    out_grad = lax.dot_general(
        grad_feat, feature_weight, (((1,), (1,)), ((), ())), preferred_element_type=jnp.float32
    )
    mixed_grad = pull_back(out_grad)[0].astype(jnp.bfloat16)
    partial_grad = lax.dot_general(
        inputs, mixed_grad, (((0,), (0,)), ((), ())), preferred_element_type=jnp.float32
    )
    student_grad = sum_by_parts(partial_grad.astype(jnp.bfloat16), (("dp_0", "dp_1"), "dp_2"))
    return (teacher, student_grad, token_distance)


def solution(mesh):
    torus = Mesh(
        mesh.devices.reshape(2, 8, 2, mesh.shape["section"]), ("dp_0", "dp_1", "dp_2", "section")
    )
    in_specs = (
        P(DP, None, None),
        P(DP, None),
        P(),
        P(DP, None),
        P(),
        P("section", DP, None),
        P("section", None, None),
        P(DP, "section"),
        P(),
        P("section", None),
        P(),
        P(DP),
    )
    out_specs = (P(DP, None, None), P(None, "section"), P(DP_SECTION))
    return jax.shard_map(local, mesh=torus, in_specs=in_specs, out_specs=out_specs, check_vma=False)
```

profile of v0, /device:TPU:1, one launch (start us, length us, event | category | flops | bytes accessed | tf_op | source)
XLA Modules:
  0.0 550.5 jit_solution(15804008191292427286)
XLA Ops:
  8.7 10.4 %while.33 = (s32[]{:T(128)}, f32[128,1544]{0,1:T(8,128)S(1)}, s32[128,77]{0,1:T(8,128)S(1)}, s32[]{:T(128)}, s32[]{:T(128)}, /*index=5*/s32[]{:T(128)}, s32[]{:T(128)}) while((s32[]{:T(128)}, f32[128,1544]{0,1:T(8,128)S(1)}, s32[128,77]{0,1:T(8,128)S(1)}, s32[]{:T(128)}, s32[]{:T(128)}, /*index=5*/s32[]{:T(128)}, s32[]{:T(128)}) %tuple.112), condition=%wide.region_2.0_spmd.clone, body=%wide.region_0.0_spmd.clone.sunk | while | flops 4347911 | bytes 3173001 | solution.py:146
  23.5 11.1 %all-to-all-start = ((f32[32,4,1536]{2,1,0:T(4,128)}), f32[32,4,1536]{2,1,0:T(4,128)}, u32[]{:S(2)}, u32[]{:S(2)}) async-start(f32[32,4,1536]{2,1,0:T(4,128)} %reshape.121), calls=%async_computation | async-start | bytes 1572864 | tf_op jit(solution)/shard_map/all_to_all | solution.py:22
  36.3 26.8 %all-to-all-done = f32[32,4,1536]{2,1,0:T(4,128)} async-done(((f32[32,4,1536]{2,1,0:T(4,128)}), f32[32,4,1536]{2,1,0:T(4,128)}, u32[]{:S(2)}, u32[]{:S(2)}) %all-to-all-start) | async-done | bytes 786464 | tf_op jit(solution)/shard_map/all_to_all | solution.py:22
  65.9 24.6 %all-gather.4.cloned.1.call-done = bf16[1,1536,1536]{2,1,0:T(8,128)(2,1)} async-done(((bf16[1,48,1536]{2,1,0:T(8,128)(2,1)}), bf16[1,1536,1536]{2,1,0:T(8,128)(2,1)}) %all-gather.4.cloned.1.call-update) | async-done | bytes 4718608 | tf_op jit(solution)/shard_map/all_gather | solution.py:158
  90.5 258.7 %while.32 = (s32[]{:T(128)}, bf16[4,64,1536]{2,1,0:T(8,128)(2,1)S(1)}, bf16[4,64,1536]{2,1,0:T(8,128)(2,1)S(1)}, s32[]{:T(128)}, s32[]{:T(128)}, /*index=5*/pred...) while((s32[]{:T(128)}, ...), condition=%wide.region_8.9_spmd, body=%wide.region_4.8_spmd.sunk | while | flops 305340000 | bytes 8762968 | solution.py:215
  97.3 9.8 %collective-permute-done = bf16[64,1536]{1,0:T(8,128)(2,1)S(1)} collective-permute-done((bf16[64,1536]{1,0:T(8,128)(2,1)S(1)}, bf16[64,1536]{1,0:T(8,128)(2,1)S(1)}, u32[]{:S(2)}, u32[]{:S(2)}) %collective-permute-start) | collective-permute-done | bytes 196640 | tf_op jit(solution)/shard_map/while/body/eval_jaxpr/ppermute | solution.py:29
  114.8 8.9 %collective-permute-done = bf16[64,1536]{1,0:T(8,128)(2,1)S(1)} collective-permute-done((bf16[64,1536]{1,0:T(8,128)(2,1)S(1)}, bf16[64,1536]{1,0:T(8,128)(2,1)S(1)}, u32[]{:S(2)}, u32[]{:S(2)}) %collective-permute-start) | collective-permute-done | bytes 196640 | tf_op jit(solution)/shard_map/while/body/eval_jaxpr/ppermute | solution.py:29
  131.4 8.1 %collective-permute-done = bf16[64,1536]{1,0:T(8,128)(2,1)S(1)} collective-permute-done((bf16[64,1536]{1,0:T(8,128)(2,1)S(1)}, bf16[64,1536]{1,0:T(8,128)(2,1)S(1)}, u32[]{:S(2)}, u32[]{:S(2)}) %collective-permute-start) | collective-permute-done | bytes 196640 | tf_op jit(solution)/shard_map/while/body/eval_jaxpr/ppermute | solution.py:29
  147.2 8.1 %collective-permute-done = bf16[64,1536]{1,0:T(8,128)(2,1)S(1)} collective-permute-done((bf16[64,1536]{1,0:T(8,128)(2,1)S(1)}, bf16[64,1536]{1,0:T(8,128)(2,1)S(1)}, u32[]{:S(2)}, u32[]{:S(2)}) %collective-permute-start) | collective-permute-done | bytes 196640 | tf_op jit(solution)/shard_map/while/body/eval_jaxpr/ppermute | solution.py:29
  189.6 7.6 %collective-permute-done = bf16[64,1536]{1,0:T(8,128)(2,1)S(1)} collective-permute-done((bf16[64,1536]{1,0:T(8,128)(2,1)S(1)}, bf16[64,1536]{1,0:T(8,128)(2,1)S(1)}, u32[]{:S(2)}, u32[]{:S(2)}) %collective-permute-start) | collective-permute-done | bytes 196640 | tf_op jit(solution)/shard_map/while/body/eval_jaxpr/ppermute | solution.py:29
  205.0 8.1 %collective-permute-done = bf16[64,1536]{1,0:T(8,128)(2,1)S(1)} collective-permute-done((bf16[64,1536]{1,0:T(8,128)(2,1)S(1)}, bf16[64,1536]{1,0:T(8,128)(2,1)S(1)}, u32[]{:S(2)}, u32[]{:S(2)}) %collective-permute-start) | collective-permute-done | bytes 196640 | tf_op jit(solution)/shard_map/while/body/eval_jaxpr/ppermute | solution.py:29
  220.8 8.1 %collective-permute-done = bf16[64,1536]{1,0:T(8,128)(2,1)S(1)} collective-permute-done((bf16[64,1536]{1,0:T(8,128)(2,1)S(1)}, bf16[64,1536]{1,0:T(8,128)(2,1)S(1)}, u32[]{:S(2)}, u32[]{:S(2)}) %collective-permute-start) | collective-permute-done | bytes 196640 | tf_op jit(solution)/shard_map/while/body/eval_jaxpr/ppermute | solution.py:29
  236.5 8.1 %collective-permute-done = bf16[64,1536]{1,0:T(8,128)(2,1)S(1)} collective-permute-done((bf16[64,1536]{1,0:T(8,128)(2,1)S(1)}, bf16[64,1536]{1,0:T(8,128)(2,1)S(1)}, u32[]{:S(2)}, u32[]{:S(2)}) %collective-permute-start) | collective-permute-done | bytes 196640 | tf_op jit(solution)/shard_map/while/body/eval_jaxpr/ppermute | solution.py:29
  252.3 8.1 %collective-permute-done = bf16[64,1536]{1,0:T(8,128)(2,1)S(1)} collective-permute-done((bf16[64,1536]{1,0:T(8,128)(2,1)S(1)}, bf16[64,1536]{1,0:T(8,128)(2,1)S(1)}, u32[]{:S(2)}, u32[]{:S(2)}) %collective-permute-start) | collective-permute-done | bytes 196640 | tf_op jit(solution)/shard_map/while/body/eval_jaxpr/ppermute | solution.py:29
  306.0 12.7 %collective-permute-done = bf16[64,1536]{1,0:T(8,128)(2,1)S(1)} collective-permute-done((bf16[64,1536]{1,0:T(8,128)(2,1)S(1)}, bf16[64,1536]{1,0:T(8,128)(2,1)S(1)}, u32[]{:S(2)}, u32[]{:S(2)}) %collective-permute-start) | collective-permute-done | bytes 196640 | tf_op jit(solution)/shard_map/while/body/eval_jaxpr/ppermute | solution.py:29
  321.1 13.0 %collective-permute-done = bf16[64,1536]{1,0:T(8,128)(2,1)S(1)} collective-permute-done((bf16[64,1536]{1,0:T(8,128)(2,1)S(1)}, bf16[64,1536]{1,0:T(8,128)(2,1)S(1)}, u32[]{:S(2)}, u32[]{:S(2)}) %collective-permute-start) | collective-permute-done | bytes 196640 | tf_op jit(solution)/shard_map/while/body/eval_jaxpr/ppermute | solution.py:29
  336.5 11.9 %collective-permute-done = bf16[64,1536]{1,0:T(8,128)(2,1)S(1)} collective-permute-done((bf16[64,1536]{1,0:T(8,128)(2,1)S(1)}, bf16[64,1536]{1,0:T(8,128)(2,1)S(1)}, u32[]{:S(2)}, u32[]{:S(2)}) %collective-permute-start) | collective-permute-done | bytes 196640 | tf_op jit(solution)/shard_map/while/body/eval_jaxpr/ppermute | solution.py:29
  351.4 24.4 %all-to-all-start.1 = ((bf16[32,48,192]{2,1,0:T(8,128)(2,1)}), bf16[32,48,192]{2,1,0:T(8,128)(2,1)S(1)}, u32[]{:S(2)}, u32[]{:S(2)}) async-start(bf16[32,48,192]{2,1,0:T(8,128)(2,1)} %broadcast_in_dim.73), calls=%async_computation.1 | async-start | bytes 1572864 | tf_op jit(solution)/shard_map/all_to_all | solution.py:44
  381.7 15.4 %all-to-all-done.1 = bf16[32,48,192]{2,1,0:T(8,128)(2,1)S(1)} async-done(((bf16[32,48,192]{2,1,0:T(8,128)(2,1)}), bf16[32,48,192]{2,1,0:T(8,128)(2,1)S(1)}, u32[]{:S(2)}, u32[]{:S(2)}) %all-to-all-start.1) | async-done | bytes 589856 | tf_op jit(solution)/shard_map/all_to_all | solution.py:44
  397.9 66.6 %all-gather.6.cloned.1.call-done = bf16[32,64,1536]{2,1,0:T(8,128)(2,1)} async-done(((bf16[4,64,1536]{2,1,0:T(8,128)(2,1)}), bf16[32,64,1536]{2,1,0:T(8,128)(2,1)}) %all-gather.6.cloned.1.call-update) | async-done | bytes 6291472 | tf_op jit(solution)/shard_map/all_gather | solution.py:33
  470.5 10.4 %all-to-all-done.2 = bf16[8,32,1024]{2,1,0:T(8,128)(2,1)S(1)} async-done(((bf16[8,32,1024]{2,1,0:T(8,128)(2,1)}), bf16[8,32,1024]{2,1,0:T(8,128)(2,1)S(1)}, u32[]{:S(2)}, u32[]{:S(2)}) %all-to-all-start.2) | async-done | bytes 524320 | tf_op jit(solution)/shard_map/all_to_all | solution.py:53
  482.0 10.3 %all_to_all.40 = bf16[8,32,512]{2,1,0:T(8,128)(2,1)S(1)} all-to-all(bf16[8,32,512]{2,1,0:T(8,128)(2,1)S(1)} %broadcast_in_dim.76), channel_id=1, replica_groups=mesh['dp_0'=2,'dp_1'=8,'dp_2'=2,'section'=8] {'section'}, dimensions={0} | all-to-all | bytes 524288 | tf_op jit(solution)/shard_map/all_to_all | solution.py:44
  500.6 17.8 %all_to_all.42 = bf16[16,48,192]{2,1,0:T(8,128)(2,1)S(1)} all-to-all(bf16[16,48,192]{2,1,0:T(8,128)(2,1)S(1)} %reduce_sum.120), channel_id=1, replica_groups=mesh['dp_0'=2,'dp_1'=8,'dp_2'=2,'section'=8] {'dp_0','dp_1'}, dimensions={0} | all-to-all | bytes 589824 | tf_op jit(solution)/shard_map/all_to_all | solution.py:80
  518.5 16.9 %all_to_all.43 = bf16[16,48,192]{2,1,0:T(8,128)(2,1)S(1)} all-to-all(bf16[16,48,192]{2,1,0:T(8,128)(2,1)S(1)} %broadcast_in_dim.77), channel_id=1, replica_groups=mesh['dp_0'=2,'dp_1'=8,'dp_2'=2,'section'=8] {'dp_0','dp_1'}, dimensions={0} | all-to-all | bytes 589824 | tf_op jit(solution)/shard_map/all_to_all | solution.py:44
  (299 shorter events, 239.5 us)
Async XLA Ops:
  7.2 83.3 %all-gather.4.cloned.1.call-start = ((), (), s32[]{:S(2)}) async-start(), calls=%async_computation.8 | async-start | bytes 4866048 | tf_op jit(solution)/shard_map/all_gather | solution.py:158
  23.5 39.6 %all-to-all-start = ((f32[32,4,1536]{2,1,0:T(4,128)}), f32[32,4,1536]{2,1,0:T(4,128)}, u32[]{:S(2)}, u32[]{:S(2)}) async-start(f32[32,4,1536]{2,1,0:T(4,128)} %reshape.121), calls=%async_computation | async-start | bytes 1572864 | tf_op jit(solution)/shard_map/all_to_all | solution.py:22
  34.6 429.8 %all-gather.6.cloned.1.call-start = ((), (), s32[]{:S(2)}) async-start(), calls=%async_computation.9 | async-start | bytes 7077888 | tf_op jit(solution)/shard_map/all_gather | solution.py:33
  97.2 9.9 %collective-permute-start = (bf16[64,1536]{1,0:T(8,128)(2,1)S(1)}, bf16[64,1536]{1,0:T(8,128)(2,1)S(1)}, u32[]{:S(2)}, u32[]{:S(2)}) collective-permute-start(bf16[64,1536]{1,0:T(8,128)(2,1)S(1)} %get-tuple-element.648), channel_id=1, source_target_pairs={{7,0},{0,1},{1,2},{2,3},{3,4},{4,5},{5,6},{6,7},{15,8},{8,9},{9,10... | collective-permute-start | bytes 589832 | tf_op jit(solution)/shard_map/while/body/eval_jaxpr/ppermute | solution.py:29
  114.7 9.0 %collective-permute-start = (bf16[64,1536]{1,0:T(8,128)(2,1)S(1)}, bf16[64,1536]{1,0:T(8,128)(2,1)S(1)}, u32[]{:S(2)}, u32[]{:S(2)}) collective-permute-start(bf16[64,1536]{1,0:T(8,128)(2,1)S(1)} %get-tuple-element.648), channel_id=1, source_target_pairs={{7,0},{0,1},{1,2},{2,3},{3,4},{4,5},{5,6},{6,7},{15,8},{8,9},{9,10... | collective-permute-start | bytes 589832 | tf_op jit(solution)/shard_map/while/body/eval_jaxpr/ppermute | solution.py:29
  131.2 8.2 %collective-permute-start = (bf16[64,1536]{1,0:T(8,128)(2,1)S(1)}, bf16[64,1536]{1,0:T(8,128)(2,1)S(1)}, u32[]{:S(2)}, u32[]{:S(2)}) collective-permute-start(bf16[64,1536]{1,0:T(8,128)(2,1)S(1)} %get-tuple-element.648), channel_id=1, source_target_pairs={{7,0},{0,1},{1,2},{2,3},{3,4},{4,5},{5,6},{6,7},{15,8},{8,9},{9,10... | collective-permute-start | bytes 589832 | tf_op jit(solution)/shard_map/while/body/eval_jaxpr/ppermute | solution.py:29
  147.0 8.2 %collective-permute-start = (bf16[64,1536]{1,0:T(8,128)(2,1)S(1)}, bf16[64,1536]{1,0:T(8,128)(2,1)S(1)}, u32[]{:S(2)}, u32[]{:S(2)}) collective-permute-start(bf16[64,1536]{1,0:T(8,128)(2,1)S(1)} %get-tuple-element.648), channel_id=1, source_target_pairs={{7,0},{0,1},{1,2},{2,3},{3,4},{4,5},{5,6},{6,7},{15,8},{8,9},{9,10... | collective-permute-start | bytes 589832 | tf_op jit(solution)/shard_map/while/body/eval_jaxpr/ppermute | solution.py:29
  157.5 8.2 %collective-permute-start = (bf16[64,1536]{1,0:T(8,128)(2,1)S(1)}, bf16[64,1536]{1,0:T(8,128)(2,1)S(1)}, u32[]{:S(2)}, u32[]{:S(2)}) collective-permute-start(bf16[64,1536]{1,0:T(8,128)(2,1)S(1)} %get-tuple-element.648), channel_id=1, source_target_pairs={{7,0},{0,1},{1,2},{2,3},{3,4},{4,5},{5,6},{6,7},{15,8},{8,9},{9,10... | collective-permute-start | bytes 589832 | tf_op jit(solution)/shard_map/while/body/eval_jaxpr/ppermute | solution.py:29
  168.0 8.2 %collective-permute-start = (bf16[64,1536]{1,0:T(8,128)(2,1)S(1)}, bf16[64,1536]{1,0:T(8,128)(2,1)S(1)}, u32[]{:S(2)}, u32[]{:S(2)}) collective-permute-start(bf16[64,1536]{1,0:T(8,128)(2,1)S(1)} %get-tuple-element.648), channel_id=1, source_target_pairs={{7,0},{0,1},{1,2},{2,3},{3,4},{4,5},{5,6},{6,7},{15,8},{8,9},{9,10... | collective-permute-start | bytes 589832 | tf_op jit(solution)/shard_map/while/body/eval_jaxpr/ppermute | solution.py:29
  178.5 8.2 %collective-permute-start = (bf16[64,1536]{1,0:T(8,128)(2,1)S(1)}, bf16[64,1536]{1,0:T(8,128)(2,1)S(1)}, u32[]{:S(2)}, u32[]{:S(2)}) collective-permute-start(bf16[64,1536]{1,0:T(8,128)(2,1)S(1)} %get-tuple-element.648), channel_id=1, source_target_pairs={{7,0},{0,1},{1,2},{2,3},{3,4},{4,5},{5,6},{6,7},{15,8},{8,9},{9,10... | collective-permute-start | bytes 589832 | tf_op jit(solution)/shard_map/while/body/eval_jaxpr/ppermute | solution.py:29
  189.0 8.2 %collective-permute-start = (bf16[64,1536]{1,0:T(8,128)(2,1)S(1)}, bf16[64,1536]{1,0:T(8,128)(2,1)S(1)}, u32[]{:S(2)}, u32[]{:S(2)}) collective-permute-start(bf16[64,1536]{1,0:T(8,128)(2,1)S(1)} %get-tuple-element.648), channel_id=1, source_target_pairs={{7,0},{0,1},{1,2},{2,3},{3,4},{4,5},{5,6},{6,7},{15,8},{8,9},{9,10... | collective-permute-start | bytes 589832 | tf_op jit(solution)/shard_map/while/body/eval_jaxpr/ppermute | solution.py:29
  204.8 8.2 %collective-permute-start = (bf16[64,1536]{1,0:T(8,128)(2,1)S(1)}, bf16[64,1536]{1,0:T(8,128)(2,1)S(1)}, u32[]{:S(2)}, u32[]{:S(2)}) collective-permute-start(bf16[64,1536]{1,0:T(8,128)(2,1)S(1)} %get-tuple-element.648), channel_id=1, source_target_pairs={{7,0},{0,1},{1,2},{2,3},{3,4},{4,5},{5,6},{6,7},{15,8},{8,9},{9,10... | collective-permute-start | bytes 589832 | tf_op jit(solution)/shard_map/while/body/eval_jaxpr/ppermute | solution.py:29
  220.6 8.2 %collective-permute-start = (bf16[64,1536]{1,0:T(8,128)(2,1)S(1)}, bf16[64,1536]{1,0:T(8,128)(2,1)S(1)}, u32[]{:S(2)}, u32[]{:S(2)}) collective-permute-start(bf16[64,1536]{1,0:T(8,128)(2,1)S(1)} %get-tuple-element.648), channel_id=1, source_target_pairs={{7,0},{0,1},{1,2},{2,3},{3,4},{4,5},{5,6},{6,7},{15,8},{8,9},{9,10... | collective-permute-start | bytes 589832 | tf_op jit(solution)/shard_map/while/body/eval_jaxpr/ppermute | solution.py:29
  236.4 8.2 %collective-permute-start = (bf16[64,1536]{1,0:T(8,128)(2,1)S(1)}, bf16[64,1536]{1,0:T(8,128)(2,1)S(1)}, u32[]{:S(2)}, u32[]{:S(2)}) collective-permute-start(bf16[64,1536]{1,0:T(8,128)(2,1)S(1)} %get-tuple-element.648), channel_id=1, source_target_pairs={{7,0},{0,1},{1,2},{2,3},{3,4},{4,5},{5,6},{6,7},{15,8},{8,9},{9,10... | collective-permute-start | bytes 589832 | tf_op jit(solution)/shard_map/while/body/eval_jaxpr/ppermute | solution.py:29
  252.2 8.2 %collective-permute-start = (bf16[64,1536]{1,0:T(8,128)(2,1)S(1)}, bf16[64,1536]{1,0:T(8,128)(2,1)S(1)}, u32[]{:S(2)}, u32[]{:S(2)}) collective-permute-start(bf16[64,1536]{1,0:T(8,128)(2,1)S(1)} %get-tuple-element.648), channel_id=1, source_target_pairs={{7,0},{0,1},{1,2},{2,3},{3,4},{4,5},{5,6},{6,7},{15,8},{8,9},{9,10... | collective-permute-start | bytes 589832 | tf_op jit(solution)/shard_map/while/body/eval_jaxpr/ppermute | solution.py:29
  262.7 8.2 %collective-permute-start = (bf16[64,1536]{1,0:T(8,128)(2,1)S(1)}, bf16[64,1536]{1,0:T(8,128)(2,1)S(1)}, u32[]{:S(2)}, u32[]{:S(2)}) collective-permute-start(bf16[64,1536]{1,0:T(8,128)(2,1)S(1)} %get-tuple-element.648), channel_id=1, source_target_pairs={{7,0},{0,1},{1,2},{2,3},{3,4},{4,5},{5,6},{6,7},{15,8},{8,9},{9,10... | collective-permute-start | bytes 589832 | tf_op jit(solution)/shard_map/while/body/eval_jaxpr/ppermute | solution.py:29
  273.2 8.2 %collective-permute-start = (bf16[64,1536]{1,0:T(8,128)(2,1)S(1)}, bf16[64,1536]{1,0:T(8,128)(2,1)S(1)}, u32[]{:S(2)}, u32[]{:S(2)}) collective-permute-start(bf16[64,1536]{1,0:T(8,128)(2,1)S(1)} %get-tuple-element.648), channel_id=1, source_target_pairs={{7,0},{0,1},{1,2},{2,3},{3,4},{4,5},{5,6},{6,7},{15,8},{8,9},{9,10... | collective-permute-start | bytes 589832 | tf_op jit(solution)/shard_map/while/body/eval_jaxpr/ppermute | solution.py:29
  283.7 8.2 %collective-permute-start = (bf16[64,1536]{1,0:T(8,128)(2,1)S(1)}, bf16[64,1536]{1,0:T(8,128)(2,1)S(1)}, u32[]{:S(2)}, u32[]{:S(2)}) collective-permute-start(bf16[64,1536]{1,0:T(8,128)(2,1)S(1)} %get-tuple-element.648), channel_id=1, source_target_pairs={{7,0},{0,1},{1,2},{2,3},{3,4},{4,5},{5,6},{6,7},{15,8},{8,9},{9,10... | collective-permute-start | bytes 589832 | tf_op jit(solution)/shard_map/while/body/eval_jaxpr/ppermute | solution.py:29
  294.2 8.2 %collective-permute-start = (bf16[64,1536]{1,0:T(8,128)(2,1)S(1)}, bf16[64,1536]{1,0:T(8,128)(2,1)S(1)}, u32[]{:S(2)}, u32[]{:S(2)}) collective-permute-start(bf16[64,1536]{1,0:T(8,128)(2,1)S(1)} %get-tuple-element.648), channel_id=1, source_target_pairs={{7,0},{0,1},{1,2},{2,3},{3,4},{4,5},{5,6},{6,7},{15,8},{8,9},{9,10... | collective-permute-start | bytes 589832 | tf_op jit(solution)/shard_map/while/body/eval_jaxpr/ppermute | solution.py:29
  304.7 14.0 %collective-permute-start = (bf16[64,1536]{1,0:T(8,128)(2,1)S(1)}, bf16[64,1536]{1,0:T(8,128)(2,1)S(1)}, u32[]{:S(2)}, u32[]{:S(2)}) collective-permute-start(bf16[64,1536]{1,0:T(8,128)(2,1)S(1)} %get-tuple-element.648), channel_id=1, source_target_pairs={{7,0},{0,1},{1,2},{2,3},{3,4},{4,5},{5,6},{6,7},{15,8},{8,9},{9,10... | collective-permute-start | bytes 589832 | tf_op jit(solution)/shard_map/while/body/eval_jaxpr/ppermute | solution.py:29
  320.9 13.1 %collective-permute-start = (bf16[64,1536]{1,0:T(8,128)(2,1)S(1)}, bf16[64,1536]{1,0:T(8,128)(2,1)S(1)}, u32[]{:S(2)}, u32[]{:S(2)}) collective-permute-start(bf16[64,1536]{1,0:T(8,128)(2,1)S(1)} %get-tuple-element.648), channel_id=1, source_target_pairs={{7,0},{0,1},{1,2},{2,3},{3,4},{4,5},{5,6},{6,7},{15,8},{8,9},{9,10... | collective-permute-start | bytes 589832 | tf_op jit(solution)/shard_map/while/body/eval_jaxpr/ppermute | solution.py:29
  336.4 12.0 %collective-permute-start = (bf16[64,1536]{1,0:T(8,128)(2,1)S(1)}, bf16[64,1536]{1,0:T(8,128)(2,1)S(1)}, u32[]{:S(2)}, u32[]{:S(2)}) collective-permute-start(bf16[64,1536]{1,0:T(8,128)(2,1)S(1)} %get-tuple-element.648), channel_id=1, source_target_pairs={{7,0},{0,1},{1,2},{2,3},{3,4},{4,5},{5,6},{6,7},{15,8},{8,9},{9,10... | collective-permute-start | bytes 589832 | tf_op jit(solution)/shard_map/while/body/eval_jaxpr/ppermute | solution.py:29
  351.4 45.6 %all-to-all-start.1 = ((bf16[32,48,192]{2,1,0:T(8,128)(2,1)}), bf16[32,48,192]{2,1,0:T(8,128)(2,1)S(1)}, u32[]{:S(2)}, u32[]{:S(2)}) async-start(bf16[32,48,192]{2,1,0:T(8,128)(2,1)} %broadcast_in_dim.73), calls=%async_computation.1 | async-start | bytes 1572864 | tf_op jit(solution)/shard_map/all_to_all | solution.py:44
  466.9 14.0 %all-to-all-start.2 = ((bf16[8,32,1024]{2,1,0:T(8,128)(2,1)}), bf16[8,32,1024]{2,1,0:T(8,128)(2,1)S(1)}, u32[]{:S(2)}, u32[]{:S(2)}) async-start(bf16[8,32,1024]{2,1,0:T(8,128)(2,1)} %bitcast.17), calls=%async_computation.2 | async-start | bytes 1048576 | tf_op jit(solution)/shard_map/all_to_all | solution.py:53
  (13 other events, 248.8 us)
Sparse Core Ops, SparseCore 0:
  9.9 80.5 all-gather.3
  350.6 113.7 all-gather.5
where the time goes:
time: 553 us; the launch traced here: 551 us
  waiting for transfers between devices  296 us (54%)
  starting transfers between devices  59.4 us (11%)
  blocking collectives  58.4 us (11%)
  other arithmetic  50.8 us (9%)
  local copies, waits for them, and re-layouts  36.1 us (7%)
  matrix products  32.4 us (6%)
  between operations  14.5 us (3%)
    ppermute x19, waiting for transfers between devices, from_behind(): return lax.ppermute(block, axis, route)  152 us
    all_gather x1, waiting for transfers between devices, picked(): lax.all_gather(x, axis)  66.6 us
    all_to_all x3, blocking collectives, from_everyone(): return lax.all_to_all(copies, axis, split_axis=0, concat_axis=0, tiled=True)  33.7 us
    dot_general x8, matrix products, teacher_block(): mixed = jnp.dot(inputs, weight, preferred_element_type=jnp.float32)  27.2 us
    all_to_all x1, waiting for transfers between devices, summed_on_arrival(): lax.all_to_all(blocks, axis, split_axis=0, concat_axis=0, tiled=True)  26.8 us
    all_gather x1, waiting for transfers between devices, local(): weights = lax.all_gather(block_weight, DP, axis=1, tiled=True)[0]  24.6 us
    all_to_all x1, starting transfers between devices, from_everyone(): return lax.all_to_all(copies, axis, split_axis=0, concat_axis=0, tiled=True)  24.4 us
    ppermute x19, starting transfers between devices, from_behind(): return lax.ppermute(block, axis, route)  20.4 us
  transfers between devices with their start and end apart: 24, of which 24 were waited for; matrix products, arithmetic and copies ran while one was open for 5% of the time, Pallas kernels for 0%

commit v1 on v0

--- a/solution.py
+++ b/solution.py
@@ -3,12 +3,15 @@
 import jax
 import jax.numpy as jnp
 from jax import lax
+from jax.experimental import pallas as pl
+from jax.experimental.pallas import tpu as pltpu
 from jax.sharding import Mesh
 from jax.sharding import PartitionSpec as P
 
 LEVELS = 1000
-DP = ("dp_0", "dp_1", "dp_2")
-DP_SECTION = ("dp_0", "dp_1", "dp_2", "section")
+DP = ("dp_x", "dp_z", "dp_c")
+DP_SECTION = ("dp_x", "dp_z", "dp_c", "section")
+MESH = pl.DeviceIdType.MESH
 
 
 def in_blocks(x, dim, count):
@@ -21,16 +24,6 @@
     blocks = in_blocks(x, dim, lax.axis_size(axis))
     arrived = lax.all_to_all(blocks, axis, split_axis=0, concat_axis=0, tiled=True)
     return arrived.sum(axis=0)
-
-
-def from_behind(block, axis, distance):
-    devices = range(lax.axis_size(axis))
-    route = [((i - distance) % len(devices), i) for i in devices]
-    return lax.ppermute(block, axis, route)
-
-
-def picked(x, axis, root):
-    return lax.dynamic_index_in_dim(lax.all_gather(x, axis), root, 0, keepdims=False)
 
 
 def in_order(blocks, dim):
@@ -110,9 +103,188 @@
     return jnp.sum(lin_weight * gap * gap, axis=-1)
 
 
-def store(buffer, value, valid, slot_id):
-    old_value = lax.dynamic_index_in_dim(buffer, slot_id, 0, keepdims=False)
-    return lax.dynamic_update_index_in_dim(buffer, jnp.where(valid, value, old_value), slot_id, 0)
+def teacher_kernel(
+    noise_ref,
+    w_ref,
+    gains_ref,
+    delta_ref,
+    out_ref,
+    held,
+    sent,
+    inbox,
+    start_x,
+    first_x,
+    inbox_recv,
+    sent_send,
+    first_send,
+    first_recv,
+    out_send,
+    out_recv,
+):
+    mbs, rows, width = noise_ref.shape
+    xl = lax.axis_index("dp_x")
+    sec = lax.axis_index("section")
+    barrier = pltpu.get_barrier_semaphore()
+    for dx in range(2):
+        for ds in range(8):
+            if dx + ds > 0:
+                pl.semaphore_signal(
+                    barrier,
+                    inc=1,
+                    device_id={"dp_x": (xl + dx) % 2, "section": (sec + ds) % 8},
+                    device_id_type=MESH,
+                )
+    pl.semaphore_wait(barrier, 15)
+
+    def pass_on(t, slot, target):
+        return pltpu.make_async_remote_copy(
+            src_ref=sent.at[t],
+            dst_ref=inbox.at[slot],
+            send_sem=sent_send.at[t],
+            recv_sem=inbox_recv.at[slot],
+            device_id={"dp_x": 1 - xl, "section": target},
+            device_id_type=MESH,
+        )
+
+    def share_first(j):
+        return pltpu.make_async_remote_copy(
+            src_ref=start_x.at[j],
+            dst_ref=first_x,
+            send_sem=first_send.at[j],
+            recv_sem=first_recv,
+            device_id={"section": j},
+            device_id_type=MESH,
+        )
+
+    def share_out(slot, target):
+        return pltpu.make_async_remote_copy(
+            src_ref=out_ref.at[slot],
+            dst_ref=out_ref.at[slot],
+            send_sem=out_send.at[target],
+            recv_sem=out_recv.at[slot],
+            device_id={"section": target},
+            device_id_type=MESH,
+        )
+
+    def run_pass(p):
+        def step(j, carry):
+            t = p * mbs + j
+            if p == 0:
+
+                @pl.when(sec == 0)
+                def _():
+                    held[...] = noise_ref[j]
+
+            @pl.when((sec > 0) | (p > 0))
+            def _():
+                pass_on(t, t, 0).wait_recv()
+                held[...] = inbox[t]
+
+            if p > 0:
+
+                @pl.when(sec == 0)
+                def _():
+                    moved = (
+                        noise_ref[j].astype(jnp.float32)
+                        + delta_ref[j // 2][:, :1] * held[...].astype(jnp.float32)
+                    ).astype(jnp.bfloat16)
+                    held[...] = moved
+                    start_x[j] = moved
+
+                    @pl.when(j == 0)
+                    def _():
+                        first_x[...] = moved
+
+                    @pl.when(j > 0)
+                    def _():
+                        share_first(j).start()
+
+            hidden = held[...].astype(jnp.float32)
+            mean_sq = jnp.mean(hidden * hidden, axis=-1, keepdims=True)
+            row = p * 4 + j // 2
+            inputs = (
+                hidden * lax.rsqrt(mean_sq + 1e-06) * gains_ref[0, row] + gains_ref[1, row]
+            ).astype(jnp.bfloat16)
+            chunk = 512
+            for c in range(width // chunk):
+                cols = pl.ds(c * chunk, chunk)
+                mixed = jnp.dot(inputs, w_ref[:, cols], preferred_element_type=jnp.float32)
+                sent[t, :, cols] = (
+                    held[:, cols].astype(jnp.float32)
+                    + gains_ref[2, row, :, cols] * jax.nn.gelu(mixed)
+                ).astype(jnp.bfloat16)
+
+            @pl.when(sec < 7)
+            def _():
+                pass_on(t, t, sec + 1).start()
+
+            @pl.when(sec == 7)
+            def _():
+                if p == 0:
+                    pass_on(t, t + mbs, 0).start()
+                else:
+                    pass_on(t, 2 * mbs, j).start()
+
+            return carry
+
+        lax.fori_loop(0, mbs, step, 0)
+
+    run_pass(0)
+    run_pass(1)
+    pass_on(0, 2 * mbs, 0).wait_recv()
+
+    @pl.when(sec > 0)
+    def _():
+        share_first(0).wait_recv()
+
+    out_ref[sec] = (
+        first_x[...].astype(jnp.float32)
+        + delta_ref[4 + sec // 2][:, :1] * inbox[2 * mbs].astype(jnp.float32)
+    ).astype(jnp.bfloat16)
+    for ds in range(1, 8):
+        share_out(sec, (sec + ds) % 8).start()
+
+    def drain(t, carry):
+        pass_on(t, t, 0).wait_send()
+        return carry
+
+    lax.fori_loop(0, 2 * mbs, drain, 0)
+
+    @pl.when(sec == 0)
+    def _():
+        for j in range(1, 8):
+            share_first(j).wait_send()
+
+    for ds in range(1, 8):
+        share_out((sec + ds) % 8, (sec + ds) % 8).wait_recv()
+        share_out(sec, (sec + ds) % 8).wait_send()
+
+
+def run_teacher(noise, weights, gains, delta):
+    mbs, rows, width = noise.shape
+    vmem = pl.BlockSpec(memory_space=pltpu.VMEM)
+    return pl.pallas_call(
+        teacher_kernel,
+        out_shape=jax.ShapeDtypeStruct((mbs, rows, width), jnp.bfloat16),
+        in_specs=[vmem] * 4,
+        out_specs=vmem,
+        scratch_shapes=[
+            pltpu.VMEM((rows, width), jnp.bfloat16),
+            pltpu.VMEM((2 * mbs, rows, width), jnp.bfloat16),
+            pltpu.VMEM((2 * mbs + 1, rows, width), jnp.bfloat16),
+            pltpu.VMEM((mbs, rows, width), jnp.bfloat16),
+            pltpu.VMEM((rows, width), jnp.bfloat16),
+            pltpu.SemaphoreType.DMA((2 * mbs + 1,)),
+            pltpu.SemaphoreType.DMA((2 * mbs,)),
+            pltpu.SemaphoreType.DMA((mbs,)),
+            pltpu.SemaphoreType.DMA,
+            pltpu.SemaphoreType.DMA((mbs,)),
+            pltpu.SemaphoreType.DMA((mbs,)),
+        ],
+        compiler_params=pltpu.CompilerParams(
+            collective_id=0, has_side_effects=True, vmem_limit_bytes=40 * 1024 * 1024
+        ),
+    )(noise, weights, gains, delta)
 
 
 def local(
@@ -160,65 +332,42 @@
     indices_f = sched_index.astype(jnp.float32)
     half_freq = time_weight.shape[0] // 2
     frequency = jnp.exp(-math.log(10000.0) * jnp.arange(half_freq, dtype=jnp.float32) / half_freq)
-    angles = indices_f[:, :, None] * frequency
-    embedding = jnp.concatenate([jnp.cos(angles), jnp.sin(angles)], axis=-1).astype(jnp.bfloat16)
-    time_embed = jnp.dot(
-        embedding.reshape(-1, 2 * half_freq), time_weight, preferred_element_type=jnp.float32
-    )
-    conditions = jax.nn.silu(
-        time_embed.reshape(batches, steps + 1, model_width) + pooled[:, None, :]
-    )
+
+    def conditions_of(pooled_in, indices_in):
+        angles = indices_in[:, :, None] * frequency
+        embedding = jnp.concatenate([jnp.cos(angles), jnp.sin(angles)], axis=-1)
+        time_embed = jnp.dot(
+            embedding.astype(jnp.bfloat16).reshape(-1, 2 * half_freq),
+            time_weight,
+            preferred_element_type=jnp.float32,
+        )
+        return jax.nn.silu(
+            time_embed.reshape(batches, steps + 1, model_width) + pooled_in[:, None, :]
+        )
+
+    conditions = conditions_of(pooled, indices_f)
     deltas = (indices_f[:, 1:] - indices_f[:, :-1]) / LEVELS
-    surplus = max(0, batches - sections)
-    period = sections + surplus
-    tick_count = steps * sections + batches - 1 + (steps - 1) * surplus
-    sender = (own_section + sections - 1) % sections
-
-    def locate(section_at, tick_now):
-        active = jnp.zeros((), jnp.bool_)
-        slot_id = jnp.zeros((), jnp.int32)
-        pass_id = jnp.zeros((), jnp.int32)
-        for pass_now in range(steps):
-            candidate = tick_now - section_at - pass_now * period
-            fits = (candidate >= 0) & (candidate < batches)
-            slot_id = jnp.where(fits, candidate, slot_id)
-            pass_id = jnp.where(fits, pass_now, pass_id)
-            active = active | fits
-        return (active, slot_id, pass_id)
-
-    def run_block(active, hidden, cond_vec):
-        return lax.cond(
-            active,
-            lambda hidden_in: teacher_block(hidden_in, weights, section_mod, cond_vec),
-            lambda hidden_in: hidden_in,
-            hidden,
-        )
-
-    def tick_entry(tick_now, buffers):
-        arrived, iterates = buffers
-        active, slot_id, pass_id = locate(own_section, tick_now)
-        hidden = lax.dynamic_index_in_dim(arrived, slot_id, 0, keepdims=False)
-        start_x = lax.dynamic_index_in_dim(iterates, slot_id, 0, keepdims=False)
-        is_first = own_section == 0
-        step_size = deltas[slot_id, jnp.maximum(pass_id - 1, 0)]
-        advanced = (start_x.astype(jnp.float32) + step_size * hidden.astype(jnp.float32)).astype(
-            jnp.bfloat16
-        )
-        hidden = jnp.where(is_first & (pass_id >= 1), advanced, hidden)
-        iterates = store(iterates, hidden, is_first & active, slot_id)
-        result = run_block(active, hidden, conditions[slot_id, pass_id])
-        got_hidden = from_behind(result, "section", 1)
-        valid, source, unused = locate(sender, tick_now)
-        arrived = store(arrived, got_hidden, valid, source)
-        return (arrived, iterates)
-
-    arrived, iterates = lax.fori_loop(0, tick_count, tick_entry, (noise, noise))
-    latest = (
-        iterates.astype(jnp.float32)
-        + deltas[:, steps - 1][:, None, None] * arrived.astype(jnp.float32)
-    ).astype(jnp.bfloat16)
-    root_section = 0
-    teacher = picked(latest, "section", root_section)
+    packed = jnp.concatenate(
+        [pooled, jnp.pad(indices_f, ((0, 0), (0, 128 - steps - 1)))], axis=1
+    )
+    other = lax.ppermute(packed, "dp_x", [(0, 1), (1, 0)])
+    odd = own_section % 2 == 1
+    packed = jnp.where(odd, other, packed)
+    pipe_cond = conditions_of(
+        packed[:, :model_width], packed[:, model_width : model_width + steps + 1]
+    )
+    pipe_cond = jnp.moveaxis(pipe_cond[:, :steps], 1, 0).reshape(1, steps * batches, 1, model_width)
+    ones = jnp.array([1.0, 0.0, 1.0], jnp.float32)[:, None, None, None]
+    gains = ones + pipe_cond * section_mod[:, None, None, :]
+    delta_lanes = jnp.broadcast_to(
+        jnp.moveaxis(deltas, 1, 0).reshape(steps * batches, 1, 1), (steps * batches, 1, 128)
+    )
+    teacher = run_teacher(
+        noise.reshape(sections, batches * tokens // sections, model_width),
+        weights,
+        gains,
+        delta_lanes,
+    ).reshape(noise.shape)
     col_count = student_weight.shape[1]
     first_col = own_section * col_count
     row_count = batches * tokens
@@ -271,13 +420,13 @@
     partial_grad = lax.dot_general(
         inputs, mixed_grad, (((0,), (0,)), ((), ())), preferred_element_type=jnp.float32
     )
-    student_grad = sum_by_parts(partial_grad.astype(jnp.bfloat16), (("dp_0", "dp_1"), "dp_2"))
+    student_grad = sum_by_parts(partial_grad.astype(jnp.bfloat16), (("dp_x", "dp_z"), "dp_c"))
     return (teacher, student_grad, token_distance)
 
 
 def solution(mesh):
     torus = Mesh(
-        mesh.devices.reshape(2, 8, 2, mesh.shape["section"]), ("dp_0", "dp_1", "dp_2", "section")
+        mesh.devices.reshape(2, 8, 2, mesh.shape["section"]), ("dp_x", "dp_z", "dp_c", "section")
     )
     in_specs = (
         P(DP, None, None),

time: 553 us -> 332 us (0.60)
  waiting for transfers between devices: 296 us -> 54.8 us
  Pallas kernels: 0 us -> 128 us
  other arithmetic: 50.8 us -> 15.9 us
  starting transfers between devices: 59.4 us -> 24.7 us
  matrix products: 32.4 us -> 8.27 us
  local copies, waits for them, and re-layouts: 36.1 us -> 17.2 us
  blocking collectives: 58.4 us -> 67.6 us
    ppermute x19 -> x1, waiting for transfers between devices: 152 us -> 0.6 us  [local(): other = lax.ppermute(packed, 'dp_x', [(0, 1), (1, 0)])]
    pallas_call x0 -> x1, Pallas kernels: none -> 128 us  [run_teacher(): pl.pallas_call(teacher_kernel, out_shape=jax.ShapeDtypeStruct((mbs, rows,...]
    all_gather x1 -> x0, waiting for transfers between devices: 66.6 us -> none  [picked(): lax.all_gather(x, axis)]
    dot_general x9 -> x2, matrix products: 27.5 us -> 0.43 us  [conditions_of(): jnp.dot(embedding.astype(jnp.bfloat16).reshape(-1, 2 * half_freq), time_w...]
    all_gather x1, waiting for transfers between devices: 24.6 us -> 0.02 us  [local(): weights = lax.all_gather(block_weight, DP, axis=1, tiled=True)[0]]
    dynamic_slice x47 -> x1, local copies, waits for them, and re-layouts: 20 us -> 0.11 us  [local(): lax.dynamic_slice_in_dim(teacher, first_col, col_count, 2)]
    ppermute x19 -> x1, starting transfers between devices: 20.4 us -> 1.48 us  [local(): other = lax.ppermute(packed, 'dp_x', [(0, 1), (1, 0)])]
    all_to_all x1, starting transfers between devices: 24.4 us -> 6.66 us  [from_everyone(): return lax.all_to_all(copies, axis, split_axis=0, concat_axis=0, tiled=True)]
  transfers between devices with their start and end apart: 24 -> 5, of which waited for: 24 -> 4; matrix products, arithmetic and copies ran while one was open for 5% -> 8% of each run, Pallas kernels for 0% -> 0%
where the time goes in v1:
time: 332 us; the launch traced here: 331 us
  Pallas kernels  128 us (39%)
  blocking collectives  67.6 us (20%)
  waiting for transfers between devices  54.8 us (17%)
  starting transfers between devices  24.7 us (7%)
  local copies, waits for them, and re-layouts  17.2 us (5%)
  other arithmetic  15.9 us (5%)
  between operations  14.4 us (4%)
  matrix products  8.27 us (2%)
    pallas_call x1, Pallas kernels, run_teacher(): pl.pallas_call(teacher_kernel, out_shape=jax.ShapeDtypeStruct((mbs, rows,...  128 us
    all_to_all x3, blocking collectives, from_everyone(): return lax.all_to_all(copies, axis, split_axis=0, concat_axis=0, tiled=True)  35 us
    all_to_all x1, waiting for transfers between devices, summed_on_arrival(): lax.all_to_all(blocks, axis, split_axis=0, concat_axis=0, tiled=True)  25.3 us
    all_to_all x1, waiting for transfers between devices, from_everyone(): return lax.all_to_all(copies, axis, split_axis=0, concat_axis=0, tiled=True)  19.2 us
    all_to_all x1, blocking collectives, sum_at_owner(): lax.all_to_all(blocks, axis, split_axis=0, concat_axis=0, tiled=True)  18.7 us
    all_to_all x1, blocking collectives, summed_rows(): lax.all_to_all(own.astype(jnp.bfloat16), far, 0, 0, tiled=True)  13.9 us
    all_to_all x1, starting transfers between devices, summed_on_arrival(): lax.all_to_all(blocks, axis, split_axis=0, concat_axis=0, tiled=True)  11.1 us
    all_to_all x1, waiting for transfers between devices, sum_at_owner(): lax.all_to_all(blocks, axis, split_axis=0, concat_axis=0, tiled=True)  8.96 us
  transfers between devices with their start and end apart: 5, of which 4 were waited for; matrix products, arithmetic and copies ran while one was open for 8% of the time, Pallas kernels for 0%

profile of v1, /device:TPU:1, one launch (start us, length us, event | category | flops | bytes accessed | tf_op | source)
XLA Modules:
  0.0 331.3 jit_solution(6538419886704961337)
XLA Ops:
  8.7 10.4 %while.14 = (s32[]{:T(128)}, f32[128,1544]{0,1:T(8,128)S(1)}, s32[128,77]{0,1:T(8,128)S(1)}, s32[]{:T(128)}, s32[]{:T(128)}, /*index=5*/s32[]{:T(128)}, s32[]{:T(128)}) while((s32[]{:T(128)}, f32[128,1544]{0,1:T(8,128)S(1)}, s32[128,77]{0,1:T(8,128)S(1)}, s32[]{:T(128)}, s32[]{:T(128)}, /*index=5*/s32[]{:T(128)}, s32[]{:T(128)}) %tuple.51), condition=%wide.region_2.0_spmd.clone, body=%wide.region_0.0_spmd.clone.sunk | while | flops 4347911 | bytes 3173001 | solution.py:318
  19.1 3.2 convolution_multiply_fusion
  22.4 1.1 reshape.145
  23.5 11.1 %all-to-all-start = ((f32[32,4,1536]{2,1,0:T(4,128)}), f32[32,4,1536]{2,1,0:T(4,128)S(1)}, u32[]{:S(2)}, u32[]{:S(2)}) async-start(f32[32,4,1536]{2,1,0:T(4,128)} %reshape.145), calls=%async_computation | async-start | bytes 1572864 | tf_op jit(solution)/shard_map/all_to_all | solution.py:25
  34.7 1.4 convert_element_type.63
  36.2 1.1 constant_dynamic-slice_fusion.2
  37.7 25.3 %all-to-all-done = f32[32,4,1536]{2,1,0:T(4,128)S(1)} async-done(((f32[32,4,1536]{2,1,0:T(4,128)}), f32[32,4,1536]{2,1,0:T(4,128)S(1)}, u32[]{:S(2)}, u32[]{:S(2)}) %all-to-all-start) | async-done | bytes 786464 | tf_op jit(solution)/shard_map/all_to_all | solution.py:25
  63.9 6.7 %all-to-all-start.1 = ((bf16[32,48,192]{2,1,0:T(8,128)(2,1)}), bf16[32,48,192]{2,1,0:T(8,128)(2,1)S(1)}, u32[]{:S(2)}, u32[]{:S(2)}) async-start(bf16[32,48,192]{2,1,0:T(8,128)(2,1)} %broadcast_in_dim.67), calls=%async_computation.1 | async-start | bytes 1572864 | tf_op jit(solution)/shard_map/all_to_all | solution.py:37
  70.7 1.5 collective-permute-start
  78.0 19.2 %all-to-all-done.1 = bf16[32,48,192]{2,1,0:T(8,128)(2,1)S(1)} async-done(((bf16[32,48,192]{2,1,0:T(8,128)(2,1)}), bf16[32,48,192]{2,1,0:T(8,128)(2,1)S(1)}, u32[]{:S(2)}, u32[]{:S(2)}) %all-to-all-start.1) | async-done | bytes 589856 | tf_op jit(solution)/shard_map/all_to_all | solution.py:37
  97.7 1.5 convolution_convert_fusion.2
  100.2 2.3 copy-done.2
  102.5 128.0 %shard_map.148 = bf16[8,32,1536]{2,1,0:T(8,128)(2,1)S(1)} custom-call(bf16[8,32,1536]{2,1,0:T(8,128)(2,1)S(1)} %bitcast.43, bf16[1536,1536]{1,0:T(8,128)(2,1)S(1)} %bitcast.44, f32[3,8,1,1536]{3,2,1,0:T(1,128)S(1)} %multiply_add_fusion.gains_ref, f32[8,1,128]{2,1,0:T(1,128)S(1)} %broadcast_in_dim.62.delta_ref), custom_call_target="tpu_custom_call" | custom-call | tf_op jit(solution)/shard_map/pallas_call | solution.py:266
  231.7 5.5 %all-to-all-start.2 = ((bf16[8,32,1024]{2,1,0:T(8,128)(2,1)}), bf16[8,32,1024]{2,1,0:T(8,128)(2,1)S(1)}, u32[]{:S(2)}, u32[]{:S(2)}) async-start(bf16[8,32,1024]{2,1,0:T(8,128)(2,1)} %bitcast.52), calls=%async_computation.2 | async-start | bytes 1048576 | tf_op jit(solution)/shard_map/all_to_all | solution.py:46
  237.3 9.0 %all-to-all-done.2 = bf16[8,32,1024]{2,1,0:T(8,128)(2,1)S(1)} async-done(((bf16[8,32,1024]{2,1,0:T(8,128)(2,1)}), bf16[8,32,1024]{2,1,0:T(8,128)(2,1)S(1)}, u32[]{:S(2)}, u32[]{:S(2)}) %all-to-all-start.2) | async-done | bytes 524320 | tf_op jit(solution)/shard_map/all_to_all | solution.py:46
  247.3 11.4 %all_to_all.40 = bf16[8,32,512]{2,1,0:T(8,128)(2,1)S(1)} all-to-all(bf16[8,32,512]{2,1,0:T(8,128)(2,1)S(1)} %broadcast_in_dim.70), channel_id=1, replica_groups=mesh['dp_x'=2,'dp_z'=8,'dp_c'=2,'section'=8] {'section'}, dimensions={0} | all-to-all | bytes 524288 | tf_op jit(solution)/shard_map/all_to_all | solution.py:37
  258.8 2.4 convolution_convert_fusion
  261.2 1.3 copy.66
  262.6 18.7 %all_to_all.41 = bf16[2,16,48,192]{3,2,1,0:T(8,128)(2,1)S(1)} all-to-all(bf16[2,16,48,192]{3,2,1,0:T(8,128)(2,1)S(1)} %copy.67), channel_id=1, replica_groups=mesh['dp_x'=2,'dp_z'=8,'dp_c'=2,'section'=8] {'dp_c'}, dimensions={0} | all-to-all | bytes 1179648 | tf_op jit(solution)/shard_map/all_to_all | solution.py:46
  281.6 13.9 %all_to_all.42 = bf16[16,48,192]{2,1,0:T(8,128)(2,1)S(1)} all-to-all(bf16[16,48,192]{2,1,0:T(8,128)(2,1)S(1)} %reduce_sum.110), channel_id=1, replica_groups=mesh['dp_x'=2,'dp_z'=8,'dp_c'=2,'section'=8] {'dp_x','dp_z'}, dimensions={0} | all-to-all | bytes 589824 | tf_op jit(solution)/shard_map/all_to_all | solution.py:73
  295.6 17.1 %all_to_all.44 = bf16[16,48,192]{2,1,0:T(8,128)(2,1)S(1)} all-to-all(bf16[16,48,192]{2,1,0:T(8,128)(2,1)S(1)} %broadcast_in_dim.71), channel_id=1, replica_groups=mesh['dp_x'=2,'dp_z'=8,'dp_c'=2,'section'=8] {'dp_x','dp_z'}, dimensions={0} | all-to-all | bytes 589824 | tf_op jit(solution)/shard_map/all_to_all | solution.py:37
  312.8 6.4 %all_to_all.43 = bf16[2,16,48,192]{3,2,1,0:T(8,128)(2,1)S(1)} all-to-all(bf16[2,16,48,192]{3,2,1,0:T(8,128)(2,1)S(1)} %broadcast_in_dim.72), channel_id=1, replica_groups=mesh['dp_x'=2,'dp_z'=8,'dp_c'=2,'section'=8] {'dp_c'}, dimensions={0} | all-to-all | bytes 1179648 | tf_op jit(solution)/shard_map/all_to_all | solution.py:37
  319.4 1.3 copy.68
  320.7 2.9 copy.69
  (128 shorter events, 24.1 us)
Async XLA Ops:
  7.2 68.4 %copy-start = (bf16[256,1536]{1,0:T(8,128)(2,1)S(1)}, bf16[256,1536]{1,0:T(8,128)(2,1)}, u32[]{:S(2)}) copy-start(bf16[256,1536]{1,0:T(8,128)(2,1)} %param.19) | copy-start | bytes 2359300
  7.2 92.2 %all-gather.2.cloned.1.call-start = ((), (), s32[]{:S(2)}) async-start(), calls=%async_computation.8 | async-start | bytes 4866048 | tf_op jit(solution)/shard_map/all_gather | solution.py:330
  22.4 12.2 %copy-start.15 = (s32[4,3]{1,0:T(4,128)S(1)}, s32[4,3]{1,0:T(4,128)}, u32[]{:S(2)}) copy-start(s32[4,3]{1,0:T(4,128)} %param.16) | copy-start | bytes 148
  22.4 12.2 %copy-start.1 = (bf16[4,64,1536]{2,1,0:T(8,128)(2,1)S(1)}, bf16[4,64,1536]{2,1,0:T(8,128)(2,1)}, u32[]{:S(2)}) copy-start(bf16[4,64,1536]{2,1,0:T(8,128)(2,1)} %param.15) | copy-start | bytes 2359300
  23.5 39.5 %all-to-all-start = ((f32[32,4,1536]{2,1,0:T(4,128)}), f32[32,4,1536]{2,1,0:T(4,128)S(1)}, u32[]{:S(2)}, u32[]{:S(2)}) async-start(f32[32,4,1536]{2,1,0:T(4,128)} %reshape.145), calls=%async_computation | async-start | bytes 1572864 | tf_op jit(solution)/shard_map/all_to_all | solution.py:25
  34.6 1.5 copy-start.11
  34.6 28.4 %copy-start.9 = (bf16[48,192]{1,0:T(8,128)(2,1)S(1)}, bf16[48,192]{1,0:T(8,128)(2,1)}, u32[]{:S(2)}) copy-start(bf16[48,192]{1,0:T(8,128)(2,1)} %param.22) | copy-start | bytes 55300
  63.9 9.4 %copy-start.10 = (f32[1,3,1536]{2,0,1:T(1,128)S(1)}, f32[1,3,1536]{2,0,1:T(1,128)}, u32[]{:S(2)}) copy-start(f32[1,3,1536]{2,0,1:T(1,128)} %param.21) | copy-start | bytes 55300
  63.9 33.2 %all-to-all-start.1 = ((bf16[32,48,192]{2,1,0:T(8,128)(2,1)}), bf16[32,48,192]{2,1,0:T(8,128)(2,1)S(1)}, u32[]{:S(2)}, u32[]{:S(2)}) async-start(bf16[32,48,192]{2,1,0:T(8,128)(2,1)} %broadcast_in_dim.67), calls=%async_computation.1 | async-start | bytes 1572864 | tf_op jit(solution)/shard_map/all_to_all | solution.py:37
  70.7 4.5 %collective-permute-start = (f32[4,1664]{1,0:T(4,128)S(1)}, f32[4,1664]{1,0:T(4,128)S(1)}, u32[]{:S(2)}, u32[]{:S(2)}) collective-permute-start(f32[4,1664]{1,0:T(4,128)S(1)} %select_maximum_fusion), channel_id=1, source_target_pairs={{0,128},{128,0},{1,129},{129,1},{2,130},{130,2},{3,131},{131,3},{4... | collective-permute-start | bytes 79880 | tf_op jit(solution)/shard_map/ppermute | solution.py:353
  73.4 24.3 %copy-start.13 = (f32[256]{0:T(256)}, f32[256]{0:T(256)S(1)}, u32[]{:S(2)}) copy-start(f32[256]{0:T(256)S(1)} %broadcast_in_dim.66) | copy-start | bytes 3076
  97.2 2.0 copy-start.7
  97.2 2.0 copy-start.8
  97.2 2.0 copy-start.16
  97.7 1.5 copy-start.4
  100.2 2.3 copy-start.2
  102.5 128.1 %copy-start.6 = (bf16[192,512]{1,0:T(8,128)(2,1)S(1)}, bf16[192,512]{1,0:T(8,128)(2,1)}, u32[]{:S(2)}) copy-start(bf16[192,512]{1,0:T(8,128)(2,1)} %param.24) | copy-start | bytes 589828
  230.5 6.7 %copy-start.17 = (f32[256]{0:T(256)S(1)}, f32[256]{0:T(256)}, u32[]{:S(2)}) copy-start(f32[256]{0:T(256)} %param.26) | copy-start | bytes 3076
  230.8 15.6 %copy-start.12 = (f32[512]{0:T(512)S(1)}, f32[512]{0:T(512)}, u32[]{:S(2)}) copy-start(f32[512]{0:T(512)} %param.25) | copy-start | bytes 6148
  231.7 27.0 %copy-start.3 = (f32[256,192]{0,1:T(8,128)S(1)}, f32[256,192]{0,1:T(8,128)}, u32[]{:S(2)}) copy-start(f32[256,192]{0,1:T(8,128)} %copy.65) | copy-start | bytes 589828
  231.7 27.0 %copy-start.5 = (f32[256,192]{0,1:T(8,128)S(1)}, f32[256,192]{0,1:T(8,128)}, u32[]{:S(2)}) copy-start(f32[256,192]{0,1:T(8,128)} %copy-done.4) | copy-start | bytes 589828
  231.7 27.0 %copy-start.14 = (f32[256]{0:T(256)S(1)}, f32[256]{0:T(256)}, u32[]{:S(2)}) copy-start(f32[256]{0:T(256)} %copy-done.13) | copy-start | bytes 3076
  231.7 14.5 %all-to-all-start.2 = ((bf16[8,32,1024]{2,1,0:T(8,128)(2,1)}), bf16[8,32,1024]{2,1,0:T(8,128)(2,1)S(1)}, u32[]{:S(2)}, u32[]{:S(2)}) async-start(bf16[8,32,1024]{2,1,0:T(8,128)(2,1)} %bitcast.52), calls=%async_computation.2 | async-start | bytes 1048576 | tf_op jit(solution)/shard_map/all_to_all | solution.py:46
Sparse Core Ops, SparseCore 0:
  9.9 87.9 all-gather.1

commit v2 on v1

--- a/solution.py
+++ b/solution.py
@@ -41,46 +41,6 @@
     return in_order(from_everyone(x, axis), dim)
 
 
-def sum_at_owner(x, axis, dim):
-    blocks = in_blocks(x, dim, lax.axis_size(axis))
-    arrived = lax.all_to_all(blocks, axis, split_axis=0, concat_axis=0, tiled=True)
-    return arrived.astype(jnp.float32).sum(axis=0)
-
-
-def side_by_side(arrays, axis, dim, along):
-    widths = [a.shape[along] for a in arrays]
-    both = jnp.concatenate(arrays, axis=along)
-    result = sum_at_owner(both, axis, dim)
-    return tuple(jnp.split(result, [sum(widths[:k]) for k in range(1, len(widths))], axis=along))
-
-
-def filled_up(lines, count):
-    spare = -len(lines) % count
-    return jnp.pad(lines, [(0, spare)] + [(0, 0)] * (lines.ndim - 1))
-
-
-def gather_axes(x, axes, dim):
-    far, near = axes
-    initial = from_everyone(x, far)
-    blocks = jnp.swapaxes(from_everyone(initial, near), 0, 1)
-    return in_order(blocks.reshape(-1, *x.shape), dim)
-
-
-def summed_rows(x, axes, dim):
-    far, near = axes
-    own = sum_at_owner(in_blocks(x, dim, lax.axis_size(far)), near, dim + 1)
-    return jnp.sum(
-        lax.all_to_all(own.astype(jnp.bfloat16), far, 0, 0, tiled=True).astype(jnp.float32), axis=0
-    )
-
-
-def sum_by_parts(x, axes):
-    lines = x.reshape(-1, x.shape[-1])
-    padded = filled_up(lines, lax.axis_size(axes[0]) * lax.axis_size(axes[1]))
-    whole = gather_axes(summed_rows(padded, axes, 0).astype(jnp.bfloat16), axes, 0)
-    return lax.slice_in_dim(whole, 0, len(lines)).reshape(x.shape).astype(jnp.float32)
-
-
 def modulated(hidden_f, cond_vec, gains):
     mean_sq = jnp.mean(hidden_f * hidden_f, axis=-1, keepdims=True)
     normed = hidden_f * lax.rsqrt(mean_sq + 1e-06)
@@ -92,15 +52,6 @@
     inputs = modulated(hidden_f, cond_vec, gains).astype(jnp.bfloat16)
     mixed = jnp.dot(inputs, weight, preferred_element_type=jnp.float32)
     return (hidden_f + (1.0 + cond_vec * gains[2]) * jax.nn.gelu(mixed)).astype(jnp.bfloat16)
-
-
-def distance(feat_student, feat_teacher, lin_weight):
-    relu_s = jax.nn.relu(feat_student)
-    relu_t = jax.nn.relu(feat_teacher)
-    unit_s = relu_s * lax.rsqrt(jnp.mean(relu_s * relu_s, axis=-1, keepdims=True) + 1e-06)
-    unit_t = relu_t * lax.rsqrt(jnp.mean(relu_t * relu_t, axis=-1, keepdims=True) + 1e-06)
-    gap = unit_s - unit_t
-    return jnp.sum(lin_weight * gap * gap, axis=-1)
 
 
 def teacher_kernel(
@@ -287,6 +238,230 @@
     )(noise, weights, gains, delta)
 
 
+def loss_kernel(
+    teacher_ref,
+    feature_ref,
+    own_feature_ref,
+    student_part_ref,
+    lin_ref,
+    token_ref,
+    inputs_ref,
+    slope_ref,
+    dist_ref,
+    grad_ref,
+    feats,
+    grads,
+    partial,
+    half_out,
+    half_in,
+    summed,
+    pieces,
+    final,
+    feat_send,
+    feat_recv,
+    grad_send,
+    grad_recv,
+    half_send,
+    half_recv,
+    piece_send,
+    piece_recv,
+    final_send,
+    final_recv,
+    twin_send,
+    twin_recv,
+):
+    sections, rows, feat = student_part_ref.shape
+    chips = summed.shape[0]
+    piece = summed.shape[1]
+    width = inputs_ref.shape[1]
+    xl = lax.axis_index("dp_x")
+    zz = lax.axis_index("dp_z")
+    core = lax.axis_index("dp_c")
+    sec = lax.axis_index("section")
+    chip = xl * 8 + zz
+
+    def at_section(k):
+        return {"section": k}
+
+    def at_chip(q):
+        return {"dp_x": q // 8, "dp_z": q % 8}
+
+    def at_twin():
+        return {"dp_c": 1 - core}
+
+    barrier = pltpu.get_barrier_semaphore()
+
+    def greet(where):
+        pl.semaphore_signal(barrier, inc=1, device_id=where, device_id_type=MESH)
+
+    for k in range(1, sections):
+        greet(at_section((sec + k) % sections))
+    for k in range(1, chips):
+        greet(at_chip((chip + k) % chips))
+    greet(at_twin())
+    pl.semaphore_wait(barrier, sections + chips - 1)
+
+    def copy(src, dst, send, recv, where):
+        return pltpu.make_async_remote_copy(
+            src_ref=src,
+            dst_ref=dst,
+            send_sem=send,
+            recv_sem=recv,
+            device_id=where,
+            device_id_type=MESH,
+        )
+
+    def send_feat(k, slot):
+        return copy(
+            student_part_ref.at[k], feats.at[slot], feat_send.at[k], feat_recv.at[slot], at_section(k)
+        )
+
+    def send_grad(k, slot):
+        return copy(grads.at[slot], grads.at[slot], grad_send.at[k], grad_recv.at[slot], at_section(k))
+
+    def send_piece(q, slot):
+        return copy(summed.at[q], pieces.at[slot], piece_send.at[q], piece_recv.at[slot], at_chip(q))
+
+    def send_final(q, slot):
+        block = final.at[core, slot]
+        return copy(block, block, final_send.at[q], final_recv.at[slot], at_chip(q))
+
+    def send_twin(half, slot):
+        block = final.at[half, slot]
+        return copy(block, block, twin_send.at[slot], twin_recv.at[slot], at_twin())
+
+    send_half = copy(half_out, half_in, half_send, half_recv, at_twin())
+
+    for k in range(1, sections):
+        send_feat((sec + k) % sections, sec).start()
+
+    feat_teacher = jnp.dot(
+        teacher_ref[sec], feature_ref[...], preferred_element_type=jnp.float32
+    )
+    feat_student = student_part_ref[sec].astype(jnp.float32)
+    for k in range(1, sections):
+        other = (sec + k) % sections
+        send_feat(other, other).wait_recv()
+        feat_student = feat_student + feats[other].astype(jnp.float32)
+
+    def unit(f):
+        positive = jnp.maximum(f, 0.0)
+        scale = lax.rsqrt(jnp.mean(positive * positive, axis=-1, keepdims=True) + 1e-06)
+        return positive * scale, scale
+
+    unit_s, scale_s = unit(feat_student)
+    unit_t, _ = unit(feat_teacher)
+    gap = unit_s - unit_t
+    lin = lin_ref[...]
+    dist_ref[...] = jnp.sum(lin * gap * gap, axis=-1, keepdims=True)
+    unit_grad = 2.0 * token_ref[...] * lin * gap
+    mean_dot = jnp.mean(unit_grad * unit_s, axis=-1, keepdims=True)
+    feat_grad = scale_s * (unit_grad - unit_s * mean_dot)
+    grads[sec] = jnp.where(feat_student > 0.0, feat_grad, 0.0).astype(jnp.bfloat16)
+    for k in range(1, sections):
+        send_grad((sec + k) % sections, sec).start()
+    for k in range(1, sections):
+        other = (sec + k) % sections
+        send_grad(other, other).wait_recv()
+
+    out_grad = lax.dot_general(
+        grads[...].reshape(sections * rows, feat),
+        own_feature_ref[...],
+        (((1,), (1,)), ((), ())),
+        preferred_element_type=jnp.float32,
+    )
+    mixed_grad = (out_grad * slope_ref[...]).astype(jnp.bfloat16)
+    half_rows = width // 2
+    for half in range(2):
+        partial[half] = lax.dot_general(
+            inputs_ref[:, half * half_rows : (half + 1) * half_rows],
+            mixed_grad,
+            (((0,), (0,)), ((), ())),
+            preferred_element_type=jnp.float32,
+        ).reshape(chips, piece, -1)
+    half_out[...] = partial[1 - core].astype(jnp.bfloat16)
+    send_half.start()
+    send_half.wait_recv()
+    summed[...] = (partial[core] + half_in[...].astype(jnp.float32)).astype(jnp.bfloat16)
+    for k in range(1, chips):
+        send_piece((chip + k) % chips, chip).start()
+    total = summed[chip].astype(jnp.float32)
+    for k in range(1, chips):
+        other = (chip + chips - k) % chips
+        send_piece(other, other).wait_recv()
+        total = total + pieces[other].astype(jnp.float32)
+    final[core, chip] = total.astype(jnp.bfloat16)
+    for k in range(1, chips):
+        send_final((chip + k) % chips, chip).start()
+    send_twin(core, chip).start()
+    grad_ref[core, chip] = final[core, chip].astype(jnp.float32)
+    for k in range(1, chips):
+        other = (chip + chips - k) % chips
+        send_final(other, other).wait_recv()
+        send_twin(core, other).start()
+        grad_ref[core, other] = final[core, other].astype(jnp.float32)
+    for k in range(chips):
+        other = (chip + chips - k) % chips
+        send_twin(1 - core, other).wait_recv()
+        grad_ref[1 - core, other] = final[1 - core, other].astype(jnp.float32)
+
+    send_half.wait_send()
+    for k in range(1, sections):
+        send_feat((sec + k) % sections, sec).wait_send()
+        send_grad((sec + k) % sections, sec).wait_send()
+    for k in range(1, chips):
+        send_piece((chip + k) % chips, chip).wait_send()
+        send_final((chip + k) % chips, chip).wait_send()
+    for k in range(chips):
+        send_twin(core, k).wait_send()
+
+
+def run_loss(teacher, feature, own_feature, student_part, lin, token, inputs, slope):
+    sections, rows, feat = student_part.shape
+    width = inputs.shape[1]
+    cols = slope.shape[1]
+    chips = 16
+    piece = width // (2 * chips)
+    vmem = pl.BlockSpec(memory_space=pltpu.VMEM)
+    dma = pltpu.SemaphoreType.DMA
+    bf16 = jnp.bfloat16
+    dist, grad = pl.pallas_call(
+        loss_kernel,
+        out_shape=(
+            jax.ShapeDtypeStruct((rows, 1), jnp.float32),
+            jax.ShapeDtypeStruct((2, chips, piece, cols), jnp.float32),
+        ),
+        in_specs=[vmem] * 8,
+        out_specs=(vmem, vmem),
+        scratch_shapes=[
+            pltpu.VMEM((sections, rows, feat), bf16),
+            pltpu.VMEM((sections, rows, feat), bf16),
+            pltpu.VMEM((2, chips, piece, cols), jnp.float32),
+            pltpu.VMEM((chips, piece, cols), bf16),
+            pltpu.VMEM((chips, piece, cols), bf16),
+            pltpu.VMEM((chips, piece, cols), bf16),
+            pltpu.VMEM((chips, piece, cols), bf16),
+            pltpu.VMEM((2, chips, piece, cols), bf16),
+            dma((sections,)),
+            dma((sections,)),
+            dma((sections,)),
+            dma((sections,)),
+            dma,
+            dma,
+            dma((chips,)),
+            dma((chips,)),
+            dma((chips,)),
+            dma((chips,)),
+            dma((chips,)),
+            dma((chips,)),
+        ],
+        compiler_params=pltpu.CompilerParams(
+            collective_id=1, has_side_effects=True, vmem_limit_bytes=40 * 1024 * 1024
+        ),
+    )(teacher, feature, own_feature, student_part, lin, token, inputs, slope)
+    return dist.reshape(rows), grad.reshape(width, cols)
+
+
 def local(
     noise,
     sched_index,
@@ -362,12 +537,13 @@
     delta_lanes = jnp.broadcast_to(
         jnp.moveaxis(deltas, 1, 0).reshape(steps * batches, 1, 1), (steps * batches, 1, 128)
     )
-    teacher = run_teacher(
+    teacher_parts = run_teacher(
         noise.reshape(sections, batches * tokens // sections, model_width),
         weights,
         gains,
         delta_lanes,
-    ).reshape(noise.shape)
+    )
+    teacher = teacher_parts.reshape(noise.shape)
     col_count = student_weight.shape[1]
     first_col = own_section * col_count
     row_count = batches * tokens
@@ -393,34 +569,23 @@
         return z_cols - t_rows * (z_cols + gate_rows * jax.nn.gelu(mixed_in))
 
     moved, pull_back = jax.vjp(advance, mixed)
+    slope = pull_back(jnp.ones_like(moved))[0]
     feat_student = jnp.dot(
         moved.astype(jnp.bfloat16), feature_weight, preferred_element_type=jnp.float32
     )
-    target_cols = lax.dynamic_slice_in_dim(teacher, first_col, col_count, 2).reshape(
-        row_count, col_count
-    )
-    feat_teacher = jnp.dot(target_cols, feature_weight, preferred_element_type=jnp.float32)
     share_rows = row_count // sections
-    part_student, part_teacher = side_by_side(
-        (feat_student.astype(jnp.bfloat16), feat_teacher.astype(jnp.bfloat16)), "section", 0, 1
-    )
     weight_share = lax.dynamic_slice_in_dim(token_weight, own_section * share_rows, share_rows, 0)
-
-    def objective(feat_in):
-        token_dist = distance(feat_in, part_teacher, lin_weight)
-        return (jnp.sum(weight_share * token_dist), token_dist)
-
-    total, pull_feat, token_distance = jax.vjp(objective, part_student, has_aux=True)
-    grad_share = pull_feat(jnp.ones_like(total))[0].astype(jnp.bfloat16)
-    grad_feat = collect(grad_share, "section", 0)
-    out_grad = lax.dot_general(
-        grad_feat, feature_weight, (((1,), (1,)), ((), ())), preferred_element_type=jnp.float32
-    )
-    mixed_grad = pull_back(out_grad)[0].astype(jnp.bfloat16)
-    partial_grad = lax.dot_general(
-        inputs, mixed_grad, (((0,), (0,)), ((), ())), preferred_element_type=jnp.float32
-    )
-    student_grad = sum_by_parts(partial_grad.astype(jnp.bfloat16), (("dp_x", "dp_z"), "dp_c"))
+    feature_full = lax.all_gather(feature_weight, "section", axis=0, tiled=True)
+    token_distance, student_grad = run_loss(
+        teacher_parts,
+        feature_full,
+        feature_weight,
+        feat_student.astype(jnp.bfloat16).reshape(sections, share_rows, -1),
+        lin_weight[None, :],
+        weight_share[:, None],
+        inputs,
+        slope,
+    )
     return (teacher, student_grad, token_distance)
 
 

time: 332 us -> 310 us (0.934)
  blocking collectives: 67.6 us -> 0 us
  Pallas kernels: 128 us -> 190 us
  waiting for transfers between devices: 54.8 us -> 47.4 us
  starting transfers between devices: 24.7 us -> 19.2 us
    all_to_all x5 -> x0, blocking collectives: 67.6 us -> none  [the longest x3 35 us: from_everyone(): return lax.all_to_all(copies, axis, split_axis=0, concat_axis=0, tiled=True)]
    pallas_call x0 -> x1, Pallas kernels: none -> 57.5 us  [run_loss(): pl.pallas_call(loss_kernel, out_shape=(jax.ShapeDtypeStruct((rows, 1), jn...]
    all_to_all x1 -> x0, waiting for transfers between devices: 8.96 us -> none  [sum_at_owner(): lax.all_to_all(blocks, axis, split_axis=0, concat_axis=0, tiled=True)]
    all_to_all x1 -> x0, starting transfers between devices: 5.46 us -> none  [sum_at_owner(): lax.all_to_all(blocks, axis, split_axis=0, concat_axis=0, tiled=True)]
    pallas_call x1, Pallas kernels: 128 us -> 132 us  [run_teacher(): pl.pallas_call(teacher_kernel, out_shape=jax.ShapeDtypeStruct((mbs, rows,...]
    unnamed x39 -> x35, local copies, waits for them, and re-layouts: 6.8 us -> 11.2 us
  transfers between devices with their start and end apart: 5 -> 5, of which waited for: 4 -> 3; matrix products, arithmetic and copies ran while one was open for 8% -> 9% of each run, Pallas kernels for 0% -> 43%
where the time goes in v2:
time: 310 us; the launch traced here: 309 us
  Pallas kernels  190 us (61%)
  waiting for transfers between devices  47.4 us (15%)
  starting transfers between devices  19.2 us (6%)
  local copies, waits for them, and re-layouts  17.3 us (6%)
  between operations  14.3 us (5%)
  other arithmetic  14 us (5%)
  matrix products  6.79 us (2%)
    pallas_call x1, Pallas kernels, run_teacher(): pl.pallas_call(teacher_kernel, out_shape=jax.ShapeDtypeStruct((mbs, rows,...  132 us
    pallas_call x1, Pallas kernels, run_loss(): pl.pallas_call(loss_kernel, out_shape=(jax.ShapeDtypeStruct((rows, 1), jn...  57.5 us
    all_to_all x1, waiting for transfers between devices, summed_on_arrival(): lax.all_to_all(blocks, axis, split_axis=0, concat_axis=0, tiled=True)  23.7 us
    all_to_all x1, waiting for transfers between devices, from_everyone(): return lax.all_to_all(copies, axis, split_axis=0, concat_axis=0, tiled=True)  20.5 us
    unnamed x35, local copies, waits for them, and re-layouts  11.2 us
    all_to_all x1, starting transfers between devices, summed_on_arrival(): lax.all_to_all(blocks, axis, split_axis=0, concat_axis=0, tiled=True)  11.1 us
    reduce_sum x11, other arithmetic, add_group(): jnp.sum((id_block[:, :, None] == vocab_ids).astype(jnp.float32), axis=1)  7.58 us
    all_to_all x1, starting transfers between devices, from_everyone(): return lax.all_to_all(copies, axis, split_axis=0, concat_axis=0, tiled=True)  6.55 us
  transfers between devices with their start and end apart: 5, of which 3 were waited for; matrix products, arithmetic and copies ran while one was open for 9% of the time, Pallas kernels for 43%

profile of v2, /device:TPU:1, one launch (start us, length us, event | category | flops | bytes accessed | tf_op | source)
XLA Modules:
  0.0 309.4 jit_solution(7258073583211004576)
XLA Ops:
  7.9 0.8 broadcast_subtract_fusion
  8.7 10.4 %while.14 = (s32[]{:T(128)}, f32[128,1544]{0,1:T(8,128)S(1)}, s32[128,77]{0,1:T(8,128)S(1)}, s32[]{:T(128)}, s32[]{:T(128)}, /*index=5*/s32[]{:T(128)}, s32[]{:T(128)}) while((s32[]{:T(128)}, f32[128,1544]{0,1:T(8,128)S(1)}, s32[128,77]{0,1:T(8,128)S(1)}, s32[]{:T(128)}, s32[]{:T(128)}, /*index=5*/s32[]{:T(128)}, s32[]{:T(128)}) %tuple.50), condition=%wide.region_2.0_spmd.clone, body=%wide.region_0.0_spmd.clone.sunk | while | flops 4347911 | bytes 3173001 | solution.py:493
  19.1 3.2 %convolution_multiply_fusion = f32[128,1536]{1,0:T(8,128)S(1)} fusion(bf16[1544,1536]{1,0:T(8,128)(2,1)} %param.18, f32[128,1544]{0,1:T(8,128)S(1)} %get-tuple-element.84), kind=kOutput, calls=%fused_computation.5 | convolution fusion | flops 607519744 | bytes 6320128 | tf_op jit(solution)/shard_map/dot_general | solution.py:500
  22.4 1.1 reshape.118
  23.5 11.1 %all-to-all-start = ((f32[32,4,1536]{2,1,0:T(4,128)}), f32[32,4,1536]{2,1,0:T(4,128)S(1)}, u32[]{:S(2)}, u32[]{:S(2)}) async-start(f32[32,4,1536]{2,1,0:T(4,128)} %reshape.118), calls=%async_computation | async-start | bytes 1572864 | tf_op jit(solution)/shard_map/all_to_all | solution.py:25
  35.4 1.3 convert_element_type.35
  37.1 1.8 constant_dynamic-slice_fusion.1
  39.3 23.7 %all-to-all-done = f32[32,4,1536]{2,1,0:T(4,128)S(1)} async-done(((f32[32,4,1536]{2,1,0:T(4,128)}), f32[32,4,1536]{2,1,0:T(4,128)S(1)}, u32[]{:S(2)}, u32[]{:S(2)}) %all-to-all-start) | async-done | bytes 786464 | tf_op jit(solution)/shard_map/all_to_all | solution.py:25
  63.0 0.9 broadcast_in_dim.55
  63.9 6.6 %all-to-all-start.1 = ((bf16[32,48,192]{2,1,0:T(8,128)(2,1)}), bf16[32,48,192]{2,1,0:T(8,128)(2,1)S(1)}, u32[]{:S(2)}, u32[]{:S(2)}) async-start(bf16[32,48,192]{2,1,0:T(8,128)(2,1)} %broadcast_in_dim.55), calls=%async_computation.1 | async-start | bytes 1572864 | tf_op jit(solution)/shard_map/all_to_all | solution.py:37
  70.6 1.5 collective-permute-start
  73.7 1.8 collective-permute-done
  76.8 20.5 %all-to-all-done.1 = bf16[32,48,192]{2,1,0:T(8,128)(2,1)S(1)} async-done(((bf16[32,48,192]{2,1,0:T(8,128)(2,1)}), bf16[32,48,192]{2,1,0:T(8,128)(2,1)S(1)}, u32[]{:S(2)}, u32[]{:S(2)}) %all-to-all-start.1) | async-done | bytes 589856 | tf_op jit(solution)/shard_map/all_to_all | solution.py:37
  97.3 2.2 fusion.14
  99.5 0.9 convolution_convert_fusion
  101.4 2.3 copy-done.2
  103.7 132.4 %shard_map.148.teacher_ref = bf16[8,32,1536]{2,1,0:T(8,128)(2,1)S(1)} custom-call(bf16[8,32,1536]{2,1,0:T(8,128)(2,1)S(1)} %bitcast.60, bf16[1536,1536]{1,0:T(8,128)(2,1)S(1)} %bitcast.64, f32[3,8,1,1536]{3,2,1,0:T(1,128)S(1)} %multiply_add_fusion.gains_ref, f32[8,1,128]{2,1,0:T(1,128)S(1)} %broadcast_in_dim.50.delta_ref), custom_call_target="tpu_custom_call" | custom-call | tf_op jit(solution)/shard_map/pallas_call | solution.py:217
  236.2 1.4 copy-done.4
  237.6 0.9 copy-done.6
  238.6 0.9 copy-done.7
  239.5 57.5 %shard_map.149 = (f32[32,1]{1,0:T(8,128)S(1)}, f32[2,16,48,192]{3,2,1,0:T(8,128)S(1)}) custom-call(bf16[8,32,1536]{2,1,0:T(8,128)(2,1)S(1)} %shard_map.148.teacher_ref, bf16[1536,512]{1,0:T(8,128)(2,1)S(1)} %copy-done.4, bf16[192,512]{1,0:T(8,128)(2,1)S(1)} %copy-done.3, bf16[8,32,512]{2,1,0:T(8,128)(2,1)S(1)} %bitcast.66, f32[1,512]{1,0:T(1,128)S(1)} %bitcast.67, ...), custom_call_target="tpu_custom_call" | custom-call | tf_op jit(solution)/shard_map/pallas_call | solution.py:428
  297.0 1.1 copy-done.5
  298.2 2.9 copy.90
  301.7 0.9 copy.103
  (102 shorter events, 16.7 us)
Async XLA Ops:
  7.2 68.6 %copy-start = (bf16[256,1536]{1,0:T(8,128)(2,1)S(1)}, bf16[256,1536]{1,0:T(8,128)(2,1)}, u32[]{:S(2)}) copy-start(bf16[256,1536]{1,0:T(8,128)(2,1)} %param.19) | copy-start | bytes 2359300
  7.2 93.5 %all-gather.3.cloned.1.call-start = ((), (), s32[]{:S(2)}) async-start(), calls=%async_computation.2 | async-start | bytes 4866048 | tf_op jit(solution)/shard_map/all_gather | solution.py:505
  22.4 13.0 %copy-start.13 = (s32[4,3]{1,0:T(4,128)S(1)}, s32[4,3]{1,0:T(4,128)}, u32[]{:S(2)}) copy-start(s32[4,3]{1,0:T(4,128)} %param.16) | copy-start | bytes 148
  22.4 13.0 %copy-start.1 = (bf16[4,64,1536]{2,1,0:T(8,128)(2,1)S(1)}, bf16[4,64,1536]{2,1,0:T(8,128)(2,1)}, u32[]{:S(2)}) copy-start(bf16[4,64,1536]{2,1,0:T(8,128)(2,1)} %param.15) | copy-start | bytes 2359300
  23.5 39.5 %all-to-all-start = ((f32[32,4,1536]{2,1,0:T(4,128)}), f32[32,4,1536]{2,1,0:T(4,128)S(1)}, u32[]{:S(2)}, u32[]{:S(2)}) async-start(f32[32,4,1536]{2,1,0:T(4,128)} %reshape.118), calls=%async_computation | async-start | bytes 1572864 | tf_op jit(solution)/shard_map/all_to_all | solution.py:25
  34.6 2.4 copy-start.12
  34.6 201.6 %all-gather.5.cloned.1.call-start = ((), (), s32[]{:S(2)}) async-start(), calls=%async_computation.3 | async-start | bytes 1769472 | tf_op jit(solution)/shard_map/all_gather | solution.py:578
  35.4 27.6 %copy-start.10 = (bf16[48,192]{1,0:T(8,128)(2,1)S(1)}, bf16[48,192]{1,0:T(8,128)(2,1)}, u32[]{:S(2)}) copy-start(bf16[48,192]{1,0:T(8,128)(2,1)} %param.22) | copy-start | bytes 55300
  39.3 32.8 %copy-start.15 = (f32[256]{0:T(256)S(1)}, f32[256]{0:T(256)}, u32[]{:S(2)}) copy-start(f32[256]{0:T(256)} %param.26) | copy-start | bytes 3076
  39.3 33.1 %copy-start.11 = (f32[1,3,1536]{2,0,1:T(1,128)S(1)}, f32[1,3,1536]{2,0,1:T(1,128)}, u32[]{:S(2)}) copy-start(f32[1,3,1536]{2,0,1:T(1,128)} %param.21) | copy-start | bytes 55300
  63.9 33.4 %all-to-all-start.1 = ((bf16[32,48,192]{2,1,0:T(8,128)(2,1)}), bf16[32,48,192]{2,1,0:T(8,128)(2,1)S(1)}, u32[]{:S(2)}, u32[]{:S(2)}) async-start(bf16[32,48,192]{2,1,0:T(8,128)(2,1)} %broadcast_in_dim.55), calls=%async_computation.1 | async-start | bytes 1572864 | tf_op jit(solution)/shard_map/all_to_all | solution.py:37
  70.6 4.9 %collective-permute-start = (f32[4,1664]{1,0:T(4,128)S(1)}, f32[4,1664]{1,0:T(4,128)S(1)}, u32[]{:S(2)}, u32[]{:S(2)}) collective-permute-start(f32[4,1664]{1,0:T(4,128)S(1)} %select_maximum_fusion), channel_id=1, source_target_pairs={{0,128},{128,0},{1,129},{129,1},{2,130},{130,2},{3,131},{131,3},{4... | collective-permute-start | bytes 79880 | tf_op jit(solution)/shard_map/ppermute | solution.py:528
  76.5 23.0 %copy-start.3 = (bf16[192,512]{1,0:T(8,128)(2,1)S(1)}, bf16[192,512]{1,0:T(8,128)(2,1)}, u32[]{:S(2)}) copy-start(bf16[192,512]{1,0:T(8,128)(2,1)} %own_feature_ref.1) | copy-start | bytes 589828
  97.3 3.1 %copy-start.9 = (f32[1,3,1536]{2,1,0:T(4,128)S(1)}, f32[1,3,1536]{2,1,0:T(4,128)}, u32[]{:S(2)}) copy-start(f32[1,3,1536]{2,1,0:T(4,128)} %copy.95) | copy-start | bytes 55300
  97.3 3.1 %copy-start.14 = (f32[3]{0:T(128)S(1)}, f32[3]{0:T(128)}, u32[]{:S(2)}) copy-start(f32[3]{0:T(128)} %constant.119.clone) | copy-start | bytes 40
  101.4 2.3 copy-start.2
  103.7 132.5 %copy-start.8 = (f32[512]{0:T(512)S(1)}, f32[512]{0:T(512)}, u32[]{:S(2)}) copy-start(f32[512]{0:T(512)} %param.25) | copy-start | bytes 6148
  236.2 1.4 copy-start.4
  237.6 0.9 copy-start.6
  238.6 0.9 copy-start.7
  297.0 1.1 copy-start.5
Sparse Core Ops, SparseCore 0:
  9.9 87.9 all-gather.2
  100.5 82.2 all-gather.4

commit v3 on v2

v3 whole, which is shorter than its diff:
```python
import math

import jax
import jax.numpy as jnp
from jax import lax
from jax.experimental import pallas as pl
from jax.experimental.pallas import tpu as pltpu
from jax.sharding import Mesh
from jax.sharding import PartitionSpec as P

LEVELS = 1000
DP = ("dp_x", "dp_z", "dp_c")
SECTION = ("sec_y", "sec_x")
MESH = pl.DeviceIdType.MESH


def modulated(hidden_f, cond_vec, gains):
    mean_sq = jnp.mean(hidden_f * hidden_f, axis=-1, keepdims=True)
    normed = hidden_f * lax.rsqrt(mean_sq + 1e-06)
    return normed * (1.0 + cond_vec * gains[0]) + cond_vec * gains[1]


def teacher_kernel(
    noise_ref,
    ids_ref,
    sched_ref,
    frequency_ref,
    time_weight_ref,
    block_ref,
    block_mod_ref,
    student_shard_ref,
    feature_shard_ref,
    table_ref,
    x2_ref,
    cond_ref,
    student_ref,
    feature_ref,
    table,
    weight,
    mods,
    rows_out,
    rows_in,
    pooled,
    sched,
    cond,
    held,
    sent,
    inbox,
    start_x,
    first_x,
    table_sem,
    weight_send,
    weight_recv,
    row_send,
    row_recv,
    pooled_send,
    pooled_recv,
    sched_send,
    sched_recv,
    noise_send,
    inbox_recv,
    sent_send,
    first_send,
    first_recv,
    student_send,
    student_recv,
    feature_send,
    feature_recv,
    mods_send,
    mods_recv,
):
    mbs, rows, width = noise_ref.shape
    xl = lax.axis_index("dp_x")
    zz = lax.axis_index("dp_z")
    core = lax.axis_index("dp_c")
    sy = lax.axis_index("sec_y")
    sx = lax.axis_index("sec_x")
    sec = sy * 2 + sx
    dev = xl * 16 + zz * 2 + core
    twin = {"dp_c": 1 - core}

    def at_section(k):
        return {"sec_y": k // 2, "sec_x": k % 2}

    def at_dp(k):
        return {"dp_x": k // 16, "dp_z": (k // 2) % 8, "dp_c": k % 2}

    load_table = pltpu.make_async_copy(table_ref, table, table_sem)
    load_table.start()

    barrier = pltpu.get_barrier_semaphore()

    def greet(where):
        pl.semaphore_signal(barrier, inc=1, device_id=where, device_id_type=MESH)

    for k in range(1, 8):
        for dc in range(2):
            greet({**at_section((sec + k) % 8), "dp_c": (core + dc) % 2})
    for k in range(1, 32):
        greet(at_dp((dev + k) % 32))
    greet({"sec_x": 1 - sx, "dp_x": 1 - xl})
    pl.semaphore_wait(barrier, 46)

    def copy(src, dst, send, recv, where):
        return pltpu.make_async_remote_copy(
            src_ref=src,
            dst_ref=dst,
            send_sem=send,
            recv_sem=recv,
            device_id=where,
            device_id_type=MESH,
        )

    started = []

    def start(what, when=None):
        started.append((what, when))
        if when is None:
            what.start()
        else:
            pl.when(when)(what.start)

    source = sx == core
    relay = sx != core

    def piece_a(a, z):
        return a * 16 + (z % 8) * 2 + core

    def piece_b(a, z):
        return a * 16 + (z % 8) * 2 + 1 - core

    z_up = {"dp_z": (zz + 1) % 8}
    z_down = {"dp_z": (zz + 7) % 8}
    x_mate = {"dp_x": 1 - xl}
    x_outer = {"dp_x": 1 - xl, "sec_x": 1 - sx}
    way = {0: z_up, 1: z_down, 2: x_mate, 3: x_outer}

    def go(p, towards, when=None):
        block = weight.at[p]
        start(
            copy(block, block, weight_send.at[p * 4 + towards], weight_recv.at[p], way[towards]),
            when,
        )

    def arrive(p):
        block = weight.at[p]
        copy(block, block, weight_send.at[p], weight_recv.at[p], twin).wait_recv()

    @pl.when(source)
    def _():
        weight[dev] = block_ref[...]
        mods[...] = block_mod_ref[...]

    lend_mods = copy(block_mod_ref, mods, mods_send, mods_recv, x_outer)
    start(lend_mods, source)

    start(copy(block_ref, weight.at[dev], weight_send.at[128], weight_recv.at[dev], twin), relay)
    go(piece_a(xl, zz), 2, source)
    go(piece_a(xl, zz), 3, source)

    sched[core] = sched_ref[...]
    start(copy(sched_ref, sched.at[core], sched_send, sched_recv, twin))
    first_chip = sy == 0
    first_stage = first_chip & (core == 0)
    lender = first_chip & (core == 1) & (sx == 1)

    for j in range(mbs):
        start(
            copy(noise_ref.at[j], inbox.at[j], noise_send.at[j], inbox_recv.at[j], twin), lender
        )

    @pl.when(first_stage & (sx == 0))
    def _():
        inbox[0:mbs] = noise_ref[...]

    for k in range(1, 4):
        start(
            copy(
                feature_shard_ref,
                feature_ref.at[sec],
                feature_send.at[k],
                feature_recv.at[sec],
                {"sec_y": (sy + k) % 4},
            )
        )
    feature_ref[sec] = feature_shard_ref[...]

    @pl.when(source)
    def _():
        arrive(piece_b(xl, zz))

    go(piece_b(xl, zz), 0, source)
    go(piece_b(xl, zz), 1, source)
    go(piece_b(xl, zz), 2, source)
    go(piece_b(xl, zz), 3, source)

    vocab = table.shape[0]
    local_ids = ids_ref[...]
    lanes = lax.broadcasted_iota(jnp.int32, (local_ids.shape[0], vocab), 1)
    counts = jnp.zeros(lanes.shape, jnp.float32)
    for t in range(local_ids.shape[1]):
        counts = counts + jnp.where(local_ids[:, t : t + 1] == lanes, 1.0, 0.0)
    load_table.wait()
    part = jnp.dot(
        counts.astype(jnp.bfloat16), table[...], preferred_element_type=jnp.float32
    ) / local_ids.shape[1]
    for g in range(16):
        rows_out[g] = part[g : g + 1]
    rows_in[dev] = rows_out[dev // 2]
    for k in range(1, 32):
        other = (dev + k) % 32
        start(
            copy(
                rows_out.at[other // 2],
                rows_in.at[dev],
                row_send.at[k],
                row_recv.at[dev],
                at_dp(other),
            )
        )

    arrive_a = piece_a(1 - xl, zz)
    arrive(arrive_a)
    go(arrive_a, 2, relay)

    @pl.when(relay)
    def _():
        arrive(piece_a(xl, zz))

    for a in range(2):
        go(piece_a(a, zz), 0)
        go(piece_a(a, zz), 1)

    def take_x(z):
        p = piece_b(1 - xl, z)
        arrive(p)
        odd = z % 2
        go(p, 3, source & (odd == 1))
        go(p, 2, relay & (odd == 0))

    def take_z_b(k, up):
        z = zz + 8 - k if up else zz + k
        p = piece_b(xl, z)
        last = k == 4
        here = source & (xl == (0 if up else 1)) if last else source

        @pl.when(here)
        def _():
            arrive(p)

        if k < 3:
            go(p, 0 if up else 1, here)
        elif k == 3:
            go(p, 0 if up else 1, source & (xl == (0 if up else 1)))
        go(p, 2, here)
        go(p, 3, here)

    def take_z_a(k, up):
        z = zz + 8 - k if up else zz + k
        for a in range(2):
            reach = (4 - a) if up else (3 + a)
            if k <= reach:
                p = piece_a(a, z)
                arrive(p)
                if k < reach:
                    go(p, 0 if up else 1)

    def ring_step(k):
        for up in (True, False):
            take_z_b(k, up)
        for up in (True, False):
            take_z_a(k, up)
        if k == 1:
            take_x(zz)
        else:
            take_x(zz + 9 - k)
            take_x(zz + k - 1)

    ring_step(1)

    total = rows_in[dev]
    for k in range(1, 32):
        other = (dev + 32 - k) % 32
        copy(
            rows_out.at[0], rows_in.at[other], row_send.at[k], row_recv.at[other], at_dp(other)
        ).wait_recv()
        total = total + rows_in[other]
    pooled[sec] = total
    for k in range(1, 8):
        start(
            copy(
                pooled.at[sec],
                pooled.at[sec],
                pooled_send.at[k],
                pooled_recv.at[sec],
                at_section((sec + k) % 8),
            )
        )
    ring_step(2)
    copy(sched_ref, sched.at[1 - core], sched_send, sched_recv, twin).wait_recv()
    for k in range(1, 8):
        other = (sec + k) % 8
        copy(
            pooled.at[other],
            pooled.at[other],
            pooled_send.at[k],
            pooled_recv.at[other],
            at_section(other),
        ).wait_recv()
    for c in range(2):
        angles = sched[c, 0] * frequency_ref[...]
        embedding = jnp.concatenate([jnp.cos(angles), jnp.sin(angles)], axis=-1)
        embed = jnp.dot(
            embedding.astype(jnp.bfloat16), time_weight_ref[...], preferred_element_type=jnp.float32
        )
        for r in range(8):
            cond[c, r] = jax.nn.silu(embed[r : r + 1] + pooled[c * 4 + r % 4])
    cond_ref[...] = cond[core]
    ring_step(3)
    ring_step(4)
    take_x(zz + 4)

    @pl.when(relay)
    def _():
        for z in range(8):
            arrive(piece_b(xl, z))

    student_ref[dev] = student_shard_ref[...]
    for k in range(1, 16):
        start(
            copy(
                student_shard_ref,
                student_ref.at[dev],
                student_send.at[k],
                student_recv.at[dev],
                at_dp((dev + 2 * k) % 32),
            )
        )
    for k in range(4):
        slot = ((sy + k) % 4) * 2 + sx
        block = feature_ref.at[slot]
        across = copy(
            block, block, feature_send.at[4 + k], feature_recv.at[slot], {"sec_x": 1 - sx}
        )
        if k > 0:
            across.wait_recv()
        start(across)

    pl.when(relay)(lend_mods.wait_recv)

    def pass_on(t, slot, where):
        return copy(sent.at[t], inbox.at[slot], sent_send.at[t], inbox_recv.at[slot], where)

    def share_first(j):
        return copy(
            start_x.at[j], first_x, first_send.at[j], first_recv, {**at_section(j), "dp_c": sx}
        )

    def run_pass(p):
        def step(j, carry):
            t = p * mbs + j
            arrived = pass_on(t, t, twin)
            if p == 0:

                @pl.when(jnp.logical_not(first_stage & (sx == 0)))
                def _():
                    arrived.wait_recv()

            else:
                arrived.wait_recv()
            held[...] = inbox[t]

            if p > 0:

                @pl.when(first_stage)
                def _():
                    moved = (
                        inbox[j].astype(jnp.float32)
                        + sched[sx, 1, pl.ds(j // 2, 1), :1] * held[...].astype(jnp.float32)
                    ).astype(jnp.bfloat16)
                    held[...] = moved
                    start_x[j] = moved

                    @pl.when((j == 0) & (sx == 0))
                    def _():
                        first_x[...] = moved

                    @pl.when((j > 0) | (sx > 0))
                    def _():
                        share_first(j).start()

            hidden = held[...].astype(jnp.float32)
            mean_sq = jnp.mean(hidden * hidden, axis=-1, keepdims=True)
            cond_row = cond[sx, p * 4 + j // 2]
            inputs = (
                hidden * lax.rsqrt(mean_sq + 1e-06) * (1.0 + cond_row * mods[0:1])
                + cond_row * mods[1:2]
            ).astype(jnp.bfloat16)
            gate = 1.0 + cond_row * mods[2:3]
            chunk = 512
            for c in range(width // chunk):
                cols = slice(c * chunk, (c + 1) * chunk)
                mixed = jnp.dot(
                    inputs,
                    weight[:, :, cols].reshape(width, chunk),
                    preferred_element_type=jnp.float32,
                )
                sent[t, :, cols] = (
                    hidden[:, cols] + gate[:, cols] * jax.nn.gelu(mixed)
                ).astype(jnp.bfloat16)

            @pl.when(core == 0)
            def _():
                pass_on(t, t, twin).start()

            @pl.when((core == 1) & (sy < 3))
            def _():
                pass_on(t, t, {"dp_c": 0, "sec_y": (sy + 1) % 4}).start()

            @pl.when((core == 1) & (sy == 3))
            def _():
                if p == 0:
                    pass_on(t, t + mbs, {"dp_c": 0, "sec_y": 0}).start()
                else:

                    @pl.when((sx == 1) & (j == mbs - 1))
                    def _():
                        inbox[2 * mbs] = sent[t]

                    @pl.when((sx == 0) | (j < mbs - 1))
                    def _():
                        pass_on(t, 2 * mbs, {**at_section(j), "dp_c": sx}).start()

            return carry

        lax.fori_loop(0, mbs, step, 0)

    run_pass(0)
    for k in range(16):
        slot = (dev + 2 * k) % 32
        block = student_ref.at[slot]
        to_twin = copy(block, block, student_send.at[16 + k], student_recv.at[slot], twin)
        if k > 0:
            to_twin.wait_recv()
        start(to_twin)
    run_pass(1)

    last_self = (core == 1) & (sec == 7)
    first_self = (core == 0) & (sec == 0)

    @pl.when(jnp.logical_not(last_self))
    def _():
        pass_on(0, 2 * mbs, twin).wait_recv()

    @pl.when(jnp.logical_not(first_self))
    def _():
        share_first(0).wait_recv()

    x2_ref[...] = (
        first_x[...].astype(jnp.float32)
        + sched[core, 1, pl.ds(4 + sec // 2, 1), :1] * inbox[2 * mbs].astype(jnp.float32)
    ).astype(jnp.bfloat16)

    def drain(t, carry):
        pass_on(t, t, twin).wait_send()
        return carry

    lax.fori_loop(0, 2 * mbs - 1, drain, 0)

    @pl.when(jnp.logical_not(last_self))
    def _():
        pass_on(2 * mbs - 1, 0, twin).wait_send()

    @pl.when(first_stage)
    def _():
        for j in range(1, mbs):
            share_first(j).wait_send()

        @pl.when(sx > 0)
        def _():
            share_first(0).wait_send()

    for k in range(16):
        slot = (dev + 2 * k) % 32 + 1 - 2 * core
        block = student_ref.at[slot]
        copy(block, block, student_send.at[0], student_recv.at[slot], twin).wait_recv()
    for k in range(4):
        slot = ((sy + k) % 4) * 2 + 1 - sx
        block = feature_ref.at[slot]
        copy(block, block, feature_send.at[0], feature_recv.at[slot], twin).wait_recv()
    for what, when in started:
        if when is None:
            what.wait_send()
        else:
            pl.when(when)(what.wait_send)


def run_teacher(
    noise, ids, sched, frequency, time_weight, block, block_mod, student_shard, feature_shard, table
):
    mbs, rows, width = noise.shape
    vocab = table.shape[0]
    piece = block.shape[0]
    cols = student_shard.shape[1]
    feat_rows, feat = feature_shard.shape
    vmem = pl.BlockSpec(memory_space=pltpu.VMEM)
    dma = pltpu.SemaphoreType.DMA
    bf16 = jnp.bfloat16
    f32 = jnp.float32
    return pl.pallas_call(
        teacher_kernel,
        out_shape=(
            jax.ShapeDtypeStruct((rows, width), bf16),
            jax.ShapeDtypeStruct((8, 1, width), f32),
            jax.ShapeDtypeStruct((32, piece, cols), bf16),
            jax.ShapeDtypeStruct((8, feat_rows, feat), bf16),
        ),
        in_specs=[vmem] * 9 + [pl.BlockSpec(memory_space=pl.ANY)],
        out_specs=(vmem,) * 4,
        scratch_shapes=[
            pltpu.VMEM((vocab, width), bf16),
            pltpu.VMEM((32, piece, width), bf16),
            pltpu.VMEM((3, width), f32),
            pltpu.VMEM((16, 1, width), f32),
            pltpu.VMEM((32, 1, width), f32),
            pltpu.VMEM((8, 1, width), f32),
            pltpu.VMEM((2, 2, 8, 128), f32),
            pltpu.VMEM((2, 8, 1, width), f32),
            pltpu.VMEM((rows, width), bf16),
            pltpu.VMEM((2 * mbs, rows, width), bf16),
            pltpu.VMEM((2 * mbs + 1, rows, width), bf16),
            pltpu.VMEM((mbs, rows, width), bf16),
            pltpu.VMEM((rows, width), bf16),
            dma,
            dma((129,)),
            dma((32,)),
            dma((32,)),
            dma((32,)),
            dma((8,)),
            dma((8,)),
            dma,
            dma,
            dma((mbs,)),
            dma((2 * mbs + 1,)),
            dma((2 * mbs,)),
            dma((mbs,)),
            dma,
            dma((32,)),
            dma((32,)),
            dma((8,)),
            dma((8,)),
            dma,
            dma,
        ],
        compiler_params=pltpu.CompilerParams(
            collective_id=0, has_side_effects=True, vmem_limit_bytes=48 * 1024 * 1024
        ),
    )(noise, ids, sched, frequency, time_weight, block, block_mod, student_shard, feature_shard, table)


def loss_kernel(
    x2_ref,
    feature_ref,
    student_part_ref,
    lin_ref,
    token_ref,
    inputs_ref,
    slope_ref,
    teacher_ref,
    dist_ref,
    grad_ref,
    feats,
    grads,
    partial,
    half_out,
    half_in,
    summed,
    pieces,
    final,
    feat_send,
    feat_recv,
    grad_send,
    grad_recv,
    half_send,
    half_recv,
    piece_send,
    piece_recv,
    final_send,
    final_recv,
    twin_send,
    twin_recv,
    out_send,
    out_recv,
):
    sections, rows, feat = student_part_ref.shape
    chips = summed.shape[0]
    piece = summed.shape[1]
    width = inputs_ref.shape[1]
    xl = lax.axis_index("dp_x")
    zz = lax.axis_index("dp_z")
    core = lax.axis_index("dp_c")
    sec = lax.axis_index(SECTION)
    chip = xl * 8 + zz

    def at_section(k):
        return {"sec_y": k // 2, "sec_x": k % 2}

    def at_chip(q):
        return {"dp_x": q // 8, "dp_z": q % 8}

    def at_twin():
        return {"dp_c": 1 - core}

    barrier = pltpu.get_barrier_semaphore()

    def greet(where):
        pl.semaphore_signal(barrier, inc=1, device_id=where, device_id_type=MESH)

    for k in range(1, sections):
        greet(at_section((sec + k) % sections))
    for k in range(1, chips):
        greet(at_chip((chip + k) % chips))
    greet(at_twin())
    pl.semaphore_wait(barrier, sections + chips - 1)

    def copy(src, dst, send, recv, where):
        return pltpu.make_async_remote_copy(
            src_ref=src,
            dst_ref=dst,
            send_sem=send,
            recv_sem=recv,
            device_id=where,
            device_id_type=MESH,
        )

    def send_feat(k, slot):
        return copy(
            student_part_ref.at[k], feats.at[slot], feat_send.at[k], feat_recv.at[slot], at_section(k)
        )

    def send_grad(k, slot):
        return copy(grads.at[slot], grads.at[slot], grad_send.at[k], grad_recv.at[slot], at_section(k))

    def send_piece(q, slot):
        return copy(summed.at[q], pieces.at[slot], piece_send.at[q], piece_recv.at[slot], at_chip(q))

    def send_final(q, slot):
        block = final.at[core, slot]
        return copy(block, block, final_send.at[q], final_recv.at[slot], at_chip(q))

    def send_twin(half, slot):
        block = final.at[half, slot]
        return copy(block, block, twin_send.at[slot], twin_recv.at[slot], at_twin())

    send_half = copy(half_out, half_in, half_send, half_recv, at_twin())

    def send_out(k, slot):
        return copy(x2_ref, teacher_ref.at[slot], out_send.at[k], out_recv.at[slot], at_section(k))

    for k in range(1, sections):
        send_feat((sec + k) % sections, sec).start()
    for k in range(1, sections):
        send_out((sec + k) % sections, sec).start()
    teacher_ref[sec] = x2_ref[...]

    feat_teacher = jnp.dot(
        x2_ref[...], feature_ref[...].reshape(width, feat), preferred_element_type=jnp.float32
    )
    feat_student = student_part_ref[sec].astype(jnp.float32)
    for k in range(1, sections):
        other = (sec + k) % sections
        send_feat(other, other).wait_recv()
        feat_student = feat_student + feats[other].astype(jnp.float32)

    def unit(f):
        positive = jnp.maximum(f, 0.0)
        scale = lax.rsqrt(jnp.mean(positive * positive, axis=-1, keepdims=True) + 1e-06)
        return positive * scale, scale

    unit_s, scale_s = unit(feat_student)
    unit_t, _ = unit(feat_teacher)
    gap = unit_s - unit_t
    lin = lin_ref[...]
    dist_ref[...] = jnp.sum(lin * gap * gap, axis=-1, keepdims=True)
    unit_grad = 2.0 * token_ref[...] * lin * gap
    mean_dot = jnp.mean(unit_grad * unit_s, axis=-1, keepdims=True)
    feat_grad = scale_s * (unit_grad - unit_s * mean_dot)
    grads[sec] = jnp.where(feat_student > 0.0, feat_grad, 0.0).astype(jnp.bfloat16)
    for k in range(1, sections):
        send_grad((sec + k) % sections, sec).start()
    for k in range(1, sections):
        other = (sec + k) % sections
        send_grad(other, other).wait_recv()

    out_grad = lax.dot_general(
        grads[...].reshape(sections * rows, feat),
        feature_ref[sec],
        (((1,), (1,)), ((), ())),
        preferred_element_type=jnp.float32,
    )
    mixed_grad = (out_grad * slope_ref[...]).astype(jnp.bfloat16)
    half_rows = width // 2
    for half in range(2):
        partial[half] = lax.dot_general(
            inputs_ref[:, half * half_rows : (half + 1) * half_rows],
            mixed_grad,
            (((0,), (0,)), ((), ())),
            preferred_element_type=jnp.float32,
        ).reshape(chips, piece, -1)
    half_out[...] = partial[1 - core].astype(jnp.bfloat16)
    send_half.start()
    send_half.wait_recv()
    summed[...] = (partial[core] + half_in[...].astype(jnp.float32)).astype(jnp.bfloat16)
    for k in range(1, chips):
        send_piece((chip + k) % chips, chip).start()
    total = summed[chip].astype(jnp.float32)
    for k in range(1, chips):
        other = (chip + chips - k) % chips
        send_piece(other, other).wait_recv()
        total = total + pieces[other].astype(jnp.float32)
    final[core, chip] = total.astype(jnp.bfloat16)
    for k in range(1, chips):
        send_final((chip + k) % chips, chip).start()
    send_twin(core, chip).start()
    grad_ref[core, chip] = final[core, chip].astype(jnp.float32)
    for k in range(1, chips):
        other = (chip + chips - k) % chips
        send_final(other, other).wait_recv()
        send_twin(core, other).start()
        grad_ref[core, other] = final[core, other].astype(jnp.float32)
    for k in range(chips):
        other = (chip + chips - k) % chips
        send_twin(1 - core, other).wait_recv()
        grad_ref[1 - core, other] = final[1 - core, other].astype(jnp.float32)

    for k in range(1, sections):
        other = (sec + k) % sections
        send_out(other, other).wait_recv()
        send_out(other, sec).wait_send()
    send_half.wait_send()
    for k in range(1, sections):
        send_feat((sec + k) % sections, sec).wait_send()
        send_grad((sec + k) % sections, sec).wait_send()
    for k in range(1, chips):
        send_piece((chip + k) % chips, chip).wait_send()
        send_final((chip + k) % chips, chip).wait_send()
    for k in range(chips):
        send_twin(core, k).wait_send()


def run_loss(x2, feature, student_part, lin, token, inputs, slope):
    sections, rows, feat = student_part.shape
    width = inputs.shape[1]
    cols = slope.shape[1]
    chips = 16
    piece = width // (2 * chips)
    vmem = pl.BlockSpec(memory_space=pltpu.VMEM)
    dma = pltpu.SemaphoreType.DMA
    bf16 = jnp.bfloat16
    teacher, dist, grad = pl.pallas_call(
        loss_kernel,
        out_shape=(
            jax.ShapeDtypeStruct((sections, rows, width), bf16),
            jax.ShapeDtypeStruct((rows, 1), jnp.float32),
            jax.ShapeDtypeStruct((2, chips, piece, cols), jnp.float32),
        ),
        in_specs=[vmem] * 7,
        out_specs=(vmem, vmem, vmem),
        scratch_shapes=[
            pltpu.VMEM((sections, rows, feat), bf16),
            pltpu.VMEM((sections, rows, feat), bf16),
            pltpu.VMEM((2, chips, piece, cols), jnp.float32),
            pltpu.VMEM((chips, piece, cols), bf16),
            pltpu.VMEM((chips, piece, cols), bf16),
            pltpu.VMEM((chips, piece, cols), bf16),
            pltpu.VMEM((chips, piece, cols), bf16),
            pltpu.VMEM((2, chips, piece, cols), bf16),
            dma((sections,)),
            dma((sections,)),
            dma((sections,)),
            dma((sections,)),
            dma,
            dma,
            dma((chips,)),
            dma((chips,)),
            dma((chips,)),
            dma((chips,)),
            dma((chips,)),
            dma((chips,)),
            dma((sections,)),
            dma((sections,)),
        ],
        compiler_params=pltpu.CompilerParams(
            collective_id=1, has_side_effects=True, vmem_limit_bytes=40 * 1024 * 1024
        ),
    )(x2, feature, student_part, lin, token, inputs, slope)
    return teacher, dist.reshape(rows), grad.reshape(width, cols)


def local(
    noise,
    sched_index,
    text_ids,
    text_table,
    time_weight,
    block_weight,
    block_mod,
    student_weight,
    student_mod,
    feature_weight,
    lin_weight,
    token_weight,
):
    batches, tokens, model_width = noise.shape
    sections = lax.axis_size(SECTION)
    own_section = lax.axis_index(SECTION)
    row_count = batches * tokens
    share_rows = row_count // sections
    vocab_rows = text_table.shape[0]
    offset = lax.axis_index(DP) * vocab_rows
    ids = lax.dynamic_index_in_dim(
        text_ids.reshape(16, 8, -1), own_section, 1, keepdims=False
    ) - offset
    indices_f = sched_index.astype(jnp.float32)
    half_freq = time_weight.shape[0] // 2
    frequency = jnp.exp(-math.log(10000.0) * jnp.arange(half_freq, dtype=jnp.float32) / half_freq)
    deltas = (indices_f[:, 1:] - indices_f[:, :-1]) / LEVELS
    sched = jnp.broadcast_to(
        jnp.stack([indices_f[:, :2].T.reshape(8), deltas.T.reshape(8)])[:, :, None], (2, 8, 128)
    )
    x2, cond, student_full, feature_full = run_teacher(
        noise.reshape(sections, share_rows, model_width),
        ids,
        sched,
        frequency[None, :],
        time_weight,
        block_weight[0],
        block_mod[0],
        student_weight,
        feature_weight,
        text_table,
    )
    col_count = student_weight.shape[1]
    first_col = own_section * col_count
    noise_f = noise.astype(jnp.float32)
    cond_zero = cond[:batches]
    time_zero = (indices_f[:, 0] / LEVELS)[:, None, None]
    inputs = (
        modulated(noise_f, cond_zero, student_mod)
        .astype(jnp.bfloat16)
        .reshape(row_count, model_width)
    )
    mixed = jnp.dot(
        inputs, student_full.reshape(model_width, col_count), preferred_element_type=jnp.float32
    )
    z_cols = lax.dynamic_slice_in_dim(noise_f, first_col, col_count, 2).reshape(
        row_count, col_count
    )
    gate_full = 1.0 + cond_zero * student_mod[2]
    gate_rows = jnp.broadcast_to(
        lax.dynamic_slice_in_dim(gate_full, first_col, col_count, 2), (batches, tokens, col_count)
    ).reshape(row_count, col_count)
    t_rows = jnp.broadcast_to(time_zero, (batches, tokens, 1)).reshape(row_count, 1)

    def advance(mixed_in):
        return z_cols - t_rows * (z_cols + gate_rows * jax.nn.gelu(mixed_in))

    moved, pull_back = jax.vjp(advance, mixed)
    slope = pull_back(jnp.ones_like(moved))[0]
    feat_student = jnp.dot(
        moved.astype(jnp.bfloat16), feature_weight, preferred_element_type=jnp.float32
    )
    weight_share = lax.dynamic_slice_in_dim(token_weight, own_section * share_rows, share_rows, 0)
    teacher, token_distance, student_grad = run_loss(
        x2,
        feature_full,
        feat_student.astype(jnp.bfloat16).reshape(sections, share_rows, -1),
        lin_weight[None, :],
        weight_share[:, None],
        inputs,
        slope,
    )
    return (teacher.reshape(noise.shape), student_grad, token_distance)


def solution(mesh):
    torus = Mesh(mesh.devices.reshape(2, 8, 2, 4, 2), DP + SECTION)
    in_specs = (
        P(DP, None, None),
        P(DP, None),
        P(),
        P(DP, None),
        P(),
        P(SECTION, DP, None),
        P(SECTION, None, None),
        P(DP, SECTION),
        P(),
        P(SECTION, None),
        P(),
        P(DP),
    )
    out_specs = (P(DP, None, None), P(None, SECTION), P(DP + SECTION))
    return jax.shard_map(local, mesh=torus, in_specs=in_specs, out_specs=out_specs, check_vma=False)
```

time: 310 us -> 181 us (0.58)
  waiting for transfers between devices: 47.4 us -> 0 us
  Pallas kernels: 190 us -> 169 us
  starting transfers between devices: 19.2 us -> 0 us
  between operations: 14.3 us -> 0.84 us
  local copies, waits for them, and re-layouts: 17.3 us -> 6.6 us
  other arithmetic: 14 us -> 3.57 us
  matrix products: 6.79 us -> 0.76 us
    all_to_all x2 -> x0, waiting for transfers between devices: 44.2 us -> none  [the longest x1 23.7 us: summed_on_arrival(): lax.all_to_all(blocks, axis, split_axis=0, concat_axis=0, tiled=True)]
    pallas_call x2, Pallas kernels: 190 us -> 169 us  [the longest x1 116 us: run_teacher(): pl.pallas_call(teacher_kernel, out_shape=(jax.ShapeDtypeStruct((rows, wid...]
    all_to_all x2 -> x0, starting transfers between devices: 17.6 us -> none  [the longest x1 11.1 us: summed_on_arrival(): lax.all_to_all(blocks, axis, split_axis=0, concat_axis=0, tiled=True)]
    reduce_sum x12 -> x0, other arithmetic: 7.71 us -> none  [the longest x11 7.58 us: add_group(): jnp.sum((id_block[:, :, None] == vocab_ids).astype(jnp.float32), axis=1)]
    unnamed x35 -> x20, local copies, waits for them, and re-layouts: 11.2 us -> 4.72 us
    dot_general x4 -> x1, matrix products: 5.87 us -> 0.55 us  [local(): jnp.dot(inputs, student_full.reshape(model_width, col_count), preferred_e...]
  transfers between devices with their start and end apart: 5 -> 0, of which waited for: 3 -> 0; matrix products, arithmetic and copies ran while one was open for 9% -> 0% of each run, Pallas kernels for 43% -> 0%
where the time goes in v3:
time: 181 us
  Pallas kernels  169 us (93%)
  local copies, waits for them, and re-layouts  6.6 us (4%)
  other arithmetic  3.57 us (2%)
    pallas_call x1, Pallas kernels, run_teacher(): pl.pallas_call(teacher_kernel, out_shape=(jax.ShapeDtypeStruct((rows, wid...  116 us
    pallas_call x1, Pallas kernels, run_loss(): pl.pallas_call(loss_kernel, out_shape=(jax.ShapeDtypeStruct((sections, ro...  53.3 us
    unnamed x20, local copies, waits for them, and re-layouts  4.72 us

profile of v3, /device:TPU:1, one launch (start us, length us, event | category | flops | bytes accessed | tf_op | source)
XLA Modules:
  0.0 180.9 jit_solution(3854480174822634320)
XLA Ops:
  0.7 0.6 copy-done
  1.4 0.7 convert_element_type.15
  2.1 0.1 multiply_reduce_fusion.1
  2.3 0.1 broadcast_in_dim.31
  2.4 1.4 multiply_reduce_fusion
  3.8 0.1 copy.39
  3.9 0.1 stack_reshape.6
  4.0 0.1 copy.40
  4.1 0.1 stack_reshape.7
  4.3 0.1 copy.48.token_ref
  4.4 0.8 copy.61
  5.2 0.9 slice_reduce_fusion.2
  6.2 0.9 copy.37
  7.1 0.2 convert_element_type.16
  7.3 0.1 constant_dynamic-slice_fusion
  7.5 115.8 %shard_map.139 = (bf16[32,1536]{1,0:T(8,128)(2,1)S(1)}, f32[8,1,1536]{2,1,0:T(1,128)S(1)}, bf16[32,48,192]{2,1,0:T(8,128)(2,1)S(1)}, bf16[8,192,512]{2,1,0:T(8,128)(2,1)S(1)}) custom-call(bf16[8,32,1536]{2,1,0:T(8,128)(2,1)S(1)} %bitcast.59, s32[16,77]{1,0:T(8,128)S(1)} %subtract_bitcast_fusion.ids_ref, f32[2,8,128]{2,1,0:T(8,128)S(1)} %broadcast_in_dim.14.sched_ref, ...), custom_call_target="tpu_custom_call" | custom-call | tf_op jit(solution)/shard_map/pallas_call | solution.py:510
  123.3 0.1 fusion.15
  123.5 0.3 add_convert_fusion
  123.8 0.5 fusion.7
  124.4 0.2 convolution_convert_fusion
  124.6 53.3 %shard_map.140 = (bf16[8,32,1536]{2,1,0:T(8,128)(2,1)S(1)}, f32[32,1]{1,0:T(8,128)S(1)}, f32[2,16,48,192]{3,2,1,0:T(8,128)S(1)}) custom-call(bf16[32,1536]{1,0:T(8,128)(2,1)S(1)} %get-tuple-element.10.x2_ref, bf16[8,192,512]{2,1,0:T(8,128)(2,1)S(1)} %get-tuple-element.11.feature_ref, bf16[8,32,512]{2,1,0:T(8,128)(2,1)S(1)} %bitcast.63, ...), custom_call_target="tpu_custom_call" | custom-call | tf_op jit(solution)/shard_map/pallas_call | solution.py:760
  177.9 1.5 copy.49
  179.4 0.6 reduce.4
  180.0 0.9 copy.64
  (27 shorter events, 0.5 us)
Async XLA Ops:
  0.6 0.7 copy-start
  0.6 6.4 %copy-start.1 = (bf16[4,64,1536]{2,1,0:T(8,128)(2,1)S(1)}, bf16[4,64,1536]{2,1,0:T(8,128)(2,1)}, u32[]{:S(2)}) copy-start(bf16[4,64,1536]{2,1,0:T(8,128)(2,1)} %param.12) | copy-start | bytes 2359300
  4.3 3.2 %copy-start.2 = (bf16[192,512]{1,0:T(8,128)(2,1)S(1)}, bf16[192,512]{1,0:T(8,128)(2,1)}, u32[]{:S(2)}) copy-start(bf16[192,512]{1,0:T(8,128)(2,1)} %feature_shard_ref.1) | copy-start | bytes 589828
  4.3 3.2 %copy-start.3 = (bf16[256,1536]{1,0:T(8,128)(2,1)S(1)}, bf16[256,1536]{1,0:T(8,128)(2,1)}, u32[]{:S(2)}) copy-start(bf16[256,1536]{1,0:T(8,128)(2,1)} %time_weight_ref.1) | copy-start | bytes 2359300
  4.3 3.2 %copy-start.4 = (bf16[1,48,1536]{2,1,0:T(8,128)(2,1)S(1)}, bf16[1,48,1536]{2,1,0:T(8,128)(2,1)}, u32[]{:S(2)}) copy-start(bf16[1,48,1536]{2,1,0:T(8,128)(2,1)} %param.17) | copy-start | bytes 442372
  4.3 3.2 %copy-start.5 = (bf16[48,192]{1,0:T(8,128)(2,1)S(1)}, bf16[48,192]{1,0:T(8,128)(2,1)}, u32[]{:S(2)}) copy-start(bf16[48,192]{1,0:T(8,128)(2,1)} %student_shard_ref.1) | copy-start | bytes 55300
  123.8 0.8 copy-start.6

commit v4 on v3

v4 whole, which is shorter than its diff:
```python
import math

import jax
import jax.numpy as jnp
from jax import lax
from jax.experimental import pallas as pl
from jax.experimental.pallas import tpu as pltpu
from jax.sharding import Mesh
from jax.sharding import PartitionSpec as P

LEVELS = 1000
DP = ("dp_x", "dp_z", "dp_c")
SECTION = ("sec_y", "sec_x")
MESH = pl.DeviceIdType.MESH


def train_kernel(
    noise_ref,
    ids_ref,
    sched_ref,
    frequency_ref,
    time_weight_ref,
    block_ref,
    block_mod_ref,
    student_shard_ref,
    feature_shard_ref,
    student_mod_ref,
    lin_ref,
    token_ref,
    table_ref,
    teacher_ref,
    dist_ref,
    grad_ref,
    table,
    weight,
    mods,
    rows_out,
    rows_in,
    pooled,
    sched,
    cond,
    held,
    sent,
    inbox,
    start_x,
    first_x,
    student_ref,
    feature_ref,
    student_t,
    slope,
    feat_part,
    feats,
    grads,
    partial,
    half_out,
    half_in,
    summed,
    pieces,
    final,
    table_sem,
    weight_send,
    weight_recv,
    row_send,
    row_recv,
    pooled_send,
    pooled_recv,
    sched_send,
    sched_recv,
    noise_send,
    inbox_recv,
    sent_send,
    first_send,
    first_recv,
    student_send,
    student_recv,
    feature_send,
    feature_recv,
    mods_send,
    mods_recv,
    feat_send,
    feat_recv,
    grad_send,
    grad_recv,
    half_send,
    half_recv,
    piece_send,
    piece_recv,
    final_send,
    final_recv,
    twin_send,
    twin_recv,
    out_send,
    out_recv,
):
    mbs, rows, width = noise_ref.shape
    chunk = 512
    chunks = width // chunk
    xl = lax.axis_index("dp_x")
    zz = lax.axis_index("dp_z")
    core = lax.axis_index("dp_c")
    sy = lax.axis_index("sec_y")
    sx = lax.axis_index("sec_x")
    sec = sy * 2 + sx
    dev = xl * 16 + zz * 2 + core
    twin = {"dp_c": 1 - core}

    def at_section(k):
        return {"sec_y": k // 2, "sec_x": k % 2}

    def at_dp(k):
        return {"dp_x": k // 16, "dp_z": (k // 2) % 8, "dp_c": k % 2}

    load_table = pltpu.make_async_copy(table_ref, table, table_sem)
    load_table.start()

    barrier = pltpu.get_barrier_semaphore()

    def greet(where):
        pl.semaphore_signal(barrier, inc=1, device_id=where, device_id_type=MESH)

    for k in range(1, 8):
        for dc in range(2):
            greet({**at_section((sec + k) % 8), "dp_c": (core + dc) % 2})
    for k in range(1, 32):
        greet(at_dp((dev + k) % 32))
    greet({"sec_x": 1 - sx, "dp_x": 1 - xl})
    pl.semaphore_wait(barrier, 46)

    def copy(src, dst, send, recv, where):
        return pltpu.make_async_remote_copy(
            src_ref=src,
            dst_ref=dst,
            send_sem=send,
            recv_sem=recv,
            device_id=where,
            device_id_type=MESH,
        )

    started = []

    def start(what, when=None):
        started.append((what, when))
        if when is None:
            what.start()
        else:
            pl.when(when)(what.start)

    source = sx == core
    relay = sx != core

    def piece_a(a, z):
        return a * 16 + (z % 8) * 2 + core

    def piece_b(a, z):
        return a * 16 + (z % 8) * 2 + 1 - core

    z_up = {"dp_z": (zz + 1) % 8}
    z_down = {"dp_z": (zz + 7) % 8}
    x_mate = {"dp_x": 1 - xl}
    x_outer = {"dp_x": 1 - xl, "sec_x": 1 - sx}
    way = {0: z_up, 1: z_down, 2: x_mate, 3: x_outer}

    def go(p, towards, when=None):
        block = weight.at[p]
        start(
            copy(block, block, weight_send.at[p * 4 + towards], weight_recv.at[p], way[towards]),
            when,
        )

    def arrive(p):
        block = weight.at[p]
        copy(block, block, weight_send.at[p], weight_recv.at[p], twin).wait_recv()

    @pl.when(source)
    def _():
        weight[dev] = block_ref[...]
        mods[...] = block_mod_ref[...]

    lend_mods = copy(block_mod_ref, mods, mods_send, mods_recv, x_outer)
    start(lend_mods, source)

    start(copy(block_ref, weight.at[dev], weight_send.at[dev * 4], weight_recv.at[dev], twin), relay)
    go(piece_a(xl, zz), 2, source)
    go(piece_a(xl, zz), 3, source)

    sched[core] = sched_ref[...]
    start(copy(sched_ref, sched.at[core], sched_send, sched_recv, twin))
    first_chip = sy == 0
    first_stage = first_chip & (core == 0)
    lender = first_chip & (core == 1) & (sx == 1)

    for j in range(mbs):
        for c in range(chunks):
            cols = slice(c * chunk, (c + 1) * chunk)
            start(
                copy(
                    noise_ref.at[j, :, cols],
                    inbox.at[j, :, cols],
                    noise_send.at[j * chunks + c],
                    inbox_recv.at[j * chunks + c],
                    twin,
                ),
                lender,
            )

    @pl.when(first_stage & (sx == 0))
    def _():
        inbox[0:mbs] = noise_ref[...]

    for k in range(1, 4):
        start(
            copy(
                feature_shard_ref,
                feature_ref.at[sec],
                feature_send.at[k],
                feature_recv.at[sec],
                {"sec_y": (sy + k) % 4},
            )
        )
    feature_ref[sec] = feature_shard_ref[...]

    @pl.when(source)
    def _():
        arrive(piece_b(xl, zz))

    go(piece_b(xl, zz), 0, source)
    go(piece_b(xl, zz), 1, source)
    go(piece_b(xl, zz), 2, source)
    go(piece_b(xl, zz), 3, source)

    vocab = table.shape[0]
    local_ids = ids_ref[...]
    lanes = lax.broadcasted_iota(jnp.int32, (local_ids.shape[0], vocab), 1)
    counts = jnp.zeros(lanes.shape, jnp.float32)
    for t in range(local_ids.shape[1]):
        counts = counts + jnp.where(local_ids[:, t : t + 1] == lanes, 1.0, 0.0)
    load_table.wait()
    part = jnp.dot(
        counts.astype(jnp.bfloat16), table[...], preferred_element_type=jnp.float32
    ) / local_ids.shape[1]
    for g in range(16):
        rows_out[g] = part[g : g + 1]
    rows_in[dev] = rows_out[dev // 2]
    for k in range(1, 32):
        other = (dev + k) % 32
        start(
            copy(
                rows_out.at[other // 2],
                rows_in.at[dev],
                row_send.at[k],
                row_recv.at[dev],
                at_dp(other),
            )
        )

    arrive_a = piece_a(1 - xl, zz)
    arrive(arrive_a)
    go(arrive_a, 2, relay)

    @pl.when(relay)
    def _():
        arrive(piece_a(xl, zz))

    for a in range(2):
        go(piece_a(a, zz), 0)
        go(piece_a(a, zz), 1)

    def take_x(z):
        p = piece_b(1 - xl, z)
        arrive(p)
        odd = z % 2
        go(p, 3, source & (odd == 1))
        go(p, 2, relay & (odd == 0))

    def take_z_b(k, up):
        z = zz + 8 - k if up else zz + k
        p = piece_b(xl, z)
        last = k == 4
        here = source & (xl == (0 if up else 1)) if last else source

        @pl.when(here)
        def _():
            arrive(p)

        if k < 3:
            go(p, 0 if up else 1, here)
        elif k == 3:
            go(p, 0 if up else 1, source & (xl == (0 if up else 1)))
        go(p, 2, here)
        go(p, 3, here)

    def take_z_a(k, up):
        z = zz + 8 - k if up else zz + k
        for a in range(2):
            reach = (4 - a) if up else (3 + a)
            if k <= reach:
                p = piece_a(a, z)
                arrive(p)
                if k < reach:
                    go(p, 0 if up else 1)

    def ring_step(k):
        for up in (True, False):
            take_z_b(k, up)
        for up in (True, False):
            take_z_a(k, up)
        if k == 1:
            take_x(zz)
        else:
            take_x(zz + 9 - k)
            take_x(zz + k - 1)

    ring_step(1)

    total = rows_in[dev]
    for k in range(1, 32):
        other = (dev + 32 - k) % 32
        copy(
            rows_out.at[0], rows_in.at[other], row_send.at[k], row_recv.at[other], at_dp(other)
        ).wait_recv()
        total = total + rows_in[other]
    pooled[sec] = total
    for k in range(1, 8):
        start(
            copy(
                pooled.at[sec],
                pooled.at[sec],
                pooled_send.at[k],
                pooled_recv.at[sec],
                at_section((sec + k) % 8),
            )
        )
    ring_step(2)
    copy(sched_ref, sched.at[1 - core], sched_send, sched_recv, twin).wait_recv()
    for k in range(1, 8):
        other = (sec + k) % 8
        copy(
            pooled.at[other],
            pooled.at[other],
            pooled_send.at[k],
            pooled_recv.at[other],
            at_section(other),
        ).wait_recv()
    for c in range(2):
        angles = sched[c, 0] * frequency_ref[...]
        embedding = jnp.concatenate([jnp.cos(angles), jnp.sin(angles)], axis=-1)
        embed = jnp.dot(
            embedding.astype(jnp.bfloat16), time_weight_ref[...], preferred_element_type=jnp.float32
        )
        for r in range(8):
            cond[c, r] = jax.nn.silu(embed[r : r + 1] + pooled[c * 4 + r % 4])
    ring_step(3)
    ring_step(4)
    take_x(zz + 4)

    @pl.when(relay)
    def _():
        for z in range(8):
            arrive(piece_b(xl, z))

    student_ref[dev] = student_shard_ref[...]
    for k in range(1, 16):
        start(
            copy(
                student_shard_ref,
                student_ref.at[dev],
                student_send.at[k],
                student_recv.at[dev],
                at_dp((dev + 2 * k) % 32),
            )
        )
    pl.when(relay)(lend_mods.wait_recv)

    def pass_on(t, slot, c, where):
        cols = pl.ds(c * chunk, chunk)
        return copy(
            sent.at[t, :, cols],
            inbox.at[slot, :, cols],
            sent_send.at[t * chunks + c],
            inbox_recv.at[slot * chunks + c],
            where,
        )

    def hop(t, p, j, c):
        @pl.when(core == 0)
        def _():
            pass_on(t, t, c, twin).start()

        @pl.when((core == 1) & (sy < 3))
        def _():
            pass_on(t, t, c, {"dp_c": 0, "sec_y": (sy + 1) % 4}).start()

        @pl.when((core == 1) & (sy == 3))
        def _():
            if p == 0:
                pass_on(t, t + mbs, c, {"dp_c": 0, "sec_y": 0}).start()
            else:

                @pl.when((sx == 1) & (j == mbs - 1))
                def _():
                    cols = slice(c * chunk, (c + 1) * chunk)
                    inbox[2 * mbs, :, cols] = sent[t, :, cols]

                @pl.when((sx == 0) | (j < mbs - 1))
                def _():
                    pass_on(t, 2 * mbs, c, {**at_section(j), "dp_c": sx}).start()

    def share_first(j):
        return copy(
            start_x.at[j], first_x, first_send.at[j], first_recv, {**at_section(j), "dp_c": sx}
        )

    def run_pass(p):
        def step(j, carry):
            t = p * mbs + j
            waited = jnp.logical_not(first_stage & (sx == 0)) if p == 0 else None
            for c in range(chunks):
                arrived = pass_on(t, t, c, twin)
                if p == 0:
                    pl.when(waited)(arrived.wait_recv)
                else:
                    arrived.wait_recv()
            held[...] = inbox[t]

            if p > 0:

                @pl.when(first_stage)
                def _():
                    moved = (
                        inbox[j].astype(jnp.float32)
                        + sched[sx, 1, pl.ds(j // 2, 1), :1] * held[...].astype(jnp.float32)
                    ).astype(jnp.bfloat16)
                    held[...] = moved
                    start_x[j] = moved

                    @pl.when((j == 0) & (sx == 0))
                    def _():
                        first_x[...] = moved

                    @pl.when((j > 0) | (sx > 0))
                    def _():
                        share_first(j).start()

            hidden = held[...].astype(jnp.float32)
            mean_sq = jnp.mean(hidden * hidden, axis=-1, keepdims=True)
            cond_row = cond[sx, p * 4 + j // 2]
            inputs = (
                hidden * lax.rsqrt(mean_sq + 1e-06) * (1.0 + cond_row * mods[0:1])
                + cond_row * mods[1:2]
            ).astype(jnp.bfloat16)
            gate = 1.0 + cond_row * mods[2:3]
            for c in range(chunks):
                cols = slice(c * chunk, (c + 1) * chunk)
                mixed = jnp.dot(
                    inputs,
                    weight[:, :, cols].reshape(width, chunk),
                    preferred_element_type=jnp.float32,
                )
                sent[t, :, cols] = (
                    hidden[:, cols] + gate[:, cols] * jax.nn.gelu(mixed)
                ).astype(jnp.bfloat16)
                hop(t, p, j, c)

            return carry

        lax.fori_loop(0, mbs, step, 0)

    run_pass(0)
    for k in range(16):
        slot = (dev + 2 * k) % 32
        block = student_ref.at[slot]
        to_twin = copy(block, block, student_send.at[16 + k], student_recv.at[slot], twin)
        if k > 0:
            to_twin.wait_recv()
        start(to_twin)
    for k in range(16):
        slot = (dev + 2 * k) % 32 + 1 - 2 * core
        block = student_ref.at[slot]
        copy(block, block, student_send.at[0], student_recv.at[slot], twin).wait_recv()

    def own_cols(x):
        n = student_ref.shape[2]
        picked = x[:, 0:n]
        for k in range(1, 8):
            picked = jnp.where(sec == k, x[:, k * n : (k + 1) * n], picked)
        return picked

    root = math.sqrt(2.0 / math.pi)
    for n in range(4):
        latents = noise_ref[2 * n : 2 * n + 2].reshape(2 * rows, width).astype(jnp.float32)
        mean_sq = jnp.mean(latents * latents, axis=-1, keepdims=True)
        cond_row = cond[core, n]
        student_in = (
            latents * lax.rsqrt(mean_sq + 1e-06) * (1.0 + cond_row * student_mod_ref[0:1])
            + cond_row * student_mod_ref[1:2]
        ).astype(jnp.bfloat16)
        mixed = jnp.dot(
            student_in,
            student_ref[...].reshape(width, student_ref.shape[2]),
            preferred_element_type=jnp.float32,
        )
        bent = jnp.tanh(root * (mixed + 0.044715 * mixed * mixed * mixed))
        half = 0.5 * (1.0 + bent)
        bend = half + 0.5 * mixed * (1.0 - bent * bent) * root * (
            1.0 + 3.0 * 0.044715 * mixed * mixed
        )
        gate = own_cols(1.0 + cond_row * student_mod_ref[2:3])
        level = sched[core, 0, n : n + 1, :1] / LEVELS
        z = own_cols(latents)
        moved = z - level * (z + gate * (mixed * half))
        slope[2 * n * rows : 2 * (n + 1) * rows] = -level * gate * bend
        student_t[:, 2 * n * rows : 2 * (n + 1) * rows] = student_in.T
        feat_part[2 * n : 2 * n + 2] = (
            jnp.dot(
                moved.astype(jnp.bfloat16),
                feature_shard_ref[...],
                preferred_element_type=jnp.float32,
            )
            .astype(jnp.bfloat16)
            .reshape(2, rows, -1)
        )

    def send_feat(k, slot):
        return copy(
            feat_part.at[k], feats.at[slot], feat_send.at[k], feat_recv.at[slot], at_section(k)
        )

    for k in range(1, 8):
        start(send_feat((sec + k) % 8, sec))
    for k in range(4):
        slot = ((sy + k) % 4) * 2 + sx
        block = feature_ref.at[slot]
        across = copy(
            block, block, feature_send.at[4 + k], feature_recv.at[slot], x_outer
        )
        if k > 0:
            across.wait_recv()
        start(across)

    run_pass(1)

    last_self = (core == 1) & (sec == 7)
    first_self = (core == 0) & (sec == 0)

    for c in range(chunks):
        pl.when(jnp.logical_not(last_self))(pass_on(0, 2 * mbs, c, twin).wait_recv)

    @pl.when(jnp.logical_not(first_self))
    def _():
        share_first(0).wait_recv()

    x2 = (
        first_x[...].astype(jnp.float32)
        + sched[core, 1, pl.ds(4 + sec // 2, 1), :1] * inbox[2 * mbs].astype(jnp.float32)
    ).astype(jnp.bfloat16)
    teacher_ref[sec] = x2
    for k in range(4):
        slot = ((sy + k) % 4) * 2 + 1 - sx
        block = feature_ref.at[slot]
        copy(block, block, feature_send.at[0], feature_recv.at[slot], twin).wait_recv()

    sections = 8
    chips = summed.shape[0]
    piece = summed.shape[1]
    feat = feats.shape[2]
    chip = xl * 8 + zz

    def at_chip(q):
        return {"dp_x": q // 8, "dp_z": q % 8}

    def send_grad(k, slot):
        return copy(grads.at[slot], grads.at[slot], grad_send.at[k], grad_recv.at[slot], at_section(k))

    def send_piece(q, slot):
        return copy(summed.at[q], pieces.at[slot], piece_send.at[q], piece_recv.at[slot], at_chip(q))

    def send_final(q, slot):
        block = final.at[core, slot]
        return copy(block, block, final_send.at[q], final_recv.at[slot], at_chip(q))

    def send_twin(half, slot):
        block = final.at[half, slot]
        return copy(block, block, twin_send.at[slot], twin_recv.at[slot], twin)

    send_half = copy(half_out, half_in, half_send, half_recv, twin)

    def send_out(k, slot):
        return copy(teacher_ref.at[slot], teacher_ref.at[slot], out_send.at[k], out_recv.at[slot], at_section(k))

    feat_teacher = jnp.dot(
        x2, feature_ref[...].reshape(width, feat), preferred_element_type=jnp.float32
    )
    feat_student = feat_part[sec].astype(jnp.float32)
    for k in range(1, sections):
        other = (sec + k) % sections
        send_feat(other, other).wait_recv()
        feat_student = feat_student + feats[other].astype(jnp.float32)

    def unit(f):
        positive = jnp.maximum(f, 0.0)
        scale = lax.rsqrt(jnp.mean(positive * positive, axis=-1, keepdims=True) + 1e-06)
        return positive * scale, scale

    unit_s, scale_s = unit(feat_student)
    unit_t, _ = unit(feat_teacher)
    gap = unit_s - unit_t
    lin = lin_ref[...]
    dist_ref[...] = lax.dot_general(
        lin,
        gap * gap,
        (((1,), (1,)), ((), ())),
        preferred_element_type=jnp.float32,
        precision=lax.Precision.HIGHEST,
    )
    unit_grad = 2.0 * token_ref[...] * lin * gap
    mean_dot = jnp.mean(unit_grad * unit_s, axis=-1, keepdims=True)
    feat_grad = scale_s * (unit_grad - unit_s * mean_dot)
    grads[sec] = jnp.where(feat_student > 0.0, feat_grad, 0.0).astype(jnp.bfloat16)
    for k in range(1, sections):
        send_grad((sec + k) % sections, sec).start()
    for k in range(1, sections):
        other = (sec + k) % sections
        send_grad(other, other).wait_recv()

    out_grad = lax.dot_general(
        grads[...].reshape(sections * rows, feat),
        feature_ref[sec],
        (((1,), (1,)), ((), ())),
        preferred_element_type=jnp.float32,
    )
    mixed_grad = (out_grad * slope[...]).astype(jnp.bfloat16)
    half_rows = width // 2
    for half in range(2):
        partial[half] = lax.dot_general(
            student_t[half * half_rows : (half + 1) * half_rows],
            mixed_grad,
            (((1,), (0,)), ((), ())),
            preferred_element_type=jnp.float32,
        ).reshape(chips, piece, -1)
    half_out[...] = partial[1 - core].astype(jnp.bfloat16)
    send_half.start()
    for k in range(1, sections):
        send_out((sec + k) % sections, sec).start()
    send_half.wait_recv()
    summed[...] = (partial[core] + half_in[...].astype(jnp.float32)).astype(jnp.bfloat16)
    for k in range(1, chips):
        send_piece((chip + k) % chips, chip).start()
    total = summed[chip].astype(jnp.float32)
    for k in range(1, chips):
        other = (chip + chips - k) % chips
        send_piece(other, other).wait_recv()
        total = total + pieces[other].astype(jnp.float32)
    final[core, chip] = total.astype(jnp.bfloat16)
    for k in range(1, chips):
        send_final((chip + k) % chips, chip).start()
    send_twin(core, chip).start()
    grad_ref[core, chip] = final[core, chip].astype(jnp.float32)
    for k in range(1, chips):
        other = (chip + chips - k) % chips
        send_final(other, other).wait_recv()
        send_twin(core, other).start()
        grad_ref[core, other] = final[core, other].astype(jnp.float32)
    for k in range(chips):
        other = (chip + chips - k) % chips
        send_twin(1 - core, other).wait_recv()
        grad_ref[1 - core, other] = final[1 - core, other].astype(jnp.float32)

    for k in range(1, sections):
        other = (sec + k) % sections
        send_out(other, other).wait_recv()
        send_out(other, sec).wait_send()
    send_half.wait_send()
    for k in range(1, sections):
        send_grad((sec + k) % sections, sec).wait_send()
    for k in range(1, chips):
        send_piece((chip + k) % chips, chip).wait_send()
        send_final((chip + k) % chips, chip).wait_send()
    for k in range(chips):
        send_twin(core, k).wait_send()

    def drain(t, carry):
        for c in range(chunks):
            pass_on(t, t, c, twin).wait_send()
        return carry

    lax.fori_loop(0, 2 * mbs - 1, drain, 0)

    for c in range(chunks):
        pl.when(jnp.logical_not(last_self))(pass_on(2 * mbs - 1, 0, c, twin).wait_send)

    @pl.when(first_stage)
    def _():
        for j in range(1, mbs):
            share_first(j).wait_send()

        @pl.when(sx > 0)
        def _():
            share_first(0).wait_send()

    for what, when in started:
        if when is None:
            what.wait_send()
        else:
            pl.when(when)(what.wait_send)


def run_train(
    noise,
    ids,
    sched,
    frequency,
    time_weight,
    block,
    block_mod,
    student_shard,
    feature_shard,
    student_mod,
    lin,
    token,
    table,
):
    mbs, rows, width = noise.shape
    vocab = table.shape[0]
    piece = block.shape[0]
    cols = student_shard.shape[1]
    feat_rows, feat = feature_shard.shape
    vmem = pl.BlockSpec(memory_space=pltpu.VMEM)
    dma = pltpu.SemaphoreType.DMA
    bf16 = jnp.bfloat16
    f32 = jnp.float32
    return pl.pallas_call(
        train_kernel,
        out_shape=(
            jax.ShapeDtypeStruct((mbs, rows, width), bf16),
            jax.ShapeDtypeStruct((1, rows), f32),
            jax.ShapeDtypeStruct((2, 16, piece, cols), f32),
        ),
        in_specs=[vmem] * 12 + [pl.BlockSpec(memory_space=pl.ANY)],
        out_specs=(vmem,) * 3,
        scratch_shapes=[
            pltpu.VMEM((vocab, width), bf16),
            pltpu.VMEM((32, piece, width), bf16),
            pltpu.VMEM((3, width), f32),
            pltpu.VMEM((16, 1, width), f32),
            pltpu.VMEM((32, 1, width), f32),
            pltpu.VMEM((8, 1, width), f32),
            pltpu.VMEM((2, 2, 8, 128), f32),
            pltpu.VMEM((2, 8, 1, width), f32),
            pltpu.VMEM((rows, width), bf16),
            pltpu.VMEM((2 * mbs, rows, width), bf16),
            pltpu.VMEM((2 * mbs + 1, rows, width), bf16),
            pltpu.VMEM((mbs, rows, width), bf16),
            pltpu.VMEM((rows, width), bf16),
            pltpu.VMEM((32, piece, cols), bf16),
            pltpu.VMEM((8, feat_rows, feat), bf16),
            pltpu.VMEM((width, mbs * rows), bf16),
            pltpu.VMEM((mbs * rows, cols), f32),
            pltpu.VMEM((8, rows, feat), bf16),
            pltpu.VMEM((8, rows, feat), bf16),
            pltpu.VMEM((8, rows, feat), bf16),
            pltpu.VMEM((2, 16, piece, cols), f32),
            pltpu.VMEM((16, piece, cols), bf16),
            pltpu.VMEM((16, piece, cols), bf16),
            pltpu.VMEM((16, piece, cols), bf16),
            pltpu.VMEM((16, piece, cols), bf16),
            pltpu.VMEM((2, 16, piece, cols), bf16),
            dma,
            dma((129,)),
            dma((32,)),
            dma((32,)),
            dma((32,)),
            dma((8,)),
            dma((8,)),
            dma,
            dma,
            dma((mbs * 3,)),
            dma(((2 * mbs + 1) * 3,)),
            dma((2 * mbs * 3,)),
            dma((mbs,)),
            dma,
            dma((32,)),
            dma((32,)),
            dma((8,)),
            dma((8,)),
            dma,
            dma,
            dma((8,)),
            dma((8,)),
            dma((8,)),
            dma((8,)),
            dma,
            dma,
            dma((16,)),
            dma((16,)),
            dma((16,)),
            dma((16,)),
            dma((16,)),
            dma((16,)),
            dma((8,)),
            dma((8,)),
        ],
        compiler_params=pltpu.CompilerParams(
            collective_id=0, has_side_effects=True, vmem_limit_bytes=56 * 1024 * 1024
        ),
    )(
        noise,
        ids,
        sched,
        frequency,
        time_weight,
        block,
        block_mod,
        student_shard,
        feature_shard,
        student_mod,
        lin,
        token,
        table,
    )


def local(
    noise,
    sched_index,
    text_ids,
    text_table,
    time_weight,
    block_weight,
    block_mod,
    student_weight,
    student_mod,
    feature_weight,
    lin_weight,
    token_weight,
):
    batches, tokens, model_width = noise.shape
    sections = lax.axis_size(SECTION)
    own_section = lax.axis_index(SECTION)
    row_count = batches * tokens
    share_rows = row_count // sections
    vocab_rows = text_table.shape[0]
    offset = lax.axis_index(DP) * vocab_rows
    ids = lax.dynamic_index_in_dim(
        text_ids.reshape(16, 8, -1), own_section, 1, keepdims=False
    ) - offset
    indices_f = sched_index.astype(jnp.float32)
    half_freq = time_weight.shape[0] // 2
    frequency = jnp.exp(-math.log(10000.0) * jnp.arange(half_freq, dtype=jnp.float32) / half_freq)
    deltas = (indices_f[:, 1:] - indices_f[:, :-1]) / LEVELS
    sched = jnp.broadcast_to(
        jnp.stack([indices_f[:, :2].T.reshape(8), deltas.T.reshape(8)])[:, :, None], (2, 8, 128)
    )
    weight_share = lax.dynamic_slice_in_dim(token_weight, own_section * share_rows, share_rows, 0)
    teacher, token_distance, student_grad = run_train(
        noise.reshape(sections, share_rows, model_width),
        ids,
        sched,
        frequency[None, :],
        time_weight,
        block_weight[0],
        block_mod[0],
        student_weight,
        feature_weight,
        student_mod,
        lin_weight[None, :],
        weight_share[:, None],
        text_table,
    )
    return (
        teacher.reshape(noise.shape),
        student_grad.reshape(model_width, -1),
        token_distance.reshape(share_rows),
    )


def solution(mesh):
    torus = Mesh(mesh.devices.reshape(2, 8, 2, 4, 2), DP + SECTION)
    in_specs = (
        P(DP, None, None),
        P(DP, None),
        P(),
        P(DP, None),
        P(),
        P(SECTION, DP, None),
        P(SECTION, None, None),
        P(DP, SECTION),
        P(),
        P(SECTION, None),
        P(),
        P(DP),
    )
    out_specs = (P(DP, None, None), P(None, SECTION), P(DP + SECTION))
    return jax.shard_map(local, mesh=torus, in_specs=in_specs, out_specs=out_specs, check_vma=False)
```

time: 181 us -> 172 us (0.950)
  Pallas kernels: 169 us -> 160 us
  local copies, waits for them, and re-layouts: 6.6 us -> 9.01 us
    pallas_call x2 -> x1, Pallas kernels: 169 us -> 160 us  [run_train(): pl.pallas_call(train_kernel, out_shape=(jax.ShapeDtypeStruct((mbs, rows,...]
    unnamed x20 -> x11, local copies, waits for them, and re-layouts: 4.72 us -> 7.21 us
where the time goes in v4:
time: 172 us
  Pallas kernels  160 us (93%)
  local copies, waits for them, and re-layouts  9.01 us (5%)
  other arithmetic  1.89 us (1%)
    pallas_call x1, Pallas kernels, run_train(): pl.pallas_call(train_kernel, out_shape=(jax.ShapeDtypeStruct((mbs, rows,...  160 us
    unnamed x11, local copies, waits for them, and re-layouts  7.21 us

profile of v4, /device:TPU:1, one launch (start us, length us, event | category | flops | bytes accessed | tf_op | source)
XLA Modules:
  0.0 171.8 jit_solution(4090293720020957175)
XLA Ops:
  0.6 0.0 copy-start
  0.7 0.7 copy-done
  1.3 0.1 dynamic-slice_bitcast_fusion
  1.4 0.5 multiply_exponential_fusion.frequency_ref
  1.9 0.7 convert_element_type.3
  2.6 0.1 slice_bitcast_fusion
  2.7 0.1 copy.21
  2.8 0.1 stack_reshape.6
  2.9 0.1 copy.22
  2.9 0.1 stack_reshape.7
  3.0 0.7 broadcast_in_dim.6.sched_ref
  3.7 0.7 copy.23.token_ref
  4.4 1.3 copy.28
  5.7 0.9 copy.19
  6.6 0.6 subtract_bitcast_fusion.ids_ref
  7.2 160.2 %shard_map.139 = (bf16[8,32,1536]{2,1,0:T(8,128)(2,1)}, f32[1,32]{1,0:T(1,128)}, f32[2,16,48,192]{3,2,1,0:T(8,128)}) custom-call(bf16[8,32,1536]{2,1,0:T(8,128)(2,1)} %bitcast.20, s32[16,77]{1,0:T(8,128)} %subtract_bitcast_fusion.ids_ref, f32[2,8,128]{2,1,0:T(8,128)} %broadcast_in_dim.6.sched_ref, f32[1,128]{1,0:T(1,128)} %multiply_exponential_fusion.frequency_ref, ...), custom_call_target="tpu_custom_call" | custom-call | tf_op jit(solution)/shard_map/pallas_call | solution.py:731
  167.4 0.0 copy-start.1
  167.4 0.0 copy-start.2
  167.4 2.9 %copy.24 = f32[1536,192]{0,1:T(8,128)} copy(f32[1536,192]{1,0:T(8,128)} %bitcast.19) | data formatting | bytes 2359296
  170.4 0.0 copy-done.1
  170.4 0.9 copy.31
  171.2 0.0 copy-done.2
  171.2 0.5 copy.32
  (2 shorter events, 0.0 us)
Async XLA Ops:
  0.6 0.7 copy-start
  167.4 3.0 %copy-start.1 = (bf16[8,32,1536]{2,1,0:T(8,128)(2,1)S(1)}, bf16[8,32,1536]{2,1,0:T(8,128)(2,1)}, u32[]{:S(2)}) copy-start(bf16[8,32,1536]{2,1,0:T(8,128)(2,1)} %get-tuple-element.6) | copy-start | bytes 2359300
  167.4 3.8 %copy-start.2 = (f32[1,32]{1,0:T(1,128)S(1)}, f32[1,32]{1,0:T(1,128)}, u32[]{:S(2)}) copy-start(f32[1,32]{1,0:T(1,128)} %get-tuple-element.8) | copy-start | bytes 388

commit v5 on v4

--- a/solution.py
+++ b/solution.py
@@ -2,6 +2,7 @@
 
 import jax
 import jax.numpy as jnp
+import numpy as np
 from jax import lax
 from jax.experimental import pallas as pl
 from jax.experimental.pallas import tpu as pltpu
@@ -31,6 +32,7 @@
     teacher_ref,
     dist_ref,
     grad_ref,
+    ids,
     table,
     weight,
     mods,
@@ -46,8 +48,9 @@
     first_x,
     student_ref,
     feature_ref,
-    student_t,
+    student_rows,
     slope,
+    slope_t,
     feat_part,
     feats,
     grads,
@@ -180,11 +183,16 @@
     start(lend_mods, source)
 
     start(copy(block_ref, weight.at[dev], weight_send.at[dev * 4], weight_recv.at[dev], twin), relay)
-    go(piece_a(xl, zz), 2, source)
-    go(piece_a(xl, zz), 3, source)
-
-    sched[core] = sched_ref[...]
-    start(copy(sched_ref, sched.at[core], sched_send, sched_recv, twin))
+    for towards in (2, 3, 0, 1):
+        go(piece_a(xl, zz), towards, source)
+
+    levels = [
+        jnp.broadcast_to(sched_ref[:, r : r + 1].astype(jnp.float32), (4, 128)) for r in range(3)
+    ]
+    for r in range(2):
+        sched[core, 0, 4 * r : 4 * r + 4] = levels[r]
+        sched[core, 1, 4 * r : 4 * r + 4] = (levels[r + 1] - levels[r]) / LEVELS
+    start(copy(sched.at[core], sched.at[core], sched_send, sched_recv, twin))
     first_chip = sy == 0
     first_stage = first_chip & (core == 0)
     lender = first_chip & (core == 1) & (sx == 1)
@@ -228,16 +236,36 @@
     go(piece_b(xl, zz), 2, source)
     go(piece_b(xl, zz), 3, source)
 
+    arrive_a = piece_a(1 - xl, zz)
+    arrive(arrive_a)
+    go(arrive_a, 2, relay)
+
+    go(arrive_a, 0)
+    go(arrive_a, 1)
+
+    @pl.when(relay)
+    def _():
+        arrive(piece_a(xl, zz))
+
+    go(piece_a(xl, zz), 0, relay)
+    go(piece_a(xl, zz), 1, relay)
+
     vocab = table.shape[0]
-    local_ids = ids_ref[...]
-    lanes = lax.broadcasted_iota(jnp.int32, (local_ids.shape[0], vocab), 1)
+    text_len, samples = ids_ref.shape
+    ids[...] = jnp.zeros_like(ids)
+    ids[0:text_len] = ids_ref[...].astype(jnp.float32)
+    by_sample = ids[...].T.reshape(samples // 8, 8, -1)
+    place = lax.broadcasted_iota(jnp.int32, by_sample.shape, 1)
+    own_ids = jnp.sum(jnp.where(place == sec, by_sample, 0.0), axis=1)
+    local_ids = own_ids.astype(jnp.int32) - dev * vocab
+    lanes = lax.broadcasted_iota(jnp.int32, (samples // 8, vocab), 1)
     counts = jnp.zeros(lanes.shape, jnp.float32)
-    for t in range(local_ids.shape[1]):
+    for t in range(text_len):
         counts = counts + jnp.where(local_ids[:, t : t + 1] == lanes, 1.0, 0.0)
     load_table.wait()
     part = jnp.dot(
         counts.astype(jnp.bfloat16), table[...], preferred_element_type=jnp.float32
-    ) / local_ids.shape[1]
+    ) / text_len
     for g in range(16):
         rows_out[g] = part[g : g + 1]
     rows_in[dev] = rows_out[dev // 2]
@@ -252,18 +280,6 @@
                 at_dp(other),
             )
         )
-
-    arrive_a = piece_a(1 - xl, zz)
-    arrive(arrive_a)
-    go(arrive_a, 2, relay)
-
-    @pl.when(relay)
-    def _():
-        arrive(piece_a(xl, zz))
-
-    for a in range(2):
-        go(piece_a(a, zz), 0)
-        go(piece_a(a, zz), 1)
 
     def take_x(z):
         p = piece_b(1 - xl, z)
@@ -331,7 +347,7 @@
             )
         )
     ring_step(2)
-    copy(sched_ref, sched.at[1 - core], sched_send, sched_recv, twin).wait_recv()
+    copy(sched.at[core], sched.at[1 - core], sched_send, sched_recv, twin).wait_recv()
     for k in range(1, 8):
         other = (sec + k) % 8
         copy(
@@ -445,10 +461,10 @@
             mean_sq = jnp.mean(hidden * hidden, axis=-1, keepdims=True)
             cond_row = cond[sx, p * 4 + j // 2]
             inputs = (
-                hidden * lax.rsqrt(mean_sq + 1e-06) * (1.0 + cond_row * mods[0:1])
-                + cond_row * mods[1:2]
+                hidden * lax.rsqrt(mean_sq + 1e-06) * (1.0 + cond_row * mods[0])
+                + cond_row * mods[1]
             ).astype(jnp.bfloat16)
-            gate = 1.0 + cond_row * mods[2:3]
+            gate = 1.0 + cond_row * mods[2]
             for c in range(chunks):
                 cols = slice(c * chunk, (c + 1) * chunk)
                 mixed = jnp.dot(
@@ -509,7 +525,7 @@
         z = own_cols(latents)
         moved = z - level * (z + gate * (mixed * half))
         slope[2 * n * rows : 2 * (n + 1) * rows] = -level * gate * bend
-        student_t[:, 2 * n * rows : 2 * (n + 1) * rows] = student_in.T
+        student_rows[2 * n * rows : 2 * (n + 1) * rows] = student_in
         feat_part[2 * n : 2 * n + 2] = (
             jnp.dot(
                 moved.astype(jnp.bfloat16),
@@ -519,6 +535,8 @@
             .astype(jnp.bfloat16)
             .reshape(2, rows, -1)
         )
+
+    slope_t[...] = slope[...].T
 
     def send_feat(k, slot):
         return copy(
@@ -612,7 +630,16 @@
         preferred_element_type=jnp.float32,
         precision=lax.Precision.HIGHEST,
     )
-    unit_grad = 2.0 * token_ref[...] * lin * gap
+    tokens = token_ref.shape[1]
+    own_token = lax.broadcasted_iota(jnp.int32, (rows, tokens), 0) + sec * rows
+    token_col = jnp.sum(
+        jnp.where(
+            lax.broadcasted_iota(jnp.int32, (rows, tokens), 1) == own_token, token_ref[...], 0.0
+        ),
+        axis=1,
+        keepdims=True,
+    )
+    unit_grad = 2.0 * token_col * lin * gap
     mean_dot = jnp.mean(unit_grad * unit_s, axis=-1, keepdims=True)
     feat_grad = scale_s * (unit_grad - unit_s * mean_dot)
     grads[sec] = jnp.where(feat_student > 0.0, feat_grad, 0.0).astype(jnp.bfloat16)
@@ -623,20 +650,21 @@
         send_grad(other, other).wait_recv()
 
     out_grad = lax.dot_general(
+        feature_ref[sec],
         grads[...].reshape(sections * rows, feat),
-        feature_ref[sec],
         (((1,), (1,)), ((), ())),
         preferred_element_type=jnp.float32,
     )
-    mixed_grad = (out_grad * slope[...]).astype(jnp.bfloat16)
-    half_rows = width // 2
+    mixed_grad = (out_grad * slope_t[...]).astype(jnp.bfloat16)
+    product = jnp.dot(mixed_grad, student_rows[...], preferred_element_type=jnp.float32)
+    lanes = 128
+    blocks = width // lanes
+    half_cols = product.shape[0] // 2
     for half in range(2):
-        partial[half] = lax.dot_general(
-            student_t[half * half_rows : (half + 1) * half_rows],
-            mixed_grad,
-            (((1,), (0,)), ((), ())),
-            preferred_element_type=jnp.float32,
-        ).reshape(chips, piece, -1)
+        kept = product[half * half_cols : (half + 1) * half_cols]
+        partial[half] = jnp.concatenate(
+            [kept[:, b * lanes : (b + 1) * lanes] for b in range(blocks)], axis=0
+        ).reshape(chips, piece, lanes)
     half_out[...] = partial[1 - core].astype(jnp.bfloat16)
     send_half.start()
     for k in range(1, sections):
@@ -654,16 +682,19 @@
     for k in range(1, chips):
         send_final((chip + k) % chips, chip).start()
     send_twin(core, chip).start()
-    grad_ref[core, chip] = final[core, chip].astype(jnp.float32)
     for k in range(1, chips):
         other = (chip + chips - k) % chips
         send_final(other, other).wait_recv()
         send_twin(core, other).start()
-        grad_ref[core, other] = final[core, other].astype(jnp.float32)
     for k in range(chips):
         other = (chip + chips - k) % chips
         send_twin(1 - core, other).wait_recv()
-        grad_ref[1 - core, other] = final[1 - core, other].astype(jnp.float32)
+    for half in range(2):
+        kept = final[half].astype(jnp.float32).reshape(blocks * half_cols, lanes)
+        for b in range(blocks):
+            grad_ref[half * half_cols : (half + 1) * half_cols, b * lanes : (b + 1) * lanes] = kept[
+                b * half_cols : (b + 1) * half_cols
+            ]
 
     for k in range(1, sections):
         other = (sec + k) % sections
@@ -724,6 +755,7 @@
     piece = block.shape[0]
     cols = student_shard.shape[1]
     feat_rows, feat = feature_shard.shape
+    part = cols * width // (32 * 128)
     vmem = pl.BlockSpec(memory_space=pltpu.VMEM)
     dma = pltpu.SemaphoreType.DMA
     bf16 = jnp.bfloat16
@@ -733,14 +765,15 @@
         out_shape=(
             jax.ShapeDtypeStruct((mbs, rows, width), bf16),
             jax.ShapeDtypeStruct((1, rows), f32),
-            jax.ShapeDtypeStruct((2, 16, piece, cols), f32),
+            jax.ShapeDtypeStruct((cols, width), f32),
         ),
         in_specs=[vmem] * 12 + [pl.BlockSpec(memory_space=pl.ANY)],
         out_specs=(vmem,) * 3,
         scratch_shapes=[
+            pltpu.VMEM((128, ids.shape[1]), f32),
             pltpu.VMEM((vocab, width), bf16),
             pltpu.VMEM((32, piece, width), bf16),
-            pltpu.VMEM((3, width), f32),
+            pltpu.VMEM((3, 1, width), f32),
             pltpu.VMEM((16, 1, width), f32),
             pltpu.VMEM((32, 1, width), f32),
             pltpu.VMEM((8, 1, width), f32),
@@ -753,17 +786,18 @@
             pltpu.VMEM((rows, width), bf16),
             pltpu.VMEM((32, piece, cols), bf16),
             pltpu.VMEM((8, feat_rows, feat), bf16),
-            pltpu.VMEM((width, mbs * rows), bf16),
+            pltpu.VMEM((mbs * rows, width), bf16),
             pltpu.VMEM((mbs * rows, cols), f32),
+            pltpu.VMEM((cols, mbs * rows), f32),
             pltpu.VMEM((8, rows, feat), bf16),
             pltpu.VMEM((8, rows, feat), bf16),
             pltpu.VMEM((8, rows, feat), bf16),
-            pltpu.VMEM((2, 16, piece, cols), f32),
-            pltpu.VMEM((16, piece, cols), bf16),
-            pltpu.VMEM((16, piece, cols), bf16),
-            pltpu.VMEM((16, piece, cols), bf16),
-            pltpu.VMEM((16, piece, cols), bf16),
-            pltpu.VMEM((2, 16, piece, cols), bf16),
+            pltpu.VMEM((2, 16, part, 128), f32),
+            pltpu.VMEM((16, part, 128), bf16),
+            pltpu.VMEM((16, part, 128), bf16),
+            pltpu.VMEM((16, part, 128), bf16),
+            pltpu.VMEM((16, part, 128), bf16),
+            pltpu.VMEM((2, 16, part, 128), bf16),
             dma,
             dma((129,)),
             dma((32,)),
@@ -835,40 +869,28 @@
 ):
     batches, tokens, model_width = noise.shape
     sections = lax.axis_size(SECTION)
-    own_section = lax.axis_index(SECTION)
     row_count = batches * tokens
     share_rows = row_count // sections
-    vocab_rows = text_table.shape[0]
-    offset = lax.axis_index(DP) * vocab_rows
-    ids = lax.dynamic_index_in_dim(
-        text_ids.reshape(16, 8, -1), own_section, 1, keepdims=False
-    ) - offset
-    indices_f = sched_index.astype(jnp.float32)
     half_freq = time_weight.shape[0] // 2
-    frequency = jnp.exp(-math.log(10000.0) * jnp.arange(half_freq, dtype=jnp.float32) / half_freq)
-    deltas = (indices_f[:, 1:] - indices_f[:, :-1]) / LEVELS
-    sched = jnp.broadcast_to(
-        jnp.stack([indices_f[:, :2].T.reshape(8), deltas.T.reshape(8)])[:, :, None], (2, 8, 128)
-    )
-    weight_share = lax.dynamic_slice_in_dim(token_weight, own_section * share_rows, share_rows, 0)
+    frequency = np.exp(-math.log(10000.0) * np.arange(half_freq, dtype=np.float32) / half_freq)
     teacher, token_distance, student_grad = run_train(
         noise.reshape(sections, share_rows, model_width),
-        ids,
-        sched,
-        frequency[None, :],
+        text_ids.T,
+        sched_index,
+        jnp.asarray(frequency[None, :], jnp.float32),
         time_weight,
         block_weight[0],
-        block_mod[0],
+        jnp.moveaxis(block_mod, 0, 1),
         student_weight,
         feature_weight,
         student_mod,
         lin_weight[None, :],
-        weight_share[:, None],
+        token_weight[None, :],
         text_table,
     )
     return (
         teacher.reshape(noise.shape),
-        student_grad.reshape(model_width, -1),
+        student_grad.T,
         token_distance.reshape(share_rows),
     )
 

time: 172 us -> 160 us (0.930)
  local copies, waits for them, and re-layouts: 9.01 us -> 3.69 us
  Pallas kernels: 160 us -> 155 us
  other arithmetic: 1.89 us -> 0 us
    pallas_call x1, Pallas kernels: 160 us -> 155 us  [run_train(): pl.pallas_call(train_kernel, out_shape=(jax.ShapeDtypeStruct((mbs, rows,...]
    unnamed x11 -> x7, local copies, waits for them, and re-layouts: 7.21 us -> 3.69 us
where the time goes in v5:
time: 160 us; the launch traced here: 159 us
  Pallas kernels  155 us (97%)
  local copies, waits for them, and re-layouts  3.69 us (2%)
    pallas_call x1, Pallas kernels, run_train(): pl.pallas_call(train_kernel, out_shape=(jax.ShapeDtypeStruct((mbs, rows,...  155 us
    unnamed x7, local copies, waits for them, and re-layouts  3.69 us

profile of v5, /device:TPU:1, one launch (start us, length us, event | category | flops | bytes accessed | tf_op | source)
XLA Modules:
  0.0 158.9 jit_solution(16300801080451936671)
XLA Ops:
  0.6 154.6 %shard_map.148 = (bf16[8,32,1536]{2,1,0:T(8,128)(2,1)}, f32[1,32]{1,0:T(1,128)}, f32[192,1536]{1,0:T(8,128)}) custom-call(bf16[8,32,1536]{2,1,0:T(8,128)(2,1)} %bitcast.10, s32[77,128]{1,0:T(8,128)} %bitcast.13, s32[4,3]{1,0:T(4,128)} %sched_ref.1, f32[1,128]{1,0:T(1,128)} %constant.2.clone.frequency_ref, bf16[256,1536]{1,0:T(8,128)(2,1)} %time_weight_ref.1, ...), custom_call_target="tpu_custom_call" | custom-call | tf_op jit(solution)/shard_map/pallas_call | solution.py:763
  155.2 0.0 copy-start
  155.2 2.2 %copy.19 = bf16[4,64,1536]{2,1,0:T(8,128)(2,1)} copy(bf16[4,64,1536]{2,1,0:T(8,128)(2,1)} %bitcast.11) | data formatting | bytes 1572864
  157.4 0.0 copy-done
  157.4 0.0 copy-start.1
  157.4 1.0 copy.20
  158.4 0.0 copy-done.1
  158.4 0.5 copy.21
Async XLA Ops:
  155.2 2.2 %copy-start = (f32[192,1536]{1,0:T(8,128)S(1)}, f32[192,1536]{1,0:T(8,128)}, u32[]{:S(2)}) copy-start(f32[192,1536]{1,0:T(8,128)} %get-tuple-element.7) | copy-start | bytes 3538948
  157.4 1.0 copy-start.1

commit v6 on v5

--- a/solution.py
+++ b/solution.py
@@ -67,9 +67,8 @@
     row_recv,
     pooled_send,
     pooled_recv,
-    sched_send,
-    sched_recv,
-    noise_send,
+    lend_send,
+    lend_recv,
     inbox_recv,
     sent_send,
     first_send,
@@ -164,56 +163,48 @@
     way = {0: z_up, 1: z_down, 2: x_mate, 3: x_outer}
 
     def go(p, towards, when=None):
-        block = weight.at[p]
+        block = weight.at[core, p]
         start(
             copy(block, block, weight_send.at[p * 4 + towards], weight_recv.at[p], way[towards]),
             when,
         )
 
-    def arrive(p):
-        block = weight.at[p]
-        copy(block, block, weight_send.at[p], weight_recv.at[p], twin).wait_recv()
+    def lend(p, when=None):
+        block = weight.at[core, p]
+        start(copy(block, block, lend_send.at[p], lend_recv.at[p], twin), when)
+
+    def arrive(p, when=None):
+        block = weight.at[core, p]
+        landed = copy(block, block, weight_send.at[p], weight_recv.at[p], twin)
+        if when is None:
+            landed.wait_recv()
+        else:
+            pl.when(when)(landed.wait_recv)
+        lend(p, when)
+
+    mods[sx] = block_mod_ref[...]
+    lend_mods = copy(block_mod_ref, mods.at[sx], mods_send, mods_recv, x_outer)
+    start(lend_mods)
 
     @pl.when(source)
     def _():
-        weight[dev] = block_ref[...]
-        mods[...] = block_mod_ref[...]
-
-    lend_mods = copy(block_mod_ref, mods, mods_send, mods_recv, x_outer)
-    start(lend_mods, source)
-
-    start(copy(block_ref, weight.at[dev], weight_send.at[dev * 4], weight_recv.at[dev], twin), relay)
+        weight[core, dev] = block_ref[...]
+
+    own_shard = copy(
+        block_ref, weight.at[1 - core, dev], weight_send.at[128], weight_recv.at[dev], twin
+    )
+    start(own_shard, relay)
     for towards in (2, 3, 0, 1):
         go(piece_a(xl, zz), towards, source)
+    lend(piece_a(xl, zz), source)
 
     levels = [
         jnp.broadcast_to(sched_ref[:, r : r + 1].astype(jnp.float32), (4, 128)) for r in range(3)
     ]
     for r in range(2):
-        sched[core, 0, 4 * r : 4 * r + 4] = levels[r]
-        sched[core, 1, 4 * r : 4 * r + 4] = (levels[r + 1] - levels[r]) / LEVELS
-    start(copy(sched.at[core], sched.at[core], sched_send, sched_recv, twin))
-    first_chip = sy == 0
-    first_stage = first_chip & (core == 0)
-    lender = first_chip & (core == 1) & (sx == 1)
-
-    for j in range(mbs):
-        for c in range(chunks):
-            cols = slice(c * chunk, (c + 1) * chunk)
-            start(
-                copy(
-                    noise_ref.at[j, :, cols],
-                    inbox.at[j, :, cols],
-                    noise_send.at[j * chunks + c],
-                    inbox_recv.at[j * chunks + c],
-                    twin,
-                ),
-                lender,
-            )
-
-    @pl.when(first_stage & (sx == 0))
-    def _():
-        inbox[0:mbs] = noise_ref[...]
+        sched[0, 4 * r : 4 * r + 4] = levels[r]
+        sched[1, 4 * r : 4 * r + 4] = (levels[r + 1] - levels[r]) / LEVELS
+    first_stage = sy == 0
 
     for k in range(1, 4):
         start(
@@ -227,9 +218,7 @@
         )
     feature_ref[sec] = feature_shard_ref[...]
 
-    @pl.when(source)
-    def _():
-        arrive(piece_b(xl, zz))
+    arrive(piece_b(xl, zz), source)
 
     go(piece_b(xl, zz), 0, source)
     go(piece_b(xl, zz), 1, source)
@@ -243,9 +232,7 @@
     go(arrive_a, 0)
     go(arrive_a, 1)
 
-    @pl.when(relay)
-    def _():
-        arrive(piece_a(xl, zz))
+    arrive(piece_a(xl, zz), relay)
 
     go(piece_a(xl, zz), 0, relay)
     go(piece_a(xl, zz), 1, relay)
@@ -294,9 +281,7 @@
         last = k == 4
         here = source & (xl == (0 if up else 1)) if last else source
 
-        @pl.when(here)
-        def _():
-            arrive(p)
+        arrive(p, here)
 
         if k < 3:
             go(p, 0 if up else 1, here)
@@ -347,7 +332,6 @@
             )
         )
     ring_step(2)
-    copy(sched.at[core], sched.at[1 - core], sched_send, sched_recv, twin).wait_recv()
     for k in range(1, 8):
         other = (sec + k) % 8
         copy(
@@ -357,22 +341,19 @@
             pooled_recv.at[other],
             at_section(other),
         ).wait_recv()
-    for c in range(2):
-        angles = sched[c, 0] * frequency_ref[...]
-        embedding = jnp.concatenate([jnp.cos(angles), jnp.sin(angles)], axis=-1)
-        embed = jnp.dot(
-            embedding.astype(jnp.bfloat16), time_weight_ref[...], preferred_element_type=jnp.float32
-        )
-        for r in range(8):
-            cond[c, r] = jax.nn.silu(embed[r : r + 1] + pooled[c * 4 + r % 4])
+    angles = sched[0] * frequency_ref[...]
+    embedding = jnp.concatenate([jnp.cos(angles), jnp.sin(angles)], axis=-1)
+    embed = jnp.dot(
+        embedding.astype(jnp.bfloat16), time_weight_ref[...], preferred_element_type=jnp.float32
+    )
+    for r in range(8):
+        cond[r] = jax.nn.silu(embed[r : r + 1] + pooled[core * 4 + r % 4])
     ring_step(3)
     ring_step(4)
     take_x(zz + 4)
 
-    @pl.when(relay)
-    def _():
-        for z in range(8):
-            arrive(piece_b(xl, z))
+    for z in range(8):
+        arrive(piece_b(xl, z), relay)
 
     student_ref[dev] = student_shard_ref[...]
     for k in range(1, 16):
@@ -385,7 +366,10 @@
                 at_dp((dev + 2 * k) % 32),
             )
         )
-    pl.when(relay)(lend_mods.wait_recv)
+    copy(block_mod_ref, mods.at[1 - sx], mods_send, mods_recv, x_outer).wait_recv()
+    for p in range(32):
+        block = weight.at[1 - core, p]
+        copy(block, block, lend_send.at[p], lend_recv.at[p], twin).wait_recv()
 
     def pass_on(t, slot, c, where):
         cols = pl.ds(c * chunk, chunk)
@@ -397,54 +381,61 @@
             where,
         )
 
+    here = mbs // 2
+
     def hop(t, p, j, c):
-        @pl.when(core == 0)
+        @pl.when(sy < 3)
         def _():
-            pass_on(t, t, c, twin).start()
-
-        @pl.when((core == 1) & (sy < 3))
-        def _():
-            pass_on(t, t, c, {"dp_c": 0, "sec_y": (sy + 1) % 4}).start()
-
-        @pl.when((core == 1) & (sy == 3))
+            pass_on(t, t, c, {"sec_y": (sy + 1) % 4}).start()
+
+        @pl.when(sy == 3)
         def _():
             if p == 0:
-                pass_on(t, t + mbs, c, {"dp_c": 0, "sec_y": 0}).start()
+                pass_on(t, t + here, c, {"sec_y": 0}).start()
             else:
 
-                @pl.when((sx == 1) & (j == mbs - 1))
+                @pl.when((sx == 1) & (j == here - 1))
                 def _():
                     cols = slice(c * chunk, (c + 1) * chunk)
-                    inbox[2 * mbs, :, cols] = sent[t, :, cols]
-
-                @pl.when((sx == 0) | (j < mbs - 1))
+                    inbox[2 * here, :, cols] = sent[t, :, cols]
+
+                @pl.when((sx == 0) | (j < here - 1))
                 def _():
-                    pass_on(t, 2 * mbs, c, {**at_section(j), "dp_c": sx}).start()
+                    pass_on(t, 2 * here, c, at_section(sx * here + j)).start()
 
     def share_first(j):
         return copy(
-            start_x.at[j], first_x, first_send.at[j], first_recv, {**at_section(j), "dp_c": sx}
+            start_x.at[j], first_x, first_send.at[j], first_recv, at_section(sx * here + j)
         )
 
     def run_pass(p):
         def step(j, carry):
-            t = p * mbs + j
-            waited = jnp.logical_not(first_stage & (sx == 0)) if p == 0 else None
+            t = p * here + j
+            sample = (sx * here + j) // 2
             for c in range(chunks):
                 arrived = pass_on(t, t, c, twin)
                 if p == 0:
-                    pl.when(waited)(arrived.wait_recv)
+                    pl.when(sy > 0)(arrived.wait_recv)
                 else:
                     arrived.wait_recv()
-            held[...] = inbox[t]
-
-            if p > 0:
+            if p == 0:
+
+                @pl.when(first_stage)
+                def _():
+                    held[...] = noise_ref[sx * here + j]
+
+                @pl.when(sy > 0)
+                def _():
+                    held[...] = inbox[t]
+
+            else:
+                held[...] = inbox[t]
 
                 @pl.when(first_stage)
                 def _():
                     moved = (
-                        inbox[j].astype(jnp.float32)
-                        + sched[sx, 1, pl.ds(j // 2, 1), :1] * held[...].astype(jnp.float32)
+                        noise_ref[sx * here + j].astype(jnp.float32)
+                        + sched[1, pl.ds(sample, 1), :1] * held[...].astype(jnp.float32)
                     ).astype(jnp.bfloat16)
                     held[...] = moved
                     start_x[j] = moved
@@ -457,29 +448,34 @@
                     def _():
                         share_first(j).start()
 
-            hidden = held[...].astype(jnp.float32)
-            mean_sq = jnp.mean(hidden * hidden, axis=-1, keepdims=True)
-            cond_row = cond[sx, p * 4 + j // 2]
-            inputs = (
-                hidden * lax.rsqrt(mean_sq + 1e-06) * (1.0 + cond_row * mods[0])
-                + cond_row * mods[1]
-            ).astype(jnp.bfloat16)
-            gate = 1.0 + cond_row * mods[2]
-            for c in range(chunks):
-                cols = slice(c * chunk, (c + 1) * chunk)
-                mixed = jnp.dot(
-                    inputs,
-                    weight[:, :, cols].reshape(width, chunk),
-                    preferred_element_type=jnp.float32,
-                )
-                sent[t, :, cols] = (
-                    hidden[:, cols] + gate[:, cols] * jax.nn.gelu(mixed)
+            cond_row = cond[p * 4 + sample]
+            for b in range(2):
+                hidden = held[...].astype(jnp.float32)
+                mean_sq = jnp.mean(hidden * hidden, axis=-1, keepdims=True)
+                inputs = (
+                    hidden * lax.rsqrt(mean_sq + 1e-06) * (1.0 + cond_row * mods[b, 0])
+                    + cond_row * mods[b, 1]
                 ).astype(jnp.bfloat16)
-                hop(t, p, j, c)
+                gate = 1.0 + cond_row * mods[b, 2]
+                for c in range(chunks):
+                    cols = slice(c * chunk, (c + 1) * chunk)
+                    mixed = jnp.dot(
+                        inputs,
+                        weight[b, :, :, cols].reshape(width, chunk),
+                        preferred_element_type=jnp.float32,
+                    )
+                    result = (hidden[:, cols] + gate[:, cols] * jax.nn.gelu(mixed)).astype(
+                        jnp.bfloat16
+                    )
+                    if b == 0:
+                        held[:, cols] = result
+                    else:
+                        sent[t, :, cols] = result
+                        hop(t, p, j, c)
 
             return carry
 
-        lax.fori_loop(0, mbs, step, 0)
+        lax.fori_loop(0, here, step, 0)
 
     run_pass(0)
     for k in range(16):
@@ -505,7 +501,7 @@
     for n in range(4):
         latents = noise_ref[2 * n : 2 * n + 2].reshape(2 * rows, width).astype(jnp.float32)
         mean_sq = jnp.mean(latents * latents, axis=-1, keepdims=True)
-        cond_row = cond[core, n]
+        cond_row = cond[n]
         student_in = (
             latents * lax.rsqrt(mean_sq + 1e-06) * (1.0 + cond_row * student_mod_ref[0:1])
             + cond_row * student_mod_ref[1:2]
@@ -521,7 +517,7 @@
             1.0 + 3.0 * 0.044715 * mixed * mixed
         )
         gate = own_cols(1.0 + cond_row * student_mod_ref[2:3])
-        level = sched[core, 0, n : n + 1, :1] / LEVELS
+        level = sched[0, n : n + 1, :1] / LEVELS
         z = own_cols(latents)
         moved = z - level * (z + gate * (mixed * half))
         slope[2 * n * rows : 2 * (n + 1) * rows] = -level * gate * bend
@@ -557,11 +553,11 @@
 
     run_pass(1)
 
-    last_self = (core == 1) & (sec == 7)
-    first_self = (core == 0) & (sec == 0)
+    last_self = sec == 7
+    first_self = sec == 0
 
     for c in range(chunks):
-        pl.when(jnp.logical_not(last_self))(pass_on(0, 2 * mbs, c, twin).wait_recv)
+        pl.when(jnp.logical_not(last_self))(pass_on(0, 2 * here, c, twin).wait_recv)
 
     @pl.when(jnp.logical_not(first_self))
     def _():
@@ -569,7 +565,7 @@
 
     x2 = (
         first_x[...].astype(jnp.float32)
-        + sched[core, 1, pl.ds(4 + sec // 2, 1), :1] * inbox[2 * mbs].astype(jnp.float32)
+        + sched[1, pl.ds(4 + sec // 2, 1), :1] * inbox[2 * here].astype(jnp.float32)
     ).astype(jnp.bfloat16)
     teacher_ref[sec] = x2
     for k in range(4):
@@ -714,14 +710,14 @@
             pass_on(t, t, c, twin).wait_send()
         return carry
 
-    lax.fori_loop(0, 2 * mbs - 1, drain, 0)
+    lax.fori_loop(0, 2 * here - 1, drain, 0)
 
     for c in range(chunks):
-        pl.when(jnp.logical_not(last_self))(pass_on(2 * mbs - 1, 0, c, twin).wait_send)
+        pl.when(jnp.logical_not(last_self))(pass_on(2 * here - 1, 0, c, twin).wait_send)
 
     @pl.when(first_stage)
     def _():
-        for j in range(1, mbs):
+        for j in range(1, here):
             share_first(j).wait_send()
 
         @pl.when(sx > 0)
@@ -772,17 +768,17 @@
         scratch_shapes=[
             pltpu.VMEM((128, ids.shape[1]), f32),
             pltpu.VMEM((vocab, width), bf16),
-            pltpu.VMEM((32, piece, width), bf16),
-            pltpu.VMEM((3, 1, width), f32),
+            pltpu.VMEM((2, 32, piece, width), bf16),
+            pltpu.VMEM((2, 3, 1, width), f32),
             pltpu.VMEM((16, 1, width), f32),
             pltpu.VMEM((32, 1, width), f32),
             pltpu.VMEM((8, 1, width), f32),
-            pltpu.VMEM((2, 2, 8, 128), f32),
-            pltpu.VMEM((2, 8, 1, width), f32),
+            pltpu.VMEM((2, 8, 128), f32),
+            pltpu.VMEM((8, 1, width), f32),
             pltpu.VMEM((rows, width), bf16),
-            pltpu.VMEM((2 * mbs, rows, width), bf16),
-            pltpu.VMEM((2 * mbs + 1, rows, width), bf16),
             pltpu.VMEM((mbs, rows, width), bf16),
+            pltpu.VMEM((mbs + 1, rows, width), bf16),
+            pltpu.VMEM((mbs // 2, rows, width), bf16),
             pltpu.VMEM((rows, width), bf16),
             pltpu.VMEM((32, piece, cols), bf16),
             pltpu.VMEM((8, feat_rows, feat), bf16),
@@ -805,12 +801,11 @@
             dma((32,)),
             dma((8,)),
             dma((8,)),
-            dma,
-            dma,
+            dma((32,)),
+            dma((32,)),
+            dma(((mbs + 1) * 3,)),
             dma((mbs * 3,)),
-            dma(((2 * mbs + 1) * 3,)),
-            dma((2 * mbs * 3,)),
-            dma((mbs,)),
+            dma((mbs // 2,)),
             dma,
             dma((32,)),
             dma((32,)),

time: 160 us -> 156 us (0.975)
  Pallas kernels: 155 us -> 151 us
    pallas_call x1, Pallas kernels: 155 us -> 151 us  [run_train(): pl.pallas_call(train_kernel, out_shape=(jax.ShapeDtypeStruct((mbs, rows,...]
where the time goes in v6:
time: 156 us; the launch traced here: 155 us
  Pallas kernels  151 us (97%)
  local copies, waits for them, and re-layouts  3.69 us (2%)
    pallas_call x1, Pallas kernels, run_train(): pl.pallas_call(train_kernel, out_shape=(jax.ShapeDtypeStruct((mbs, rows,...  151 us
    unnamed x7, local copies, waits for them, and re-layouts  3.69 us

profile of v6, /device:TPU:1, one launch (start us, length us, event | category | flops | bytes accessed | tf_op | source)
XLA Modules:
  0.0 154.9 jit_solution(9830843624001492398)
XLA Ops:
  0.6 150.6 %shard_map.148 = (bf16[8,32,1536]{2,1,0:T(8,128)(2,1)}, f32[1,32]{1,0:T(1,128)}, f32[192,1536]{1,0:T(8,128)}) custom-call(bf16[8,32,1536]{2,1,0:T(8,128)(2,1)} %bitcast.10, s32[77,128]{1,0:T(8,128)} %bitcast.13, s32[4,3]{1,0:T(4,128)} %sched_ref.1, f32[1,128]{1,0:T(1,128)} %constant.2.clone.frequency_ref, bf16[256,1536]{1,0:T(8,128)(2,1)} %time_weight_ref.1, ...), custom_call_target="tpu_custom_call" | custom-call | tf_op jit(solution)/shard_map/pallas_call | solution.py:759
  151.2 0.0 copy-start
  151.2 2.2 %copy.19 = bf16[4,64,1536]{2,1,0:T(8,128)(2,1)} copy(bf16[4,64,1536]{2,1,0:T(8,128)(2,1)} %bitcast.11) | data formatting | bytes 1572864
  153.4 0.0 copy-done
  153.4 0.0 copy-start.1
  153.4 1.0 copy.20
  154.4 0.0 copy-done.1
  154.4 0.5 copy.21
Async XLA Ops:
  151.2 2.2 %copy-start = (f32[192,1536]{1,0:T(8,128)S(1)}, f32[192,1536]{1,0:T(8,128)}, u32[]{:S(2)}) copy-start(f32[192,1536]{1,0:T(8,128)} %get-tuple-element.7) | copy-start | bytes 3538948
  153.4 1.0 copy-start.1

commit v7 on v6

--- a/solution.py
+++ b/solution.py
@@ -121,12 +121,22 @@
         pl.semaphore_signal(barrier, inc=1, device_id=where, device_id_type=MESH)
 
     for k in range(1, 8):
-        for dc in range(2):
-            greet({**at_section((sec + k) % 8), "dp_c": (core + dc) % 2})
+        greet(at_section((sec + k) % 8))
     for k in range(1, 32):
         greet(at_dp((dev + k) % 32))
     greet({"sec_x": 1 - sx, "dp_x": 1 - xl})
-    pl.semaphore_wait(barrier, 46)
+    levels = [
+        jnp.broadcast_to(sched_ref[:, r : r + 1].astype(jnp.float32), (4, 128)) for r in range(3)
+    ]
+    for r in range(2):
+        sched[0, 4 * r : 4 * r + 4] = levels[r]
+        sched[1, 4 * r : 4 * r + 4] = (levels[r + 1] - levels[r]) / LEVELS
+    angles = sched[0] * frequency_ref[...]
+    embedding = jnp.concatenate([jnp.cos(angles), jnp.sin(angles)], axis=-1)
+    embed = jnp.dot(
+        embedding.astype(jnp.bfloat16), time_weight_ref[...], preferred_element_type=jnp.float32
+    )
+    pl.semaphore_wait(barrier, 39)
 
     def copy(src, dst, send, recv, where):
         return pltpu.make_async_remote_copy(
@@ -198,12 +208,6 @@
         go(piece_a(xl, zz), towards, source)
     lend(piece_a(xl, zz), source)
 
-    levels = [
-        jnp.broadcast_to(sched_ref[:, r : r + 1].astype(jnp.float32), (4, 128)) for r in range(3)
-    ]
-    for r in range(2):
-        sched[0, 4 * r : 4 * r + 4] = levels[r]
-        sched[1, 4 * r : 4 * r + 4] = (levels[r + 1] - levels[r]) / LEVELS
     first_stage = sy == 0
 
     for k in range(1, 4):
@@ -313,6 +317,7 @@
 
     ring_step(1)
 
+    ring_step(2)
     total = rows_in[dev]
     for k in range(1, 32):
         other = (dev + 32 - k) % 32
@@ -331,7 +336,8 @@
                 at_section((sec + k) % 8),
             )
         )
-    ring_step(2)
+    ring_step(3)
+    ring_step(4)
     for k in range(1, 8):
         other = (sec + k) % 8
         copy(
@@ -341,15 +347,8 @@
             pooled_recv.at[other],
             at_section(other),
         ).wait_recv()
-    angles = sched[0] * frequency_ref[...]
-    embedding = jnp.concatenate([jnp.cos(angles), jnp.sin(angles)], axis=-1)
-    embed = jnp.dot(
-        embedding.astype(jnp.bfloat16), time_weight_ref[...], preferred_element_type=jnp.float32
-    )
     for r in range(8):
         cond[r] = jax.nn.silu(embed[r : r + 1] + pooled[core * 4 + r % 4])
-    ring_step(3)
-    ring_step(4)
     take_x(zz + 4)
 
     for z in range(8):
@@ -477,6 +476,16 @@
 
         lax.fori_loop(0, here, step, 0)
 
+    for k in range(4):
+        slot = ((sy + k) % 4) * 2 + sx
+        block = feature_ref.at[slot]
+        across = copy(
+            block, block, feature_send.at[4 + k], feature_recv.at[slot], x_outer
+        )
+        if k > 0:
+            across.wait_recv()
+        start(across)
+
     run_pass(0)
     for k in range(16):
         slot = (dev + 2 * k) % 32
@@ -541,16 +550,6 @@
 
     for k in range(1, 8):
         start(send_feat((sec + k) % 8, sec))
-    for k in range(4):
-        slot = ((sy + k) % 4) * 2 + sx
-        block = feature_ref.at[slot]
-        across = copy(
-            block, block, feature_send.at[4 + k], feature_recv.at[slot], x_outer
-        )
-        if k > 0:
-            across.wait_recv()
-        start(across)
-
     run_pass(1)
 
     last_self = sec == 7

time: 156 us -> 153 us (0.981)
  Pallas kernels: 151 us -> 149 us
    pallas_call x1, Pallas kernels: 151 us -> 149 us  [run_train(): pl.pallas_call(train_kernel, out_shape=(jax.ShapeDtypeStruct((mbs, rows,...]
where the time goes in v7:
time: 153 us
  Pallas kernels  149 us (97%)
  local copies, waits for them, and re-layouts  3.69 us (2%)
    pallas_call x1, Pallas kernels, run_train(): pl.pallas_call(train_kernel, out_shape=(jax.ShapeDtypeStruct((mbs, rows,...  149 us
    unnamed x7, local copies, waits for them, and re-layouts  3.69 us

profile of v7, /device:TPU:1, one launch (start us, length us, event | category | flops | bytes accessed | tf_op | source)
XLA Modules:
  0.0 153.2 jit_solution(8043088340416301734)
XLA Ops:
  0.6 148.9 %shard_map.148 = (bf16[8,32,1536]{2,1,0:T(8,128)(2,1)}, f32[1,32]{1,0:T(1,128)}, f32[192,1536]{1,0:T(8,128)}) custom-call(bf16[8,32,1536]{2,1,0:T(8,128)(2,1)} %bitcast.10, s32[77,128]{1,0:T(8,128)} %bitcast.13, s32[4,3]{1,0:T(4,128)} %sched_ref.1, f32[1,128]{1,0:T(1,128)} %constant.2.clone.frequency_ref, bf16[256,1536]{1,0:T(8,128)(2,1)} %time_weight_ref.1, ...), custom_call_target="tpu_custom_call" | custom-call | tf_op jit(solution)/shard_map/pallas_call | solution.py:758
  149.5 0.0 copy-start
  149.5 2.2 %copy.19 = bf16[4,64,1536]{2,1,0:T(8,128)(2,1)} copy(bf16[4,64,1536]{2,1,0:T(8,128)(2,1)} %bitcast.11) | data formatting | bytes 1572864
  151.7 0.0 copy-done
  151.7 0.0 copy-start.1
  151.7 1.0 copy.20
  152.7 0.0 copy-done.1
  152.7 0.5 copy.21
Async XLA Ops:
  149.5 2.2 %copy-start = (f32[192,1536]{1,0:T(8,128)S(1)}, f32[192,1536]{1,0:T(8,128)}, u32[]{:S(2)}) copy-start(f32[192,1536]{1,0:T(8,128)} %get-tuple-element.7) | copy-start | bytes 3538948
  151.7 1.0 copy-start.1

commit v8 on v7

--- a/solution.py
+++ b/solution.py
@@ -95,7 +95,7 @@
     out_recv,
 ):
     mbs, rows, width = noise_ref.shape
-    chunk = 512
+    chunk = 256
     chunks = width // chunk
     xl = lax.axis_index("dp_x")
     zz = lax.axis_index("dp_z")
@@ -662,12 +662,12 @@
         ).reshape(chips, piece, lanes)
     half_out[...] = partial[1 - core].astype(jnp.bfloat16)
     send_half.start()
-    for k in range(1, sections):
-        send_out((sec + k) % sections, sec).start()
     send_half.wait_recv()
     summed[...] = (partial[core] + half_in[...].astype(jnp.float32)).astype(jnp.bfloat16)
     for k in range(1, chips):
         send_piece((chip + k) % chips, chip).start()
+    for k in range(1, sections):
+        send_out((sec + k) % sections, sec).start()
     total = summed[chip].astype(jnp.float32)
     for k in range(1, chips):
         other = (chip + chips - k) % chips
@@ -802,8 +802,8 @@
             dma((8,)),
             dma((32,)),
             dma((32,)),
-            dma(((mbs + 1) * 3,)),
-            dma((mbs * 3,)),
+            dma(((mbs + 1) * 6,)),
+            dma((mbs * 6,)),
             dma((mbs // 2,)),
             dma,
             dma((32,)),

time: 153 us -> 158 us (1.033)
  Pallas kernels: 149 us -> 153 us
    pallas_call x1, Pallas kernels: 149 us -> 153 us  [run_train(): pl.pallas_call(train_kernel, out_shape=(jax.ShapeDtypeStruct((mbs, rows,...]
where the time goes in v8:
time: 158 us; the launch traced here: 157 us
  Pallas kernels  153 us (97%)
  local copies, waits for them, and re-layouts  3.69 us (2%)
    pallas_call x1, Pallas kernels, run_train(): pl.pallas_call(train_kernel, out_shape=(jax.ShapeDtypeStruct((mbs, rows,...  153 us
    unnamed x7, local copies, waits for them, and re-layouts  3.69 us

profile of v8, /device:TPU:1, one launch (start us, length us, event | category | flops | bytes accessed | tf_op | source)
XLA Modules:
  0.0 157.4 jit_solution(12081017844294194108)
XLA Ops:
  0.6 153.1 %shard_map.148 = (bf16[8,32,1536]{2,1,0:T(8,128)(2,1)}, f32[1,32]{1,0:T(1,128)}, f32[192,1536]{1,0:T(8,128)}) custom-call(bf16[8,32,1536]{2,1,0:T(8,128)(2,1)} %bitcast.10, s32[77,128]{1,0:T(8,128)} %bitcast.13, s32[4,3]{1,0:T(4,128)} %sched_ref.1, f32[1,128]{1,0:T(1,128)} %constant.2.clone.frequency_ref, bf16[256,1536]{1,0:T(8,128)(2,1)} %time_weight_ref.1, ...), custom_call_target="tpu_custom_call" | custom-call | tf_op jit(solution)/shard_map/pallas_call | solution.py:758
  153.7 0.0 copy-start
  153.8 2.2 %copy.19 = bf16[4,64,1536]{2,1,0:T(8,128)(2,1)} copy(bf16[4,64,1536]{2,1,0:T(8,128)(2,1)} %bitcast.11) | data formatting | bytes 1572864
  155.9 0.0 copy-done
  155.9 0.0 copy-start.1
  155.9 1.0 copy.20
  156.9 0.0 copy-done.1
  156.9 0.5 copy.21
Async XLA Ops:
  153.7 2.2 %copy-start = (f32[192,1536]{1,0:T(8,128)S(1)}, f32[192,1536]{1,0:T(8,128)}, u32[]{:S(2)}) copy-start(f32[192,1536]{1,0:T(8,128)} %get-tuple-element.7) | copy-start | bytes 3538948
  155.9 1.0 copy-start.1
